TPU v7x, 32 devices: a whole 2x2x4 slice. The times are simulated.
32 devices in a mesh: depth: 4 (over y, x), row: 8 (over z, core).
Axes of the slice: x: 2, y: 2, z: 4, core: 2. Of those that a mesh axis runs over, the one named last changes fastest.
Arguments:
- field: float32 [2, 4, 4096, 4096], P(None, 'depth', 'row'), may hold values from -6 to 6
- hologram: float32 [4096, 4096], P('row'), may hold values from -6 to 6
- defocus: float32 [4], P('depth'), may hold values from 512 to 2048
Outputs:
- estimate: float32 [2, 4, 4096, 4096], P(None, 'depth', 'row')
All inputs are finite; a program needn't handle non-finite values.
Results may differ from a plain program's by a relative error of at most 0.00045.
Values sent between devices are 32-bit elements; how exact they have to be, the bound alone decides.
No kernel may reach another device: no remote copies, remote signals or barrier semaphores. Data moves between devices by JAX's collectives and lax.ppermute only.
A program may use at most 320 MiB of HBM per device.

v0:
```python
import math

import jax
import jax.numpy as jnp
from jax import lax
from jax.sharding import PartitionSpec as P

tv_step_size = 1.0 / 12.0
tv_sharpness = 0.25


def passed_along(block, axis, distance):
    devices = range(lax.axis_size(axis))
    route = [(i - distance, i) for i in devices if i - distance in devices]
    return lax.ppermute(block, axis, route)


def split_length(length_total):
    smaller = 1
    candidate = 1
    while candidate * candidate <= length_total:
        if length_total % candidate == 0:
            smaller = candidate
        candidate = candidate + 1
    return (smaller, length_total // smaller)


def block_table(cosines, sines):
    return jnp.stack([jnp.stack([cosines, -sines]), jnp.stack([sines, cosines])])


def dft_tables(length_total, inverse):
    outer_len, inner_len = split_length(length_total)
    direction = 2.0 * math.pi if inverse else -2.0 * math.pi
    first_k = jnp.arange(outer_len, dtype=jnp.int32)[:, None]
    first_a = jnp.arange(outer_len, dtype=jnp.int32)[None, :]
    radians_one = (first_k * first_a % outer_len).astype(jnp.float32) * (direction / outer_len)
    first_table = block_table(jnp.cos(radians_one), jnp.sin(radians_one))
    second_k = jnp.arange(outer_len, dtype=jnp.int32)[:, None, None]
    second_b = jnp.arange(inner_len, dtype=jnp.int32)[None, :, None]
    second_m = jnp.arange(inner_len, dtype=jnp.int32)[None, None, :]
    whole_index = (second_k * second_b + second_b * second_m * outer_len) % length_total
    radians_two = whole_index.astype(jnp.float32) * (direction / length_total)
    scale = 1.0 / length_total if inverse else 1.0
    second_table = block_table(jnp.cos(radians_two) * scale, jnp.sin(radians_two) * scale)
    return (first_table, second_table, outer_len, inner_len)


def contract(formula, table, data):
    return jnp.einsum(
        formula, table, data, precision=lax.Precision.HIGHEST, preferred_element_type=jnp.float32
    )


def transform_last(data, tables, real_input, real_only):
    first_table, second_table, outer_len, inner_len = tables
    if real_input:
        data = data[None]
        first_table = first_table[:, :1]
    if real_only:
        second_table = second_table[:1]
    leading = data.shape[1:-1]
    folded = data.reshape((data.shape[0],) + leading + (outer_len, inner_len))
    middle = contract("rqka,q...ab->r...kb", first_table, folded)
    result = contract("rqkbm,q...kb->r...mk", second_table, middle)
    result = result.reshape((result.shape[0],) + leading + (outer_len * inner_len,))
    if real_only:
        return result[0]
    return result


def transform_rows(data, tables):
    first_table, second_table, outer_len, inner_len = tables
    leading = data.shape[1:-2]
    trailing = data.shape[-1]
    folded = data.reshape((2,) + leading + (outer_len, inner_len, trailing))
    middle = contract("rqka,q...abc->r...kbc", first_table, folded)
    result = contract("rqkbm,q...kbc->r...mkc", second_table, middle)
    return result.reshape((2,) + leading + (outer_len * inner_len, trailing))


def centred_squares(length_total, offset_start, length_part):
    indices = offset_start + jnp.arange(length_part, dtype=jnp.int32)
    centred = jnp.where(indices < length_total // 2, indices, indices - length_total)
    return (centred * centred).astype(jnp.float32)


def transfer_phase(depth_values, length_total, column_start, column_len):
    ky_squares = centred_squares(length_total, 0, length_total)
    kx_squares = centred_squares(length_total, column_start, column_len)
    grid_sum = (ky_squares[:, None] + kx_squares[None, :]) * (
        math.pi / (length_total * length_total)
    )
    return depth_values[:, None, None] * grid_sum[None]


def ahead_diff(values, incoming, axis_pos):
    extent = values.shape[axis_pos]
    shifted = jnp.concatenate(
        [lax.slice_in_dim(values, 1, extent, axis=axis_pos), incoming], axis=axis_pos
    )
    return shifted - values


def behind_diff(values, incoming, axis_pos):
    extent = values.shape[axis_pos]
    shifted = jnp.concatenate(
        [incoming, lax.slice_in_dim(values, 0, extent - 1, axis=axis_pos)], axis=axis_pos
    )
    return values - shifted


def flux_terms(depth_diff, row_diff, col_diff):
    magnitude = jnp.sqrt(
        jnp.sum(depth_diff * depth_diff + row_diff * row_diff + col_diff * col_diff, axis=0)
    )
    factor = 1.0 / (1.0 + tv_sharpness * magnitude)
    return (depth_diff * factor, row_diff * factor, col_diff * factor)


def shrink_shifts(moved_field, depth_index, row_index, plane_total, length_total):
    planes_dev = moved_field.shape[1]
    rows_dev = moved_field.shape[2]
    plane_next = passed_along(moved_field, "depth", -1)
    row_next = passed_along(moved_field[:, :, :1], "row", -1)
    plane_ids = depth_index * planes_dev + jnp.arange(planes_dev, dtype=jnp.int32)
    row_ids = row_index * rows_dev + jnp.arange(rows_dev, dtype=jnp.int32)
    depth_diff = jnp.where(
        (plane_ids == plane_total - 1)[None, :, None, None],
        0.0,
        ahead_diff(moved_field, plane_next, 1),
    )
    row_diff = jnp.where(
        (row_ids == length_total - 1)[None, None, :, None],
        0.0,
        ahead_diff(moved_field, row_next, 2),
    )
    col_diff = ahead_diff(moved_field, moved_field[..., -1:], 3)
    flux_z, flux_y, flux_x = flux_terms(depth_diff, row_diff, col_diff)
    prior_plane = passed_along(flux_z, "depth", 1)
    prior_row = passed_along(flux_y[:, :, -1:], "row", 1)
    divergence = (
        behind_diff(flux_z, prior_plane, 1)
        + behind_diff(flux_y, prior_row, 2)
        + behind_diff(flux_x, jnp.zeros_like(flux_x[..., :1]), 3)
    )
    return moved_field + tv_step_size * divergence


def per_device(field, hologram, defocus):
    planes_dev = field.shape[1]
    rows_dev = field.shape[2]
    length_total = field.shape[3]
    row_devices = lax.axis_size("row")
    depth_devices = lax.axis_size("depth")
    row_index = lax.axis_index("row")
    depth_index = lax.axis_index("depth")
    cols_dev = length_total // row_devices
    rows_piece = rows_dev // depth_devices
    plane_total = planes_dev * depth_devices
    forward_tables = dft_tables(length_total, False)
    inverse_tables = dft_tables(length_total, True)
    phase_table = transfer_phase(defocus, length_total, row_index * cols_dev, cols_dev)
    cosine_table = jnp.cos(phase_table)
    sine_table = jnp.sin(phase_table)
    hologram_part = lax.dynamic_slice_in_dim(hologram, depth_index * rows_piece, rows_piece, 0)
    estimate = field
    spectrum = transform_last(estimate, forward_tables, False, False)
    spectrum = lax.all_to_all(spectrum, "row", split_axis=3, concat_axis=2, tiled=True)
    spectrum = transform_rows(spectrum, forward_tables)
    sum_real = jnp.sum(spectrum[0] * cosine_table + spectrum[1] * sine_table, axis=0)
    sum_imag = jnp.sum(spectrum[1] * cosine_table - spectrum[0] * sine_table, axis=0)
    summed = transform_rows(jnp.stack([sum_real, sum_imag]), inverse_tables)
    by_rows = lax.all_to_all(summed, "row", split_axis=1, concat_axis=2, tiled=True)
    image_part = transform_last(by_rows, inverse_tables, False, True)
    image_sum = lax.psum_scatter(image_part, "depth", scatter_dimension=0, tiled=True)
    misfit = image_sum - hologram_part
    misfit_block = lax.all_gather(misfit, "depth", axis=0, tiled=True)
    misfit_pair = transform_last(misfit_block, forward_tables, True, False)
    misfit_spec = lax.all_to_all(misfit_pair, "row", split_axis=2, concat_axis=1, tiled=True)
    misfit_spec = transform_rows(misfit_spec, forward_tables)
    adj_real = misfit_spec[0][None] * cosine_table - misfit_spec[1][None] * sine_table
    adj_imag = misfit_spec[0][None] * sine_table + misfit_spec[1][None] * cosine_table
    adjoint = transform_rows(jnp.stack([adj_real, adj_imag]), inverse_tables)
    adjoint = lax.all_to_all(adjoint, "row", split_axis=2, concat_axis=3, tiled=True)
    gradient = transform_last(adjoint, inverse_tables, False, False)
    moved_field = estimate - 1.0 / plane_total * gradient
    estimate = shrink_shifts(moved_field, depth_index, row_index, plane_total, length_total)
    return estimate


def solution(mesh):
    return jax.shard_map(
        per_device,
        mesh=mesh,
        in_specs=(P(None, "depth", "row", None), P("row", None), P("depth")),
        out_specs=P(None, "depth", "row", None),
        check_vma=False,
    )
```

profile of v0, /device:TPU:0, one launch (start us, length us, event | category | flops | bytes accessed | tf_op | source)
XLA Modules:
  0.0 3440.7 jit_solution(5713302355342407365)
XLA Ops:
  6.9 17.5 copy.130
  24.4 16.6 sine_multiply_fusion
  42.4 35.5 %fusion.79 = f32[2,512,64,64,1]{1,2,3,0,4:T(8,128)} fusion(f32[2,512,64,64]{1,3,2,0:T(8,128)} %bitcast.239, f32[1,2,64,64]{3,2,1,0:T(8,128)S(1)} %get-tuple-element.25, f32[1,2,64,64]{3,2,1,0:T(8,128)S(1)} %get-tuple-element.24), kind=kOutput, calls=%fused_computation.83 | convolution fusion | flops 6442467328 | bytes 33619968 | tf_op jit(solution)/shard_map/rqka,q...ab->r...kb/dot_general | solution.py:50
  77.9 31.3 fusion.39
  109.2 15.2 copy.92
  124.5 32.5 copy.93
  157.0 6.3 all-to-all-start
  164.4 7.8 fusion.88
  172.2 355.0 %all-to-all-done = f32[2,1,512,4096]{2,0,1,3:T(2,128)} async-done(((f32[2,1,512,4096]{2,0,1,3:T(2,128)}), f32[2,1,512,4096]{2,0,1,3:T(2,128)}, u32[]{:S(2)}, u32[]{:S(2)}) %all-to-all-start) | async-done | bytes 16777248 | tf_op jit(solution)/shard_map/all_to_all | solution.py:169
  527.2 14.2 copy.94
  541.4 17.3 copy.95
  558.7 31.3 fusion.42
  589.9 25.4 fusion.45
  615.4 36.4 %multiply_add_fusion.1 = (f32[1,64,64,512]{3,1,2,0:T(8,128)}, f32[1,64,64,512]{3,1,2,0:T(8,128)}) fusion(f32[2,1,64,64,512]{4,2,0,3,1:T(8,128)} %fusion.45, f32[]{:T(128)} %bitcast.41, f32[512]{0:T(512)S(1)} %fusion.116, f32[64,64]{0,1:T(8,128)S(1)} %fusion.109), kind=kLoop, calls=%fused_computation.76 | loop fusion | flops 16777216 | bytes 33572868 | tf_op jit(solution)/shard_map/add | solution.py:171
  651.8 22.3 fusion.82
  674.1 31.4 fusion.48
  705.5 19.5 copy.102
  725.1 28.0 copy.103
  753.1 367.1 %all_to_all.60 = f32[2,4096,512]{2,0,1:T(2,128)S(1)} all-to-all(f32[2,4096,512]{2,0,1:T(2,128)S(1)} %copy.103), channel_id=1, replica_groups=mesh['depth'=4,'row'=8] {'row'}, dimensions={1} | all-to-all | bytes 33554432 | tf_op jit(solution)/shard_map/all_to_all | solution.py:174
  1120.2 8.8 copy.104
  1129.0 17.3 copy.105
  1146.3 31.1 fusion.51
  1177.4 23.5 fusion.89
  1201.0 8.1 copy.108
  1209.2 3.2 constant_dynamic-slice_fusion
  1214.5 80.0 %reduce-scatter.2.cloned.1.call-done = f32[128,4096]{0,1:T(8,128)} async-done(((f32[512,4096]{0,1:T(8,128)}), f32[128,4096]{0,1:T(8,128)}) %reduce-scatter.2.cloned.1.call-update) | async-done | bytes 2097168 | tf_op jit(solution)/shard_map/reduce_scatter | solution.py:176
  1294.5 3.2 sub.63
  1297.7 87.6 %all-gather.2.cloned.1.call-done = f32[512,4096]{0,1:T(8,128)} async-done(((f32[128,4096]{0,1:T(8,128)}), f32[512,4096]{0,1:T(8,128)}) %all-gather.2.cloned.1.call-update) | async-done | bytes 8388624 | tf_op jit(solution)/shard_map/all_gather | solution.py:178
  1385.4 24.1 convolution_bitcast_fusion
  1409.5 25.4 fusion.54
  1434.9 15.2 copy.112
  1450.2 32.2 copy.113
  1482.4 369.0 %all_to_all.61 = f32[2,512,4096]{1,0,2:T(2,128)S(1)} all-to-all(f32[2,512,4096]{1,0,2:T(2,128)} %copy.113), channel_id=1, replica_groups=mesh['depth'=4,'row'=8] {'row'}, dimensions={2} | all-to-all | bytes 33554432 | tf_op jit(solution)/shard_map/all_to_all | solution.py:180
  1851.4 8.8 copy.114
  1860.2 17.3 copy.115
  1877.5 33.1 fusion.85
  1910.6 31.3 fusion.57
  1941.9 36.4 %multiply_subtract_fusion = (f32[1,1,64,64,512]{4,2,3,1,0:T(8,128)}, f32[1,1,64,64,512]{4,2,3,1,0:T(8,128)}) fusion(f32[2,64,64,512]{3,1,0,2:T(8,128)} %fusion.57, f32[]{:T(128)} %bitcast.41, f32[512]{0:T(512)S(1)} %copy-done.18, f32[64,64]{0,1:T(8,128)S(1)} %copy-done.16), kind=kLoop, calls=%fused_computation.71 | loop fusion | flops 16777216 | bytes 33572868 | tf_op jit(solution)/shard_map/sub | solution.py:182
  1978.4 21.3 fusion.60
  1999.7 25.0 fusion.63
  2024.7 15.4 copy.122
  2040.1 32.2 copy.123
  2072.4 368.8 %all_to_all.62 = f32[2,1,4096,512]{3,0,1,2:T(2,128)S(1)} all-to-all(f32[2,1,4096,512]{3,0,1,2:T(2,128)} %copy.123), channel_id=1, replica_groups=mesh['depth'=4,'row'=8] {'row'}, dimensions={2} | all-to-all | bytes 33554432 | tf_op jit(solution)/shard_map/all_to_all | solution.py:185
  2441.1 8.8 copy.124
  2449.9 17.3 copy.125
  2467.2 31.1 fusion.66
  2498.3 32.7 fusion.5
  2531.0 17.8 copy.129
  2548.9 12.7 bitcast_subtract_fusion
  2563.1 4.4 slice.69
  2567.5 2.8 copy.131
  2572.5 11.4 slice.70
  2583.8 12.9 slice.68
  2599.3 326.1 %collective-permute-done = f32[2,1,512,4096]{2,3,0,1:T(8,128)} collective-permute-done((f32[2,1,512,4096]{2,3,0,1:T(8,128)}, f32[2,1,512,4096]{2,3,0,1:T(8,128)}, u32[]{:S(2)}, u32[]{:S(2)}) %collective-permute-start) | collective-permute-done | bytes 16777248 | tf_op jit(solution)/shard_map/ppermute | solution.py:15
  2925.5 28.8 add_reduce_fusion
  2954.2 9.6 add_divide_fusion
  2963.8 44.2 %broadcast_multiply_fusion.2 = (f32[2,1,512,4096]{2,3,0,1:T(8,128)}, f32[2,1,512,4096]{2,3,0,1:T(8,128)}, f32[2,1,512,4096]{2,3,0,1:T(8,128)}) fusion(f32[512,4096]{0,1:T(8,128)} %add_divide_fusion, f32[2,1,512,4096]{2,3,0,1:T(8,128)} %collective-permute-done, f32[2,1,512,4096]{2,3,0,1:T(8,128)} %bitcast_subtract_fusion, pred[]{:T(512)S(6)} %eq.20, ...), kind=kLoop, calls=%fused_computation.68 | loop fusion | flops 41943040 | bytes 125829632 | tf_op jit(solution)/shard_map/mul | solution.py:118
  3008.0 10.2 collective-permute-start.2
  3018.2 5.3 slice.72
  3023.5 2.8 copy.133
  3028.4 2.7 copy.134
  3031.1 339.6 %collective-permute-done.2 = f32[2,1,512,4096]{2,3,0,1:T(8,128)} collective-permute-done((f32[2,1,512,4096]{2,3,0,1:T(8,128)}, f32[2,1,512,4096]{2,3,0,1:T(8,128)}, u32[]{:S(2)}, u32[]{:S(2)}) %collective-permute-start.2) | collective-permute-done | bytes 16777248 | tf_op jit(solution)/shard_map/ppermute | solution.py:15
  3370.7 45.4 %fusion.4 = f32[2,1,512,4096]{2,3,0,1:T(8,128)} fusion(f32[2,1,512,4096]{2,3,0,1:T(8,128)} %bitcast_subtract_fusion, f32[2,1,512,4096]{2,3,0,1:T(8,128)} %get-tuple-element.6, f32[2,1,511,4096]{2,3,0,1:T(8,128)} %bitcast.237, f32[2,1,1,4096]{2,3,0,1:T(8,128)} %copy.134, f32[2,1,512,4096]{2,3,0,1:T(8,128)} %get-tuple-element.7, ...), kind=kLoop, calls=%fused_computation.9 | loop fusion | flops 33554432 | bytes 134213632 | tf_op jit(solution)/shard_map/add | solution.py:147
  3416.2 17.5 copy.135
  (72 shorter events, 12.6 us)
Async XLA Ops:
  42.3 35.5 %copy-start = (f32[1,2,64,64,64]{3,4,1,0,2:T(8,128)}, f32[1,2,64,64,64]{3,4,1,0,2:T(8,128)S(1)}, u32[]{:S(2)}) copy-start(f32[1,2,64,64,64]{3,4,1,0,2:T(8,128)S(1)} %get-tuple-element.14) | copy-start | bytes 6291460
  42.3 35.5 %copy-start.4 = (f32[1,2,64,64,64]{3,4,1,0,2:T(8,128)}, f32[1,2,64,64,64]{3,4,1,0,2:T(8,128)S(1)}, u32[]{:S(2)}) copy-start(f32[1,2,64,64,64]{3,4,1,0,2:T(8,128)S(1)} %get-tuple-element.15) | copy-start | bytes 6291460
  157.0 370.2 %all-to-all-start = ((f32[2,1,512,4096]{2,0,1,3:T(2,128)}), f32[2,1,512,4096]{2,0,1,3:T(2,128)}, u32[]{:S(2)}, u32[]{:S(2)}) async-start(f32[2,1,512,4096]{2,0,1,3:T(2,128)} %copy.93), calls=%async_computation | async-start | bytes 33554432 | tf_op jit(solution)/shard_map/all_to_all | solution.py:169
  163.3 1131.2 %reduce-scatter.2.cloned.1.call-start = ((), (), s32[]{:S(2)}) async-start(), calls=%async_computation.5 | async-start | bytes 10485760 | tf_op jit(solution)/shard_map/reduce_scatter | solution.py:176
  164.0 451.4 %copy-start.17 = (f32[512]{0:T(512)}, f32[512]{0:T(512)S(1)}, u32[]{:S(2)}) copy-start(f32[512]{0:T(512)S(1)} %fusion.116) | copy-start | bytes 6148
  164.0 451.3 %copy-start.15 = (f32[64,64]{0,1:T(8,128)}, f32[64,64]{0,1:T(8,128)S(1)}, u32[]{:S(2)}) copy-start(f32[64,64]{0,1:T(8,128)S(1)} %fusion.109) | copy-start | bytes 49156
  558.7 31.3 copy-start.1
  558.7 31.3 copy-start.5
  651.8 22.3 copy-start.8
  651.8 22.3 copy-start.11
  1146.3 31.1 copy-start.14
  1209.2 176.2 %all-gather.2.cloned.1.call-start = ((), (), s32[]{:S(2)}) async-start(), calls=%async_computation.6 | async-start | bytes 10485760 | tf_op jit(solution)/shard_map/all_gather | solution.py:178
  1385.3 24.1 copy-start.2
  1385.4 24.1 copy-start.6
  1877.5 33.1 copy-start.3
  1877.5 33.1 copy-start.7
  1910.6 31.3 copy-start.16
  1910.6 31.3 copy-start.18
  1978.4 21.3 copy-start.9
  1978.4 21.3 copy-start.12
  2467.2 31.1 copy-start.10
  2467.2 31.1 copy-start.13
  2498.3 50.6 %slice-start = ((s8[16777216]{0:T(1024)(128)(4,1)}), s8[4194304]{0:T(1024)(128)(4,1)S(1)}, s32[]{:S(2)}) async-start(s8[16777216]{0:T(1024)(128)(4,1)} %bitcast.240), calls=%async_computation.7 | async-start | bytes 8388608
  2498.3 50.6 %slice-start.1 = ((s8[16777216]{0:T(1024)(128)(4,1)}), s8[4194304]{0:T(1024)(128)(4,1)S(1)}, s32[]{:S(2)}) async-start(s8[16777216]{0:T(1024)(128)(4,1)} %bitcast.240), calls=%async_computation.8 | async-start | bytes 8388608
  2498.3 50.6 %slice-start.2 = ((s8[16777216]{0:T(1024)(128)(4,1)}), s8[4194304]{0:T(1024)(128)(4,1)S(1)}, s32[]{:S(2)}) async-start(s8[16777216]{0:T(1024)(128)(4,1)} %bitcast.240), calls=%async_computation.9 | async-start | bytes 8388608
  2531.0 17.9 slice-start.3
  2561.6 363.8 %collective-permute-start = (f32[2,1,512,4096]{2,3,0,1:T(8,128)}, f32[2,1,512,4096]{2,3,0,1:T(8,128)}, u32[]{:S(2)}, u32[]{:S(2)}) collective-permute-start(f32[2,1,512,4096]{2,3,0,1:T(8,128)} %bitcast_subtract_fusion), channel_id=1, source_target_pairs={{8,0},{16,8},{24,16},{9,1},{17,9},{25,17},{10,2},{18,10},{26,18},{... | collective-permute-start | bytes 50331656 | tf_op jit(solution)/shard_map/ppermute | solution.py:15
  2570.4 26.3 collective-permute-start.1
  3008.0 362.7 %collective-permute-start.2 = (f32[2,1,512,4096]{2,3,0,1:T(8,128)}, f32[2,1,512,4096]{2,3,0,1:T(8,128)}, u32[]{:S(2)}, u32[]{:S(2)}) collective-permute-start(f32[2,1,512,4096]{2,3,0,1:T(8,128)} %get-tuple-element.5), channel_id=1, source_target_pairs={{0,8},{8,16},{16,24},{1,9},{9,17},{17,25},{2,10},{10,18},{18,26},{... | collective-permute-start | bytes 50331656 | tf_op jit(solution)/shard_map/ppermute | solution.py:15
  3026.3 2.1 collective-permute-start.3
Sparse Core Ops, SparseCore 0:
  1209.3 85.2 reduce-scatter.1
  1297.9 87.4 all-gather.1
where the time goes:
time: 3450 us; the launch traced here: 3440 us
  waiting for transfers between devices  1190 us (34%)
  blocking collectives  1100 us (32%)
  matrix products  456 us (13%)
  local copies, waits for them, and re-layouts  412 us (12%)
  other arithmetic  243 us (7%)
    ppermute x4, waiting for transfers between devices, passed_along(): return lax.ppermute(block, axis, route)  667 us
    dot_general x16, matrix products, contract(): jnp.einsum(formula, table, data, precision=lax.Precision.HIGHEST, preferr...  456 us
    all_to_all x1, blocking collectives, per_device(): lax.all_to_all(misfit_pair, 'row', split_axis=2, concat_axis=1, tiled=True)  369 us
    all_to_all x1, blocking collectives, per_device(): lax.all_to_all(adjoint, 'row', split_axis=2, concat_axis=3, tiled=True)  369 us
    all_to_all x1, blocking collectives, per_device(): lax.all_to_all(summed, 'row', split_axis=1, concat_axis=2, tiled=True)  367 us
    all_to_all x1, waiting for transfers between devices, per_device(): lax.all_to_all(spectrum, 'row', split_axis=3, concat_axis=2, tiled=True)  355 us
    all_gather x1, waiting for transfers between devices, per_device(): misfit_block = lax.all_gather(misfit, 'depth', axis=0, tiled=True)  87.6 us
    reduce_scatter x1, waiting for transfers between devices, per_device(): lax.psum_scatter(image_part, 'depth', scatter_dimension=0, tiled=True)  80 us
  transfers between devices with their start and end apart: 7, of which 6 were waited for; matrix products, arithmetic and copies ran while one was open for 2% of the time, Pallas kernels for 0%

commit v1 on v0

v1 whole, which is shorter than its diff:
```python
import math

import jax
import jax.numpy as jnp
import numpy as np
from jax import lax
from jax.experimental import pallas as pl
from jax.experimental.pallas import tpu as pltpu
from jax.sharding import Mesh, PartitionSpec as P

tv_step_size = 1.0 / 12.0
tv_sharpness = 0.25
LANES = 128
GROUPS = 4
PASSES = 2
VMEM_BYTES = 60 * 1024 * 1024
f32 = jnp.float32
bf16 = jnp.bfloat16


def c_add(u, v):
    return (u[0] + v[0], u[1] + v[1])


def c_sub(u, v):
    return (u[0] - v[0], u[1] - v[1])


def c_rot(u, num, den):
    num = num % den
    if num == 0:
        return u
    if 4 * num == den:
        return (-u[1], u[0])
    if 2 * num == den:
        return (-u[0], -u[1])
    if 4 * num == 3 * den:
        return (u[1], -u[0])
    if (8 * num) % den == 0:
        half = math.sqrt(0.5)
        eighth = (8 * num) // den
        plus = (u[0] + u[1]) * half
        minus = (u[0] - u[1]) * half
        if eighth == 1:
            return (minus, plus)
        if eighth == 3:
            return (-plus, minus)
        if eighth == 5:
            return (-minus, -plus)
        return (plus, -minus)
    cos = math.cos(2 * math.pi * num / den)
    sin = math.sin(2 * math.pi * num / den)
    return (u[0] * cos - u[1] * sin, u[0] * sin + u[1] * cos)


def dft4(v, sign):
    s, d = c_add(v[0], v[2]), c_sub(v[0], v[2])
    t, u = c_add(v[1], v[3]), c_sub(v[1], v[3])
    u = c_rot(u, sign, 4)
    return [c_add(s, t), c_add(d, u), c_sub(s, t), c_sub(d, u)]


def dft8(v, sign):
    even, odd = dft4(v[0::2], sign), dft4(v[1::2], sign)
    odd = [c_rot(odd[q], sign * q, 8) for q in range(4)]
    return [c_add(even[q], odd[q]) for q in range(4)] + [c_sub(even[q], odd[q]) for q in range(4)]


def real_rot(value, num, den):
    cos = math.cos(2 * math.pi * num / den)
    sin = math.sin(2 * math.pi * num / den)
    return (value * cos, value * sin)


def total(values):
    out = values[0]
    for value in values[1:]:
        out = out + value
    return out


def slab_forward(x, group):
    count = len(x)
    if group == 0 and count == 8:
        s0, d0, s1, d1 = x[0] + x[4], x[0] - x[4], x[2] + x[6], x[2] - x[6]
        s2, d2, s3, d3 = x[1] + x[5], x[1] - x[5], x[3] + x[7], x[3] - x[7]
        e0, e2, o0, o2 = s0 + s1, s0 - s1, s2 + s3, s2 - s3
        p1 = c_rot((d2, -d3), -1, 8)
        p3 = c_rot((d2, d3), -3, 8)
        return [(e0 + o0, e0 - o0), (d0 + p1[0], p1[1] - d1), (e2, -o2), (d0 + p3[0], d1 + p3[1])]
    if count == 8:
        w = [(x[0], None)] + [real_rot(x[j], -group * j, 32) for j in range(1, 8)]
        s, d = (x[0] + w[4][0], w[4][1]), (x[0] - w[4][0], -w[4][1])
        t, u = c_add(w[2], w[6]), c_rot(c_sub(w[2], w[6]), -1, 4)
        even = [c_add(s, t), c_add(d, u), c_sub(s, t), c_sub(d, u)]
        odd = dft4(w[1::2], -1)
        return [c_add(even[q], c_rot(odd[q], -q, 8)) for q in range(4)]
    outs = []
    for q in range(4):
        parts = [real_rot(x[j], -(group + 4 * q) * j, 32) for j in range(count)]
        outs.append((total([v[0] for v in parts]), total([v[1] for v in parts])))
    if group == 0:
        outs[0] = (total(x), total([x[j] if j % 2 == 0 else -x[j] for j in range(count)]))
    return outs


def slab_inverse(g, group, count):
    if group == 0:
        (top, alt), rest = g[0], g[1:]
        if count == 8:
            (a1, b1), (a2, b2), (a3, b3) = rest
            half = math.sqrt(0.5)
            p, m = top + alt, top - alt
            s13, d13 = a1 + a3, b1 - b3
            x0, x4 = p + a2 + s13, p + a2 - s13
            x2, x6 = p - a2 - d13, p - a2 + d13
            u = (a1 - a3) * half
            v = (b1 + b3) * half
            x1, x5 = m - b2 + (u - v), m - b2 - (u - v)
            x3, x7 = m + b2 - (u + v), m + b2 + (u + v)
            return [x0, x1, x2, x3, x4, x5, x6, x7]
        outs = []
        for j in range(count):
            terms = [c_rot(rest[q - 1], q * j, 8)[0] for q in range(1, 4)]
            outs.append((top + alt if j % 2 == 0 else top - alt) + total(terms))
        return outs
    if count == 8:
        even = dft4(g, 1)
        odd = dft4([c_rot(g[q], q, 8) for q in range(4)], 1)
        v = [even[0], odd[0], even[1], odd[1], even[2], odd[2], even[3], odd[3]]
        outs = [v[0][0]]
        for j in range(1, 8):
            cos = math.cos(2 * math.pi * group * j / 32)
            sin = math.sin(2 * math.pi * group * j / 32)
            outs.append(v[j][0] * cos - v[j][1] * sin)
        return outs
    outs = []
    for j in range(count):
        terms = [c_rot(g[q], (group + 4 * q) * j, 32)[0] for q in range(4)]
        outs.append(total(terms))
    return outs


def two_parts(value):
    high = value.astype(bf16)
    low = (value - high.astype(f32)).astype(bf16)
    return high, low


def dot(left, right):
    return jnp.dot(left, right, preferred_element_type=f32)


def host_parts(matrix):
    high = matrix.astype(np.float32).astype(jnp.bfloat16)
    low = (matrix - high.astype(np.float64)).astype(np.float32).astype(jnp.bfloat16)
    return high, low


def lane_tables():
    n = np.arange(LANES)
    angle = 2 * np.pi * (n[:, None] * n[None, :] % LANES) / LANES
    cos, sin = np.cos(angle), np.sin(angle)
    forward = np.block([[cos, -sin], [sin, cos]])
    inverse = np.block([[cos, sin], [-sin, cos]])
    stacked = []
    for matrix in (forward, inverse):
        high, low = host_parts(matrix)
        stacked.append(np.concatenate([high, high, low], axis=0))
    return stacked


def twiddle_table(length, tiles):
    k = np.arange(tiles)[:, None]
    n = np.arange(LANES)[None, :]
    angle = -2 * np.pi * (k * n % length) / length
    return np.stack([np.cos(angle), np.sin(angle)]).astype(np.float32)


def slot_bases(length):
    n = np.arange(LANES)[:, None]
    bases = np.zeros((16, 2 * LANES, 2 * LANES))
    freqs = np.zeros((16, 2 * LANES), np.int64)
    for group in range(GROUPS):
        for q in range(4):
            k = group + 4 * q
            slot = group * 4 + q
            if k == 0:
                column = 0
                for half, start in ((0, 0), (1, 16)):
                    rows = slice(half * LANES, (half + 1) * LANES)
                    for step in range(LANES // 2 + 1):
                        a = start + 32 * step
                        if a > length // 2:
                            continue
                        angle = 2 * np.pi * (a * n[:, 0] % length) / length
                        if a in (0, length // 2):
                            bases[slot, rows, column] = np.cos(angle) / np.sqrt(LANES)
                            freqs[slot, column] = a
                            column += 1
                            continue
                        bases[slot, rows, column] = np.cos(angle) * np.sqrt(2 / LANES)
                        bases[slot, rows, column + 1] = np.sin(angle) * np.sqrt(2 / LANES)
                        freqs[slot, column : column + 2] = a
                        column += 2
                assert column == 2 * LANES
                continue
            a = k + 32 * np.arange(LANES)[None, :]
            angle = 2 * np.pi * (a * n % length) / length
            cos, sin = np.cos(angle) / np.sqrt(LANES), np.sin(angle) / np.sqrt(LANES)
            bases[slot] = np.block([[cos, -sin], [sin, cos]])
            freqs[slot] = np.concatenate([a[0], a[0]])
    return bases.astype(np.float32), freqs


def chirp(depth_values, freqs, length):
    centred = np.where(freqs < length // 2, freqs, freqs - length)
    squares = (centred.astype(np.int64) ** 2).astype(np.int64)
    coarse = (squares // 2048 * 2048).astype(np.float32)
    fine = (squares % 2048).astype(np.float32)
    unit = 0.5 / (float(length) * float(length))
    whole = jnp.floor(depth_values * 2.0) * 0.5
    rest = depth_values - whole

    def turn(left, right):
        value = left * right * unit
        return value - jnp.floor(value)

    turns = turn(whole, coarse) + turn(whole, fine) + rest * (coarse * unit) + rest * (fine * unit)
    angle = (turns - jnp.floor(turns)) * (2.0 * math.pi)
    return jnp.cos(angle), jnp.sin(angle)


def lane_convolve(rows, load, store, work, parts, spec, forward_ref, inverse_ref, twiddle_ref, transfer):
    def put_parts(tile, row, pair):
        for at, value in enumerate(pair):
            high, low = two_parts(value)
            span = pl.ds(tile * rows + row, 16)
            parts[span, at * LANES : (at + 1) * LANES] = high
            parts[span, (2 + at) * LANES : (3 + at) * LANES] = low
            parts[span, (4 + at) * LANES : (5 + at) * LANES] = high

    def multiply(table_ref):
        step = min(512, 32 * rows)

        def body(i, carry):
            span = pl.ds(i * step, step)
            spec[span, :] = dot(parts[span, :], table_ref[...])
            return carry

        lax.fori_loop(0, 32 * rows // step, body, 0)

    def forward(i, carry):
        row = i * 16
        span = pl.ds(row, 16)
        for b in range(8):
            x = [load(8 * a + b, row) for a in range(4)]
            y = dft4(x, -1)
            for k in range(4):
                v = c_rot(y[k], -b * k, 32)
                work[0, k * 8 + b, span, :] = v[0]
                work[1, k * 8 + b, span, :] = v[1]
        for k in range(4):
            x = [(work[0, k * 8 + b, span, :], work[1, k * 8 + b, span, :]) for b in range(8)]
            y = dft8(x, -1)
            for m in range(8):
                tile = k + 4 * m
                tr, ti = twiddle_ref[0, tile : tile + 1, :], twiddle_ref[1, tile : tile + 1, :]
                re, im = y[m]
                put_parts(tile, row, (re * tr - im * ti, re * ti + im * tr))
        return carry

    lax.fori_loop(0, rows // 16, forward, 0)
    multiply(forward_ref)

    def middle(tile, carry):
        tr, ti = transfer(tile)
        for row in range(0, rows, 16):
            span = pl.ds(tile * rows + row, 16)
            re, im = spec[span, :LANES], spec[span, LANES:]
            put_parts(tile, row, (re * tr - im * ti, re * ti + im * tr))
        return carry

    lax.fori_loop(0, 32, middle, 0)
    multiply(inverse_ref)

    def inverse(i, carry):
        row = i * 16
        span = pl.ds(row, 16)
        for k in range(4):
            x = []
            for m in range(8):
                tile = k + 4 * m
                tr, ti = twiddle_ref[0, tile : tile + 1, :], twiddle_ref[1, tile : tile + 1, :]
                at = pl.ds(tile * rows + row, 16)
                re, im = spec[at, :LANES], spec[at, LANES:]
                x.append((re * tr + im * ti, im * tr - re * ti))
            y = dft8(x, 1)
            for b in range(8):
                v = c_rot(y[b], b * k, 32)
                work[0, k * 8 + b, span, :] = v[0]
                work[1, k * 8 + b, span, :] = v[1]
        for b in range(8):
            x = [(work[0, k * 8 + b, span, :], work[1, k * 8 + b, span, :]) for k in range(4)]
            y = dft4(x, 1)
            for a in range(4):
                store(8 * a + b, row, y[a])
        return carry

    lax.fori_loop(0, rows // 16, inverse, 0)


def lane_scratch(rows):
    return [
        pltpu.VMEM((2, 32, rows, LANES), f32),
        pltpu.VMEM((32 * rows, 6 * LANES), bf16),
        pltpu.VMEM((32 * rows, 2 * LANES), f32),
    ]


def params():
    return pltpu.CompilerParams(vmem_limit_bytes=VMEM_BYTES)


def whole_block(array):
    rank = array.ndim
    return pl.BlockSpec(array.shape, lambda *_: (0,) * rank)


def column_pass(plan, scalars, field, tables, transfer):
    rows = min(64, plan.rows_dev)
    level, chunk, cols = plan.level, plan.chunk, plan.cols_dev
    per_piece = cols // LANES
    n_out = level * PASSES

    def kernel(scal, f_ref, fwd, inv, twd, tra, *rest):
        outs, (work, parts, spec, staged) = rest[:n_out], rest[n_out:]

        def load(tile, row):
            at = slice(tile * LANES, (tile + 1) * LANES)
            return (f_ref[0, pl.ds(row, 16), at], f_ref[1, pl.ds(row, 16), at])

        def store(tile, row, value):
            staged[tile, 0, pl.ds(row, 16), :] = value[0]
            staged[tile, 1, pl.ds(row, 16), :] = value[1]

        def pick(tile):
            return tra[0, pl.ds(tile, 1), :], tra[1, pl.ds(tile, 1), :]

        lane_convolve(rows, load, store, work, parts, spec, fwd, inv, twd, pick)
        for part in range(PASSES):
            for s in range(level):
                first = jnp.bitwise_xor(scal[0], s) * per_piece + part * (chunk // LANES)
                for t in range(chunk // LANES):
                    for ri in range(2):
                        outs[part * level + s][ri, :, t * LANES : (t + 1) * LANES] = staged[first + t, ri]

    width = field.shape[-1]
    fixed = [tables["forward"], tables["inverse"], tables["twiddle"], transfer]
    return pl.pallas_call(
        kernel,
        grid_spec=pltpu.PrefetchScalarGridSpec(
            num_scalar_prefetch=1,
            grid=(plan.rows_dev // rows,),
            in_specs=[pl.BlockSpec((2, rows, width), lambda i, _: (0, i, 0))] + [whole_block(a) for a in fixed],
            out_specs=[pl.BlockSpec((2, rows, chunk), lambda i, _: (0, i, 0))] * n_out,
            scratch_shapes=lane_scratch(rows) + [pltpu.VMEM((32, 2, rows, LANES), f32)],
        ),
        out_shape=[jax.ShapeDtypeStruct((2, plan.rows_dev, chunk), f32)] * n_out,
        compiler_params=params(),
        cost_estimate=pl.CostEstimate(flops=13 * 10**9, bytes_accessed=34 * 10**6, transcendentals=0),
        name="column_pass",
    )(scalars, field, *fixed)


def slot_matrices(plan, bases, weights):
    kinds = weights.shape[1]
    size = 2 * LANES

    def kernel(b_ref, w_ref, high_ref, low_ref):
        basis = b_ref[0]
        for kind in range(kinds):
            scaled = basis * w_ref[0, kind : kind + 1, :]
            product = lax.dot_general(
                scaled,
                basis,
                (((1,), (1,)), ((), ())),
                precision=lax.Precision.HIGHEST,
                preferred_element_type=f32,
            )
            high, low = two_parts(product)
            high_ref[0, :, kind * size : (kind + 1) * size] = high
            low_ref[0, :, kind * size : (kind + 1) * size] = low

    shape = jax.ShapeDtypeStruct((16, size, kinds * size), bf16)
    return pl.pallas_call(
        kernel,
        grid=(16,),
        in_specs=[
            pl.BlockSpec((1, size, size), lambda i: (i, 0, 0)),
            pl.BlockSpec((1, kinds, size), lambda i: (i, 0, 0)),
        ],
        out_specs=[pl.BlockSpec((1, size, kinds * size), lambda i: (i, 0, 0))] * 2,
        out_shape=[shape, shape],
        compiler_params=params(),
        cost_estimate=pl.CostEstimate(flops=26 * 10**9, bytes_accessed=34 * 10**6, transcendentals=0),
        name="slot_matrices",
    )(bases, weights)


def row_forward(plan, scalars, phases, pieces, holos, high, low):
    level, chunk, count = plan.level, plan.chunk, plan.slab_tiles
    kinds = plan.planes * 2
    size = 2 * LANES
    half = count // 2

    def kernel(scal, phase, *refs):
        x_refs, (h0, h1, wh, wl, out, eh, el, eo) = refs[:level], refs[level:]
        flip = scal[3] != 0

        def tiles(first, second, row):
            left = [first(j, row) for j in range(half)]
            right = [second(j, row) for j in range(half)]
            lower = [jnp.where(flip, b, a) for a, b in zip(left, right)]
            upper = [jnp.where(flip, a, b) for a, b in zip(left, right)]
            return lower + upper

        for group in range(GROUPS):

            @pl.when(pl.program_id(0) == group)
            def _(group=group):
                def rows_of(i, carry):
                    row = i * 16
                    for kind in range(kinds):
                        t, ri = kind // 2, kind % 2

                        def first(j, row, t=t, ri=ri):
                            return x_refs[2 * t][ri, pl.ds(j * LANES + row, 16), :]

                        def second(j, row, t=t, ri=ri):
                            return x_refs[2 * t + 1][ri, pl.ds(j * LANES + row, 16), :]

                        outs = slab_forward(tiles(first, second, row), group)
                        for q in range(4):
                            for at in range(2):
                                a, b = two_parts(outs[q][at])
                                span = pl.ds(kind * size + at * LANES + row, 16)
                                eh[q, span, :] = a
                                el[q, span, :] = b
                    held = slab_forward(
                        tiles(
                            lambda j, row: h0[pl.ds(j * LANES + row, 16), :],
                            lambda j, row: h1[pl.ds(j * LANES + row, 16), :],
                            row,
                        ),
                        group,
                    )
                    for q in range(4):
                        for at in range(2):
                            eo[q, pl.ds(at * LANES + row, 16), :] = held[q][at]
                    return carry

                lax.fori_loop(0, LANES // 16, rows_of, 0)

        for q in range(4):
            value = dot(wh[q], eh[q]) + dot(wh[q], el[q]) + dot(wl[q], eh[q]) - eo[q]
            slot = pl.program_id(0) * 4 + q
            cos, sin = phase[0, slot], phase[1, slot]
            re, im = value[:LANES], value[LANES:]
            out[q, :LANES, :] = re * cos - im * sin
            out[q, LANES:, :] = re * sin + im * cos

    return pl.pallas_call(
        kernel,
        grid_spec=pltpu.PrefetchScalarGridSpec(
            num_scalar_prefetch=2,
            grid=(GROUPS,),
            in_specs=[whole_block(a) for a in pieces]
            + [whole_block(a) for a in holos]
            + [pl.BlockSpec((4, size, kinds * size), lambda g, *_: (g, 0, 0))] * 2,
            out_specs=pl.BlockSpec((4, size, chunk), lambda g, *_: (g, 0, 0)),
            scratch_shapes=[
                pltpu.VMEM((4, kinds * size, chunk), bf16),
                pltpu.VMEM((4, kinds * size, chunk), bf16),
                pltpu.VMEM((4, size, chunk), f32),
            ],
        ),
        out_shape=jax.ShapeDtypeStruct((16, size, chunk), f32),
        compiler_params=params(),
        cost_estimate=pl.CostEstimate(flops=13 * 10**9, bytes_accessed=60 * 10**6, transcendentals=0),
        name="row_forward",
    )(scalars, phases, *pieces, *holos, high, low)


def row_backward(plan, scalars, phases, misfit, high, low):
    level, chunk, count = plan.level, plan.chunk, plan.slab_tiles
    size = 2 * LANES
    piece = plan.piece

    def kernel(scal, phase, m_ref, wh, wl, *rest):
        outs, (mh, ml, field) = rest[:level], rest[level:]
        kind, step = pl.program_id(0), pl.program_id(1)

        @pl.when(kind == 0)
        def _():
            for q in range(4):
                slot = step * 4 + q
                cos, sin = phase[2, slot], phase[3, slot]
                re, im = m_ref[q, :LANES, :], m_ref[q, LANES:, :]
                for at, value in enumerate((re * cos - im * sin, re * sin + im * cos)):
                    a, b = two_parts(value)
                    mh[slot, at * LANES : (at + 1) * LANES, :] = a
                    ml[slot, at * LANES : (at + 1) * LANES, :] = b

        grads = []
        for q in range(4):
            slot = step * 4 + q
            grads.append(dot(wh[q], mh[slot]) + dot(wh[q], ml[slot]) + dot(wl[q], mh[slot]))
        for group in range(GROUPS):

            @pl.when(step == group)
            def _(group=group):
                for row in range(0, LANES, 16):
                    g = [(v[row : row + 16], v[LANES + row : LANES + row + 16]) for v in grads]
                    values = slab_inverse(g, group, count)
                    for j in range(count):
                        span = pl.ds(j * LANES + row, 16)
                        if group == 0:
                            field[span, :] = values[j]
                        else:
                            field[span, :] = field[span, :] + values[j]

        @pl.when(step == GROUPS - 1)
        def _():
            for s in range(level):
                other = jnp.bitwise_xor(scal[0], s)
                start = jnp.bitwise_and(other, 1) * plan.rows_dev + jnp.right_shift(other, 1) * piece
                outs[s][0] = field[pl.ds(pl.multiple_of(start, 16), piece), :]

    kinds = plan.planes * 2

    def weight_at(kind, step, scal, phase):
        return (step, 0, jnp.bitwise_xor(kind // 2, scal[1]) * 2 + kind % 2)

    return pl.pallas_call(
        kernel,
        grid_spec=pltpu.PrefetchScalarGridSpec(
            num_scalar_prefetch=2,
            grid=(kinds, GROUPS),
            in_specs=[
                pl.BlockSpec((4, size, chunk), lambda kind, step, *_: (jnp.where(kind == 0, step, GROUPS - 1), 0, 0)),
                pl.BlockSpec((4, size, size), weight_at),
                pl.BlockSpec((4, size, size), weight_at),
            ],
            out_specs=[pl.BlockSpec((1, piece, chunk), lambda kind, step, *_: (kind, 0, 0))] * level,
            scratch_shapes=[
                pltpu.VMEM((16, size, chunk), bf16),
                pltpu.VMEM((16, size, chunk), bf16),
                pltpu.VMEM((count * LANES, chunk), f32),
            ],
        ),
        out_shape=[jax.ShapeDtypeStruct((kinds, piece, chunk), f32)] * level,
        compiler_params=params(),
        cost_estimate=pl.CostEstimate(flops=13 * 10**9, bytes_accessed=60 * 10**6, transcendentals=0),
        name="row_backward",
    )(scalars, phases, misfit, high, low)


def step_pass(plan, scalars, pieces, held, tables, transfer):
    rows = min(64, plan.piece)
    level, chunk = plan.level, plan.chunk
    width = held.shape[-1]
    per_piece = plan.cols_dev // LANES
    n_in = level * PASSES
    flat = [piece for part in pieces for piece in part]
    scale = 1.0 / plan.planes

    def kernel(scal, *refs):
        g_refs, (h_ref, fwd, inv, twd, tra, out, work, parts, spec, staged) = refs[:n_in], refs[n_in:]
        for part in range(PASSES):
            for s in range(level):
                first = jnp.bitwise_xor(scal[0], s) * per_piece + part * (chunk // LANES)
                for t in range(chunk // LANES):
                    for ri in range(2):
                        staged[first + t, ri] = g_refs[part * level + s][ri, :, t * LANES : (t + 1) * LANES]

        def load(tile, row):
            return (staged[tile, 0, pl.ds(row, 16), :], staged[tile, 1, pl.ds(row, 16), :])

        def store(tile, row, value):
            at = slice(tile * LANES, (tile + 1) * LANES)
            for ri in range(2):
                before = h_ref[0, ri, pl.ds(row, 16), at]
                out[0, ri, pl.ds(row, 16), at] = before - scale * value[ri]

        def pick(tile):
            return tra[0, 0, pl.ds(tile, 1), :], tra[0, 1, pl.ds(tile, 1), :]

        lane_convolve(rows, load, store, work, parts, spec, fwd, inv, twd, pick)

    fixed = [tables["forward"], tables["inverse"], tables["twiddle"]]
    return pl.pallas_call(
        kernel,
        grid_spec=pltpu.PrefetchScalarGridSpec(
            num_scalar_prefetch=1,
            grid=(plan.planes, plan.piece // rows),
            in_specs=[pl.BlockSpec((2, rows, chunk), lambda p, i, _: (p, i, 0))] * n_in
            + [pl.BlockSpec((1, 2, rows, width), lambda p, i, scal: (jnp.bitwise_xor(p, scal[1]), 0, i, 0))]
            + [whole_block(a) for a in fixed]
            + [pl.BlockSpec((1, 2, 32, LANES), lambda p, i, _: (p, 0, 0, 0))],
            out_specs=pl.BlockSpec((1, 2, rows, width), lambda p, i, _: (p, 0, i, 0)),
            scratch_shapes=lane_scratch(rows) + [pltpu.VMEM((32, 2, rows, LANES), f32)],
        ),
        out_shape=jax.ShapeDtypeStruct((plan.planes, 2, plan.piece, width), f32),
        compiler_params=params(),
        cost_estimate=pl.CostEstimate(flops=13 * 10**9, bytes_accessed=51 * 10**6, transcendentals=0),
        name="step_pass",
    )(scalars, *flat, held, *fixed, transfer)


def shrink_pass(plan, scalars, moved, above, below):
    planes, width = plan.planes, moved.shape[-1]
    steps = plan.piece // 8
    cols = 1024

    def kernel(scal, cur, nxt, up, down, *rest):
        outs, (carry, est) = rest[:planes], rest[planes:]
        i = pl.program_id(0)
        last = i == steps - 1
        row_ids = lax.broadcasted_iota(jnp.int32, (8, cols), 0)
        lane_ids = lax.broadcasted_iota(jnp.int32, (8, cols), 1)
        end_row = jnp.logical_and(last, scal[5] != 0)

        def flux(tile, next_row, p, start):
            at_end = start + cols == width
            here = [tile(p, ri, start, cols) for ri in range(2)]
            dz, dy, dx = [], [], []
            for ri in range(2):
                if p + 1 < planes:
                    dz.append(tile(p + 1, ri, start, cols) - here[ri])
                follow = jnp.where(row_ids == 7, next_row(p, ri, start), pltpu.roll(here[ri], 7, 0))
                dy.append(follow - here[ri])
                if at_end:
                    ahead = jnp.where(lane_ids == cols - 1, here[ri], pltpu.roll(here[ri], cols - 1, 1))
                else:
                    joined = jnp.concatenate([here[ri], tile(p, ri, start + cols, LANES)], axis=1)
                    ahead = pltpu.roll(joined, cols + LANES - 1, 1)[:, :cols]
                dx.append(ahead - here[ri])
            squares = [v * v for v in dz + dy + dx]
            magnitude = jnp.sqrt(total(squares))
            factor = 1.0 / (1.0 + tv_sharpness * magnitude)
            return here, [v * factor for v in dz], [v * factor for v in dy], [v * factor for v in dx]

        @pl.when(i == 0)
        def _():
            for p in range(planes):
                for start in range(0, width, cols):
                    def tile(p, ri, at, wide):
                        return jnp.broadcast_to(up[p, ri, 0:1, at : at + wide], (8, wide))

                    def next_row(p, ri, at):
                        return cur[p, ri, 0:1, at : at + cols]

                    fy = flux(tile, next_row, p, start)[2]
                    for ri in range(2):
                        carry[p, ri, :, start : start + cols] = jnp.where(scal[4] != 0, 0.0, fy[ri])

        def tile(p, ri, at, wide):
            return cur[p, ri, :, at : at + wide]

        def next_row(p, ri, at):
            inner = nxt[p, ri, 0:1, at : at + cols]
            outer = down[p, ri, 0:1, at : at + cols]
            own = cur[p, ri, 7:8, at : at + cols]
            return jnp.where(end_row, own, jnp.where(last, outer, inner))

        prior_x = {}
        for start in range(0, width, cols):
            prior_z = None
            for p in range(planes):
                here, fz, fy, fx = flux(tile, next_row, p, start)
                for ri in range(2):
                    behind_y = jnp.where(row_ids == 0, carry[p, ri, 7:8, start : start + cols], pltpu.roll(fy[ri], 1, 0))
                    if start == 0:
                        behind_x = jnp.where(lane_ids == 0, 0.0, pltpu.roll(fx[ri], 1, 1))
                    else:
                        joined = jnp.concatenate([prior_x[p, ri], fx[ri]], axis=1)
                        behind_x = pltpu.roll(joined, 1, 1)[:, LANES:]
                    divergence = (fy[ri] - behind_y) + (fx[ri] - behind_x)
                    if fz:
                        divergence = divergence + fz[ri]
                    if prior_z:
                        divergence = divergence - prior_z[ri]
                    est[p, ri, :, start : start + cols] = here[ri] + tv_step_size * divergence
                    carry[p, ri, :, start : start + cols] = fy[ri]
                    prior_x[p, ri] = fx[ri][:, cols - LANES :]
                prior_z = fz
        for s in range(planes):
            outs[s][...] = est[jnp.bitwise_xor(scal[1], s)]

    return pl.pallas_call(
        kernel,
        grid_spec=pltpu.PrefetchScalarGridSpec(
            num_scalar_prefetch=1,
            grid=(steps,),
            in_specs=[
                pl.BlockSpec((planes, 2, 8, width), lambda i, _: (0, 0, i, 0)),
                pl.BlockSpec((planes, 2, 8, width), lambda i, _: (0, 0, jnp.minimum(i + 1, steps - 1), 0)),
                whole_block(above),
                whole_block(below),
            ],
            out_specs=[pl.BlockSpec((2, 8, width), lambda i, _: (0, i, 0))] * planes,
            scratch_shapes=[
                pltpu.VMEM((planes, 2, 8, width), f32),
                pltpu.VMEM((planes, 2, 8, width), f32),
            ],
        ),
        out_shape=[jax.ShapeDtypeStruct((2, plan.piece, width), f32)] * planes,
        compiler_params=params(),
        cost_estimate=pl.CostEstimate(flops=10**8, bytes_accessed=34 * 10**6, transcendentals=4 * 10**6),
        name="shrink_pass",
    )(scalars, moved, moved, above, below)


class Plan:
    def __init__(self, field_shape, depth, slabs):
        self.planes = depth
        self.slabs = slabs
        self.length = field_shape[-1]
        self.rows_dev = field_shape[-2]
        self.level = depth * 2
        self.cols_dev = self.length // self.level
        self.chunk = self.cols_dev // PASSES
        self.piece = self.rows_dev // depth
        self.slab_tiles = 2 * self.rows_dev // LANES


def swapped(value, axes, size, step):
    return lax.ppermute(value, axes, [(i, i ^ step) for i in range(size)])


def per_device(field, hologram, defocus):
    depth, slabs = lax.axis_size("depth"), lax.axis_size("slab")
    plan = Plan(field.shape, depth, slabs)
    length = plan.length
    d, z, c = lax.axis_index("depth"), lax.axis_index("slab"), lax.axis_index("core")
    me = d * 2 + c
    order = (z * 2 + c) * depth + d
    n_order = slabs * 2 * depth
    scalars = jnp.stack([me, d, z, c, (order == 0).astype(jnp.int32), (order == n_order - 1).astype(jnp.int32)])
    scalars = scalars.astype(jnp.int32)
    level_axes = ("depth", "core")

    forward, inverse = lane_tables()
    tables = {
        "forward": jnp.asarray(forward),
        "inverse": jnp.asarray(inverse),
        "twiddle": jnp.asarray(twiddle_table(length, 32)),
    }
    column_freqs = np.arange(32)[:, None] + 32 * np.arange(LANES)[None, :]
    cos, sin = chirp(defocus[0], column_freqs, length)
    transfer = jnp.stack([cos, -sin]) * (1.0 / length)

    own = field[:, 0]
    sent = column_pass(plan, scalars, own, tables, transfer)
    level = plan.level
    arrived = []
    for part in range(PASSES):
        group = sent[part * level : (part + 1) * level]
        arrived.append([group[0]] + [swapped(group[s], level_axes, level, s) for s in range(1, level)])

    depths = lax.all_gather(defocus, "depth", axis=0, tiled=True)
    ordered = depths[jnp.bitwise_xor(jnp.arange(depth, dtype=jnp.int32), d)]
    bases, freqs = slot_bases(length)
    cos, sin = chirp(ordered[None, :, None], freqs[:, None, :], length)
    weights = jnp.stack([cos, sin], axis=2).reshape(16, 2 * depth, 2 * LANES)
    high, low = slot_matrices(plan, jnp.asarray(bases), weights)

    slot_k = np.array([g + 4 * q for g in range(GROUPS) for q in range(4)])
    turns = (jnp.asarray(slot_k * plan.slab_tiles, jnp.int32) * z) % 32
    angle = turns.astype(f32) * (2.0 * math.pi / 32)
    unit = jnp.asarray(np.where(slot_k == 0, 1.0 / 32, 2.0 / 32), f32)
    phases = jnp.stack([jnp.cos(angle), -jnp.sin(angle), jnp.cos(angle) * unit, jnp.sin(angle) * unit])

    mine = lax.dynamic_slice_in_dim(hologram, me * plan.cols_dev, plan.cols_dev, 1)
    theirs = lax.dynamic_slice_in_dim(hologram, jnp.bitwise_xor(me, 1) * plan.cols_dev, plan.cols_dev, 1)
    theirs = swapped(theirs, "core", 2, 1)

    by_rows = own.reshape(2, depth, plan.piece, length)
    held = [lax.dynamic_index_in_dim(by_rows, jnp.bitwise_xor(d, s), 1, keepdims=False) for s in range(depth)]
    held = jnp.stack([held[0]] + [swapped(held[s], "depth", depth, s) for s in range(1, depth)])

    back = []
    for part in range(PASSES):
        span = slice(part * plan.chunk, (part + 1) * plan.chunk)
        partial = row_forward(plan, scalars, phases, arrived[part], [mine[:, span], theirs[:, span]], high, low)
        misfit = lax.psum(partial, "slab")
        group = row_backward(plan, scalars, phases, misfit, high, low)
        back.append([group[0]] + [swapped(group[s], level_axes, level, s) for s in range(1, level)])

    cos, sin = chirp(depths[:, None, None], column_freqs[None], length)
    transfer = jnp.stack([cos, sin], axis=1) * (1.0 / length)
    moved = step_pass(plan, scalars, back, held, tables, transfer)

    all_axes = ("depth", "slab", "core")
    device_at = [(i % depth) * (slabs * 2) + i // depth for i in range(n_order)]
    downward = [(device_at[i], device_at[i + 1]) for i in range(n_order - 1)]
    above = lax.ppermute(moved[:, :, -1:], all_axes, downward)
    below = lax.ppermute(moved[:, :, :1], all_axes, [(b, a) for a, b in downward])
    parts = shrink_pass(plan, scalars, moved, above, below)
    parts = [parts[0]] + [swapped(parts[s], "depth", depth, s) for s in range(1, depth)]
    stacked = jnp.stack(parts, axis=1)
    stacked = jnp.take(stacked, jnp.bitwise_xor(jnp.arange(depth, dtype=jnp.int32), d), axis=1)
    return stacked.reshape(field.shape)


def solution(mesh):
    depth, row = mesh.shape["depth"], mesh.shape["row"]
    split = Mesh(mesh.devices.reshape(depth, row // 2, 2), ("depth", "slab", "core"))
    rows = ("slab", "core")
    return jax.shard_map(
        per_device,
        mesh=split,
        in_specs=(P(None, "depth", rows, None), P(rows, None), P("depth")),
        out_specs=P(None, "depth", rows, None),
        check_vma=False,
    )
```

time: 3450 us -> 1210 us (0.35)
  blocking collectives: 1100 us -> 46.2 us
  waiting for transfers between devices: 1190 us -> 680 us
  matrix products: 456 us -> 0 us
  local copies, waits for them, and re-layouts: 412 us -> 52 us
  Pallas kernels: 0 us -> 338 us
  other arithmetic: 243 us -> 33.1 us
    all_to_all x3 -> x0, blocking collectives: 1100 us -> none  [the longest x1 369 us: per_device(): lax.all_to_all(misfit_pair, 'row', split_axis=2, concat_axis=1, tiled=True)]
    dot_general x16 -> x0, matrix products: 456 us -> none  [contract(): jnp.einsum(formula, table, data, precision=lax.Precision.HIGHEST, preferr...]
    all_to_all x1 -> x0, waiting for transfers between devices: 355 us -> none  [per_device(): lax.all_to_all(spectrum, 'row', split_axis=3, concat_axis=2, tiled=True)]
    pallas_call x0 -> x8, Pallas kernels: none -> 338 us  [the longest x2 84 us: row_backward(): pl.pallas_call(kernel, grid_spec=pltpu.PrefetchScalarGridSpec(num_scalar_...]
    psum x0 -> x1, waiting for transfers between devices: none -> 277 us  [per_device(): misfit = lax.psum(partial, 'slab')]
    ppermute x4 -> x37, waiting for transfers between devices: 667 us -> 403 us  [the longest x35 396 us: swapped(): return lax.ppermute(value, axes, [(i, i ^ step) for i in range(size)])]
    reshape x4 -> x1, local copies, waits for them, and re-layouts: 125 us -> 0.73 us  [per_device(): weights = jnp.stack([cos, sin], axis=2).reshape(16, 2 * depth, 2 * LANES)]
    all_to_all x8 -> x0, local copies, waits for them, and re-layouts: 110 us -> none  [the longest x2 31.4 us: per_device(): lax.all_to_all(spectrum, 'row', split_axis=3, concat_axis=2, tiled=True)]
  transfers between devices with their start and end apart: 7 -> 38, of which waited for: 6 -> 12; matrix products, arithmetic and copies ran while one was open for 2% -> 3% of each run, Pallas kernels for 0% -> 13%
where the time goes in v1:
time: 1210 us; the launch traced here: 1200 us
  waiting for transfers between devices  680 us (56%)
  Pallas kernels  338 us (28%)
  local copies, waits for them, and re-layouts  52 us (4%)
  blocking collectives  46.2 us (4%)
  starting transfers between devices  38.3 us (3%)
  other arithmetic  33.1 us (3%)
  between operations  14.3 us (1%)
    ppermute x35, waiting for transfers between devices, swapped(): return lax.ppermute(value, axes, [(i, i ^ step) for i in range(size)])  396 us
    psum x1, waiting for transfers between devices, per_device(): misfit = lax.psum(partial, 'slab')  277 us
    pallas_call x2, Pallas kernels, row_backward(): pl.pallas_call(kernel, grid_spec=pltpu.PrefetchScalarGridSpec(num_scalar_...  84 us
    pallas_call x2, Pallas kernels, row_forward(): pl.pallas_call(kernel, grid_spec=pltpu.PrefetchScalarGridSpec(num_scalar_...  78.9 us
    pallas_call x1, Pallas kernels, step_pass(): pl.pallas_call(kernel, grid_spec=pltpu.PrefetchScalarGridSpec(num_scalar_...  56.1 us
    pallas_call x1, Pallas kernels, column_pass(): pl.pallas_call(kernel, grid_spec=pltpu.PrefetchScalarGridSpec(num_scalar_...  53.6 us
    unnamed x1, blocking collectives  46.2 us
    ppermute x35, starting transfers between devices, swapped(): return lax.ppermute(value, axes, [(i, i ^ step) for i in range(size)])  34.6 us
  transfers between devices with their start and end apart: 38, of which 12 were waited for; matrix products, arithmetic and copies ran while one was open for 3% of the time, Pallas kernels for 13%

profile of v1, /device:TPU:0, one launch (start us, length us, event | category | flops | bytes accessed | tf_op | source)
XLA Modules:
  0.0 1202.6 jit_solution(14534208518432668444)
XLA Ops:
  7.2 0.9 cosine_bitcast_fusion
  8.7 0.7 stack.99.scal
  9.4 53.6 %column_pass.1 = (f32[2,512,256]{2,1,0:T(8,128)}, f32[2,512,256]{2,1,0:T(8,128)}, f32[2,512,256]{2,1,0:T(8,128)}, f32[2,512,256]{2,1,0:T(8,128)}, f32[2,512,256]...) custom-call(s32[6]{0:T(128)} %stack.99.scal, ...), custom_call_target="tpu_custom_call" | custom-call | flops 12999999488 | bytes 34000000 | tf_op jit(solution)/shard_map/column_pass/pallas_call | solution.py:360
  63.5 2.6 collective-permute-start.1
  66.1 1.8 collective-permute-start.3
  67.9 1.3 constant_dynamic-slice_fusion.1
  69.3 0.7 dynamic-slice
  70.0 0.8 dynamic-update-slice
  70.8 46.2 %all-reduce = f32[4]{0:T(128)S(1)} all-reduce(f32[4]{0:T(128)S(1)} %dynamic-update-slice), channel_id=1, replica_groups=mesh['depth'=4,'slab'=4,'core'=2] {'depth'}, use_global_device_ids=true, to_apply=%add | all-reduce | flops 4 | bytes 32
  118.0 0.7 copy.39.w_ref
  119.4 3.2 collective-permute-start.6
  122.7 33.2 %slot_matrices.1 = (bf16[16,256,2048]{2,1,0:T(8,128)(2,1)}, bf16[16,256,2048]{2,1,0:T(8,128)(2,1)}) custom-call(f32[16,256,256]{2,1,0:T(8,128)} %constant.133.clone.b_ref, f32[16,8,256]{2,1,0:T(8,128)} %copy.39.w_ref), custom_call_target="tpu_custom_call" | custom-call | flops 25999998976 | bytes 34000000 | tf_op jit(solution)/shard_map/slot_matrices/pallas_call | solution.py:396
  156.7 2.2 constant_dynamic-slice_fusion.2
  158.9 1.1 fusion.26
  160.0 29.4 %collective-permute-done.4.refs_5_ = f32[2,512,256]{2,1,0:T(8,128)} collective-permute-done((f32[2,512,256]{2,1,0:T(8,128)}, f32[2,512,256]{2,1,0:T(8,128)}, u32[]{:S(2)}, u32[]{:S(2)}) %collective-permute-start.4) | collective-permute-done | bytes 1048608 | tf_op jit(solution)/shard_map/ppermute | solution.py:739
  189.4 0.9 collective-permute-start.18
  190.3 0.7 collective-permute-start.19
  190.9 2.0 collective-permute-start.20
  193.0 0.8 collective-permute-start.21
  193.8 39.4 %row_forward.2 = f32[16,256,256]{2,1,0:T(8,128)} custom-call(s32[6]{0:T(128)} %stack.99.scal, f32[4,16]{1,0:T(4,128)} %pad_maximum_fusion.4.phase, f32[2,512,256]{2,1,0:T(8,128)} %get-tuple-element.43.refs_0_, f32[2,512,256]{2,1,0:T(8,128)} %collective-permute-done.refs_1_, f32[2,512,256]{2,1,0:T(8,128)} %collective-permute-done.1.refs_2_, ...), custom_call_target="tpu_custom_call" | custom-call | flops 12999999488 | bytes 60000000 | tf_op jit(solution)/shard_map/row_forward/pallas_call | solution.py:473
  233.2 27.4 %collective-permute-done.18.refs_4_ = f32[2,512,256]{2,1,0:T(8,128)S(1)} collective-permute-done((f32[2,512,256]{2,1,0:T(8,128)}, f32[2,512,256]{2,1,0:T(8,128)S(1)}, u32[]{:S(2)}, u32[]{:S(2)}) %collective-permute-start.18) | collective-permute-done | bytes 1048608 | tf_op jit(solution)/shard_map/ppermute | solution.py:739
  260.5 21.1 %collective-permute-done.19.refs_5_ = f32[2,512,256]{2,1,0:T(8,128)} collective-permute-done((f32[2,512,256]{2,1,0:T(8,128)}, f32[2,512,256]{2,1,0:T(8,128)}, u32[]{:S(2)}, u32[]{:S(2)}) %collective-permute-start.19) | collective-permute-done | bytes 1048608 | tf_op jit(solution)/shard_map/ppermute | solution.py:739
  281.6 39.6 %row_forward.3 = f32[16,256,256]{2,1,0:T(8,128)} custom-call(s32[6]{0:T(128)} %stack.99.scal, f32[4,16]{1,0:T(4,128)} %pad_maximum_fusion.4.phase, f32[2,512,256]{2,1,0:T(8,128)} %get-tuple-element.61.refs_0_, f32[2,512,256]{2,1,0:T(8,128)} %collective-permute-done.15.refs_1_, f32[2,512,256]{2,1,0:T(8,128)} %collective-permute-done.16.refs_2_, ...), custom_call_target="tpu_custom_call" | custom-call | flops 12999999488 | bytes 60000000 | tf_op jit(solution)/shard_map/row_forward/pallas_call | solution.py:473
  321.2 12.5 %dynamic-slice_bitcast_fusion.3 = (f32[1,2,128,4096]{3,2,1,0:T(8,128)}, f32[2,128,4096]{2,1,0:T(8,128)}, f32[2,128,4096]{2,1,0:T(8,128)}, f32[2,128,4096]{2,1,0:T(8,128)}) fusion(f32[2,4,128,4096]{3,2,1,0:T(8,128)} %bitcast.59, s32[]{:T(128)S(6)} %select_n.59, s32[]{:T(128)S(6)} %select_n.61, s32[]{:T(128)S(6)} %select_n.60, s32[]{:T(128)S(6)} %select_n.62), kind=kLoop, calls=%fused_computation.10 | loop fusion | bytes 33554448 | tf_op jit(solution)/shard_map/stack | solution.py:791
  333.8 2.8 collective-permute-start.31
  336.6 0.8 collective-permute-start.30
  337.4 277.1 %all-reduce.4.cloned.1.call-done = (f32[16,256,256]{2,1,0:T(8,128)}, f32[16,256,256]{2,1,0:T(8,128)}) async-done(((f32[16,256,256]{2,1,0:T(8,128)}, f32[16,256,256]{2,1,0:T(8,128)}), (f32[16,256,256]{2,1,0:T(8,128)}, f32[16,256,256]{2,1,0:T(8,128)})) %all-reduce.4.cloned.1.call-update) | async-done | bytes 8388624 | tf_op jit(solution)/shard_map/psum | solution.py:797
  614.5 41.9 %row_backward.2 = (f32[8,128,256]{2,1,0:T(8,128)}, f32[8,128,256]{2,1,0:T(8,128)}, f32[8,128,256]{2,1,0:T(8,128)}, f32[8,128,256]{2,1,0:T(8,128)}, f32[8,128,256...) custom-call(s32[6]{0:T(128)} %stack.99.scal, ...), custom_call_target="tpu_custom_call" | custom-call | flops 12999999488 | bytes 60000000 | tf_op jit(solution)/shard_map/row_backward/pallas_call | solution.py:545
  656.5 1.6 collective-permute-start.9
  658.4 1.5 collective-permute-start.11
  659.9 42.1 %row_backward.3 = (f32[8,128,256]{2,1,0:T(8,128)}, f32[8,128,256]{2,1,0:T(8,128)}, f32[8,128,256]{2,1,0:T(8,128)}, f32[8,128,256]{2,1,0:T(8,128)}, f32[8,128,256...) custom-call(s32[6]{0:T(128)} %stack.99.scal, ...), custom_call_target="tpu_custom_call" | custom-call | flops 12999999488 | bytes 60000000 | tf_op jit(solution)/shard_map/row_backward/pallas_call | solution.py:545
  702.3 2.4 collective-permute-start.13
  705.3 1.5 collective-permute-start.23
  706.8 65.7 %collective-permute-done.12.refs_5_ = f32[8,128,256]{2,1,0:T(8,128)} collective-permute-done((f32[8,128,256]{2,1,0:T(8,128)}, f32[8,128,256]{2,1,0:T(8,128)}, u32[]{:S(2)}, u32[]{:S(2)}) %collective-permute-start.12) | collective-permute-done | bytes 1048608 | tf_op jit(solution)/shard_map/ppermute | solution.py:739
  772.5 1.4 collective-permute-start.24
  774.5 1.0 collective-permute-start.26
  776.1 2.3 collective-permute-start.28
  778.7 0.7 maximum_multiply_fusion.refs_20_
  779.4 11.7 pad_maximum_fusion.refs_16_
  791.1 6.6 collective-permute-done.24.refs_11_
  797.8 1.0 copy-done.3
  798.8 46.4 %collective-permute-done.25.refs_12_ = f32[8,128,256]{2,1,0:T(8,128)S(1)} collective-permute-done((f32[8,128,256]{2,1,0:T(8,128)}, f32[8,128,256]{2,1,0:T(8,128)S(1)}, u32[]{:S(2)}, u32[]{:S(2)}) %collective-permute-start.25) | collective-permute-done | bytes 1048608 | tf_op jit(solution)/shard_map/ppermute | solution.py:739
  845.1 1.0 copy-done.4
  846.1 19.9 %collective-permute-done.26.refs_13_ = f32[8,128,256]{2,1,0:T(8,128)S(1)} collective-permute-done((f32[8,128,256]{2,1,0:T(8,128)}, f32[8,128,256]{2,1,0:T(8,128)S(1)}, u32[]{:S(2)}, u32[]{:S(2)}) %collective-permute-start.26) | collective-permute-done | bytes 1048608 | tf_op jit(solution)/shard_map/ppermute | solution.py:739
  866.0 1.0 copy-done.5
  867.0 1.0 copy-done.6
  868.0 1.0 copy-done.7
  869.0 56.1 %step_pass.1.cur.nxt = f32[4,2,128,4096]{3,2,1,0:T(8,128)} custom-call(s32[6]{0:T(128)} %stack.99.scal, f32[8,128,256]{2,1,0:T(8,128)} %get-tuple-element.53.refs_0_, f32[8,128,256]{2,1,0:T(8,128)} %copy-done, f32[8,128,256]{2,1,0:T(8,128)} %copy-done.1, f32[8,128,256]{2,1,0:T(8,128)} %copy-done.2, f32[8,128,256]{2,1,0:T(8,128)} %collective-permute-done.11.refs_4_, ...), custom_call_target="tpu_custom_call" | custom-call | flops 12999999488 | bytes 51000000 | tf_op jit(solution)/shard_map/step_pass/pallas_call | solution.py:602
  925.1 1.7 fusion.25
  926.9 2.5 collective-permute-start.32
  929.3 1.3 collective-permute-start.33
  930.6 2.2 collective-permute-done.32.up
  932.8 4.7 collective-permute-done.33.down
  938.2 32.5 %shrink_pass.1 = (f32[2,128,4096]{2,1,0:T(8,128)}, f32[2,128,4096]{2,1,0:T(8,128)}, f32[2,128,4096]{2,1,0:T(8,128)}, f32[2,128,4096]{2,1,0:T(8,128)}) custom-call(s32[6]{0:T(128)} %stack.99.scal, f32[4,2,128,4096]{3,2,1,0:T(8,128)} %step_pass.1.cur.nxt, f32[4,2,128,4096]{3,2,1,0:T(8,128)} %step_pass.1.cur.nxt, f32[4,2,1,4096]{3,2,1,0:T(1,128)} %copy-done.8, ...), custom_call_target="tpu_custom_call" | custom-call | flops 100000000 | bytes 34000000 | tf_op jit(solution)/shard_map/shrink_pass/pallas_call | solution.py:701
  970.7 2.9 collective-permute-start.36
  974.3 91.0 %collective-permute-done.36 = f32[2,128,4096]{2,1,0:T(8,128)S(1)} collective-permute-done((f32[2,128,4096]{2,1,0:T(8,128)}, f32[2,128,4096]{2,1,0:T(8,128)S(1)}, u32[]{:S(2)}, u32[]{:S(2)}) %collective-permute-start.36) | collective-permute-done | bytes 4194336 | tf_op jit(solution)/shard_map/ppermute | solution.py:739
  1065.3 88.7 %collective-permute-done.35 = f32[2,128,4096]{2,1,0:T(8,128)S(1)} collective-permute-done((f32[2,128,4096]{2,1,0:T(8,128)}, f32[2,128,4096]{2,1,0:T(8,128)S(1)}, u32[]{:S(2)}, u32[]{:S(2)}) %collective-permute-start.35) | collective-permute-done | bytes 4194336 | tf_op jit(solution)/shard_map/ppermute | solution.py:739
  1154.0 3.8 pad_maximum_fusion.1
  1157.8 6.5 fusion.24
  1164.3 7.8 gather_fusion.2
  1172.1 7.8 gather_fusion.1
  1179.8 6.7 pad_maximum_fusion.2
  1186.6 1.9 copy.37
  1188.5 7.3 bitcast_select_fusion
  (104 shorter events, 8.0 us)
Async XLA Ops:
  6.5 608.0 %all-reduce.4.cloned.1.call-start = ((), (), s32[]{:S(2)}) async-start(), calls=%async_computation | async-start | bytes 16777216 | tf_op jit(solution)/shard_map/psum | solution.py:797
  9.3 60.0 %copy-start.23 = (u32[32]{0:T(128)S(1)}, u32[32]{0:T(128)}, u32[]{:S(2)}) copy-start(u32[32]{0:T(128)} %constant.152) | copy-start | bytes 388
  9.3 108.3 %copy-start.14 = (f32[16,256]{1,0:T(8,128)S(1)}, f32[16,256]{1,0:T(8,128)}, u32[]{:S(2)}) copy-start(f32[16,256]{1,0:T(8,128)} %constant.145) | copy-start | bytes 49156
  9.3 108.3 %copy-start.15 = (f32[16,256]{1,0:T(8,128)S(1)}, f32[16,256]{1,0:T(8,128)}, u32[]{:S(2)}) copy-start(f32[16,256]{1,0:T(8,128)} %constant.144) | copy-start | bytes 49156
  9.3 108.3 %copy-start.16 = (f32[16,256]{1,0:T(8,128)S(1)}, f32[16,256]{1,0:T(8,128)}, u32[]{:S(2)}) copy-start(f32[16,256]{1,0:T(8,128)} %constant.143) | copy-start | bytes 49156
  9.3 108.3 %copy-start.17 = (f32[16,256]{1,0:T(8,128)S(1)}, f32[16,256]{1,0:T(8,128)}, u32[]{:S(2)}) copy-start(f32[16,256]{1,0:T(8,128)} %constant.142) | copy-start | bytes 49156
  63.0 55.8 %collective-permute-start = (f32[2,512,256]{2,1,0:T(8,128)}, f32[2,512,256]{2,1,0:T(8,128)}, u32[]{:S(2)}, u32[]{:S(2)}) collective-permute-start(f32[2,512,256]{2,1,0:T(8,128)} %get-tuple-element.44), channel_id=1, source_target_pairs={{0,1},{1,0},{8,9},{9,8},{16,17},{17,16},{24,25},{25,24},{2,3},{3,2... | collective-permute-start | bytes 3145736 | tf_op jit(solution)/shard_map/ppermute | solution.py:739
  63.5 55.2 %collective-permute-start.1 = (f32[2,512,256]{2,1,0:T(8,128)}, f32[2,512,256]{2,1,0:T(8,128)}, u32[]{:S(2)}, u32[]{:S(2)}) collective-permute-start(f32[2,512,256]{2,1,0:T(8,128)} %get-tuple-element.45), channel_id=1, source_target_pairs={{0,8},{1,9},{8,0},{9,1},{16,24},{17,25},{24,16},{25,17},{2,10},{3,... | collective-permute-start | bytes 3145736 | tf_op jit(solution)/shard_map/ppermute | solution.py:739
  66.1 53.3 %collective-permute-start.2 = (f32[2,512,256]{2,1,0:T(8,128)}, f32[2,512,256]{2,1,0:T(8,128)}, u32[]{:S(2)}, u32[]{:S(2)}) collective-permute-start(f32[2,512,256]{2,1,0:T(8,128)} %get-tuple-element.46), channel_id=1, source_target_pairs={{0,9},{1,8},{8,1},{9,0},{16,25},{17,24},{24,17},{25,16},{2,11},{3,... | collective-permute-start | bytes 3145736 | tf_op jit(solution)/shard_map/ppermute | solution.py:739
  66.1 56.5 %collective-permute-start.3 = (f32[2,512,256]{2,1,0:T(8,128)}, f32[2,512,256]{2,1,0:T(8,128)}, u32[]{:S(2)}, u32[]{:S(2)}) collective-permute-start(f32[2,512,256]{2,1,0:T(8,128)} %get-tuple-element.47), channel_id=1, source_target_pairs={{0,16},{1,17},{8,24},{9,25},{16,0},{17,1},{24,8},{25,9},{2,18},{3,... | collective-permute-start | bytes 3145736 | tf_op jit(solution)/shard_map/ppermute | solution.py:739
  69.2 53.4 %collective-permute-start.7 = (f32[512,512]{1,0:T(8,128)S(1)}, f32[512,512]{1,0:T(8,128)S(1)}, u32[]{:S(2)}, u32[]{:S(2)}) collective-permute-start(f32[512,512]{1,0:T(8,128)S(1)} %constant_dynamic-slice_fusion.1), channel_id=1, source_target_pairs={{0,1},{1,0},{2,3},{3,2},{4,5},{5,4},{6,7},{7,6},{8,9},{9,8},{10,11... | collective-permute-start | bytes 3145736 | tf_op jit(solution)/shard_map/ppermute | solution.py:739
  118.7 70.7 %collective-permute-start.4 = (f32[2,512,256]{2,1,0:T(8,128)}, f32[2,512,256]{2,1,0:T(8,128)}, u32[]{:S(2)}, u32[]{:S(2)}) collective-permute-start(f32[2,512,256]{2,1,0:T(8,128)} %get-tuple-element.48), channel_id=1, source_target_pairs={{0,17},{1,16},{8,25},{9,24},{16,1},{17,0},{24,9},{25,8},{2,19},{3,... | collective-permute-start | bytes 3145736 | tf_op jit(solution)/shard_map/ppermute | solution.py:739
  118.7 70.7 %collective-permute-start.5 = (f32[2,512,256]{2,1,0:T(8,128)}, f32[2,512,256]{2,1,0:T(8,128)}, u32[]{:S(2)}, u32[]{:S(2)}) collective-permute-start(f32[2,512,256]{2,1,0:T(8,128)} %get-tuple-element.49), channel_id=1, source_target_pairs={{0,24},{1,25},{8,16},{9,17},{16,8},{17,9},{24,0},{25,1},{2,26},{3,... | collective-permute-start | bytes 3145736 | tf_op jit(solution)/shard_map/ppermute | solution.py:739
  119.4 70.9 %collective-permute-start.6 = (f32[2,512,256]{2,1,0:T(8,128)}, f32[2,512,256]{2,1,0:T(8,128)}, u32[]{:S(2)}, u32[]{:S(2)}) collective-permute-start(f32[2,512,256]{2,1,0:T(8,128)} %get-tuple-element.50), channel_id=1, source_target_pairs={{0,25},{1,24},{8,17},{9,16},{16,9},{17,8},{24,1},{25,0},{2,27},{3,... | collective-permute-start | bytes 3145736 | tf_op jit(solution)/shard_map/ppermute | solution.py:739
  122.6 68.3 %collective-permute-start.15 = (f32[2,512,256]{2,1,0:T(8,128)}, f32[2,512,256]{2,1,0:T(8,128)}, u32[]{:S(2)}, u32[]{:S(2)}) collective-permute-start(f32[2,512,256]{2,1,0:T(8,128)} %get-tuple-element.62), channel_id=1, source_target_pairs={{0,1},{1,0},{8,9},{9,8},{16,17},{17,16},{24,25},{25,24},{2,3},{3,2... | collective-permute-start | bytes 3145736 | tf_op jit(solution)/shard_map/ppermute | solution.py:739
  122.6 33.3 %copy-start.19 = (s32[16]{0:T(128)S(1)}, s32[16]{0:T(128)}, u32[]{:S(2)}) copy-start(s32[16]{0:T(128)} %constant.134.clone) | copy-start | bytes 196
  122.6 33.4 %copy-start.18 = (f32[16]{0:T(128)S(1)}, f32[16]{0:T(128)}, u32[]{:S(2)}) copy-start(f32[16]{0:T(128)} %constant.135.clone) | copy-start | bytes 196
  122.6 70.3 %copy-start.20 = (f32[2,512,256]{2,1,0:T(8,128)S(1)}, f32[2,512,256]{2,1,0:T(8,128)}, u32[]{:S(2)}) copy-start(f32[2,512,256]{2,1,0:T(8,128)} %get-tuple-element.68) | copy-start | bytes 3145732
  122.7 70.3 %collective-permute-start.16 = (f32[2,512,256]{2,1,0:T(8,128)}, f32[2,512,256]{2,1,0:T(8,128)}, u32[]{:S(2)}, u32[]{:S(2)}) collective-permute-start(f32[2,512,256]{2,1,0:T(8,128)} %get-tuple-element.63), channel_id=1, source_target_pairs={{0,8},{1,9},{8,0},{9,1},{16,24},{17,25},{24,16},{25,17},{2,10},{3,... | collective-permute-start | bytes 3145736 | tf_op jit(solution)/shard_map/ppermute | solution.py:739
  189.4 43.8 %collective-permute-start.17 = (f32[2,512,256]{2,1,0:T(8,128)}, f32[2,512,256]{2,1,0:T(8,128)S(1)}, u32[]{:S(2)}, u32[]{:S(2)}) collective-permute-start(f32[2,512,256]{2,1,0:T(8,128)} %get-tuple-element.64), channel_id=1, source_target_pairs={{0,9},{1,8},{8,1},{9,0},{16,25},{17,24},{24,17},{25,16},{2,11},{3,... | collective-permute-start | bytes 3145736 | tf_op jit(solution)/shard_map/ppermute | solution.py:739
  189.4 71.2 %collective-permute-start.18 = (f32[2,512,256]{2,1,0:T(8,128)}, f32[2,512,256]{2,1,0:T(8,128)S(1)}, u32[]{:S(2)}, u32[]{:S(2)}) collective-permute-start(f32[2,512,256]{2,1,0:T(8,128)} %get-tuple-element.65), channel_id=1, source_target_pairs={{0,16},{1,17},{8,24},{9,25},{16,0},{17,1},{24,8},{25,9},{2,18},{3,... | collective-permute-start | bytes 3145736 | tf_op jit(solution)/shard_map/ppermute | solution.py:739
  190.3 91.3 %collective-permute-start.19 = (f32[2,512,256]{2,1,0:T(8,128)}, f32[2,512,256]{2,1,0:T(8,128)}, u32[]{:S(2)}, u32[]{:S(2)}) collective-permute-start(f32[2,512,256]{2,1,0:T(8,128)} %get-tuple-element.66), channel_id=1, source_target_pairs={{0,17},{1,16},{8,25},{9,24},{16,1},{17,0},{24,9},{25,8},{2,19},{3,... | collective-permute-start | bytes 3145736 | tf_op jit(solution)/shard_map/ppermute | solution.py:739
  190.9 90.7 %collective-permute-start.20 = (f32[2,512,256]{2,1,0:T(8,128)}, f32[2,512,256]{2,1,0:T(8,128)}, u32[]{:S(2)}, u32[]{:S(2)}) collective-permute-start(f32[2,512,256]{2,1,0:T(8,128)} %get-tuple-element.67), channel_id=1, source_target_pairs={{0,24},{1,25},{8,16},{9,17},{16,8},{17,9},{24,0},{25,1},{2,26},{3,... | collective-permute-start | bytes 3145736 | tf_op jit(solution)/shard_map/ppermute | solution.py:739
  193.0 88.6 %collective-permute-start.21 = (f32[2,512,256]{2,1,0:T(8,128)S(1)}, f32[2,512,256]{2,1,0:T(8,128)}, u32[]{:S(2)}, u32[]{:S(2)}) collective-permute-start(f32[2,512,256]{2,1,0:T(8,128)S(1)} %copy-done.20), channel_id=1, source_target_pairs={{0,25},{1,24},{8,17},{9,16},{16,9},{17,8},{24,1},{25,0},{2,27},{3,... | collective-permute-start | bytes 3145736 | tf_op jit(solution)/shard_map/ppermute | solution.py:739
  233.2 48.4 %copy-start.21 = (f32[2,512,256]{2,1,0:T(8,128)}, f32[2,512,256]{2,1,0:T(8,128)S(1)}, u32[]{:S(2)}) copy-start(f32[2,512,256]{2,1,0:T(8,128)S(1)} %collective-permute-done.17.refs_3_) | copy-start | bytes 3145732
  260.5 21.1 %copy-start.22 = (f32[2,512,256]{2,1,0:T(8,128)}, f32[2,512,256]{2,1,0:T(8,128)S(1)}, u32[]{:S(2)}) copy-start(f32[2,512,256]{2,1,0:T(8,128)S(1)} %collective-permute-done.18.refs_4_) | copy-start | bytes 3145732
  333.8 324.3 %collective-permute-start.31 = (f32[2,128,4096]{2,1,0:T(8,128)}, f32[2,128,4096]{2,1,0:T(8,128)}, u32[]{:S(2)}, u32[]{:S(2)}) collective-permute-start(f32[2,128,4096]{2,1,0:T(8,128)} %get-tuple-element.92), channel_id=1, source_target_pairs={{0,24},{8,16},{16,8},{24,0},{1,25},{9,17},{17,9},{25,1},{2,26},{10... | collective-permute-start | bytes 12582920 | tf_op jit(solution)/shard_map/ppermute | solution.py:739
  336.6 321.8 %collective-permute-start.30 = (f32[2,128,4096]{2,1,0:T(8,128)}, f32[2,128,4096]{2,1,0:T(8,128)}, u32[]{:S(2)}, u32[]{:S(2)}) collective-permute-start(f32[2,128,4096]{2,1,0:T(8,128)} %get-tuple-element.90), channel_id=1, source_target_pairs={{0,16},{8,24},{16,0},{24,8},{1,17},{9,25},{17,1},{25,9},{2,18},{10... | collective-permute-start | bytes 12582920 | tf_op jit(solution)/shard_map/ppermute | solution.py:739
  337.4 364.6 %collective-permute-start.29 = (f32[2,128,4096]{2,1,0:T(8,128)}, f32[2,128,4096]{2,1,0:T(8,128)}, u32[]{:S(2)}, u32[]{:S(2)}) collective-permute-start(f32[2,128,4096]{2,1,0:T(8,128)} %get-tuple-element.91), channel_id=1, source_target_pairs={{0,8},{8,0},{16,24},{24,16},{1,9},{9,1},{17,25},{25,17},{2,10},{10... | collective-permute-start | bytes 12582920 | tf_op jit(solution)/shard_map/ppermute | solution.py:739
  656.4 45.8 %collective-permute-start.8 = (f32[8,128,256]{2,1,0:T(8,128)}, f32[8,128,256]{2,1,0:T(8,128)S(1)}, u32[]{:S(2)}, u32[]{:S(2)}) collective-permute-start(f32[8,128,256]{2,1,0:T(8,128)} %get-tuple-element.54), channel_id=1, source_target_pairs={{0,1},{1,0},{8,9},{9,8},{16,17},{17,16},{24,25},{25,24},{2,3},{3,2... | collective-permute-start | bytes 3145736 | tf_op jit(solution)/shard_map/ppermute | solution.py:739
  656.5 48.2 %collective-permute-start.9 = (f32[8,128,256]{2,1,0:T(8,128)}, f32[8,128,256]{2,1,0:T(8,128)S(1)}, u32[]{:S(2)}, u32[]{:S(2)}) collective-permute-start(f32[8,128,256]{2,1,0:T(8,128)} %get-tuple-element.55), channel_id=1, source_target_pairs={{0,8},{1,9},{8,0},{9,1},{16,24},{17,25},{24,16},{25,17},{2,10},{3,... | collective-permute-start | bytes 3145736 | tf_op jit(solution)/shard_map/ppermute | solution.py:739
  658.1 46.9 %collective-permute-start.10 = (f32[8,128,256]{2,1,0:T(8,128)}, f32[8,128,256]{2,1,0:T(8,128)S(1)}, u32[]{:S(2)}, u32[]{:S(2)}) collective-permute-start(f32[8,128,256]{2,1,0:T(8,128)} %get-tuple-element.56), channel_id=1, source_target_pairs={{0,9},{1,8},{8,1},{9,0},{16,25},{17,24},{24,17},{25,16},{2,11},{3,... | collective-permute-start | bytes 3145736 | tf_op jit(solution)/shard_map/ppermute | solution.py:739
  658.4 46.9 %collective-permute-start.11 = (f32[8,128,256]{2,1,0:T(8,128)}, f32[8,128,256]{2,1,0:T(8,128)}, u32[]{:S(2)}, u32[]{:S(2)}) collective-permute-start(f32[8,128,256]{2,1,0:T(8,128)} %get-tuple-element.57), channel_id=1, source_target_pairs={{0,16},{1,17},{8,24},{9,25},{16,0},{17,1},{24,8},{25,9},{2,18},{3,... | collective-permute-start | bytes 3145736 | tf_op jit(solution)/shard_map/ppermute | solution.py:739
  659.9 118.5 %copy-start.10 = (f32[32,128]{1,0:T(8,128)S(1)}, f32[32,128]{1,0:T(8,128)}, u32[]{:S(2)}) copy-start(f32[32,128]{1,0:T(8,128)} %constant.128.clone) | copy-start | bytes 49156
  659.9 118.5 %copy-start.11 = (f32[32,128]{1,0:T(8,128)S(1)}, f32[32,128]{1,0:T(8,128)}, u32[]{:S(2)}) copy-start(f32[32,128]{1,0:T(8,128)} %constant.127.clone) | copy-start | bytes 49156
  659.9 118.5 %copy-start.12 = (f32[32,128]{1,0:T(8,128)S(1)}, f32[32,128]{1,0:T(8,128)}, u32[]{:S(2)}) copy-start(f32[32,128]{1,0:T(8,128)} %constant.126.clone) | copy-start | bytes 49156
  659.9 118.5 %copy-start.13 = (f32[32,128]{1,0:T(8,128)S(1)}, f32[32,128]{1,0:T(8,128)}, u32[]{:S(2)}) copy-start(f32[32,128]{1,0:T(8,128)} %constant.125.clone) | copy-start | bytes 49156
  702.0 70.5 %collective-permute-start.12 = (f32[8,128,256]{2,1,0:T(8,128)}, f32[8,128,256]{2,1,0:T(8,128)}, u32[]{:S(2)}, u32[]{:S(2)}) collective-permute-start(f32[8,128,256]{2,1,0:T(8,128)} %get-tuple-element.58), channel_id=1, source_target_pairs={{0,17},{1,16},{8,25},{9,24},{16,1},{17,0},{24,9},{25,8},{2,19},{3,... | collective-permute-start | bytes 3145736 | tf_op jit(solution)/shard_map/ppermute | solution.py:739
  702.2 88.9 %copy-start = (f32[8,128,256]{2,1,0:T(8,128)}, f32[8,128,256]{2,1,0:T(8,128)S(1)}, u32[]{:S(2)}) copy-start(f32[8,128,256]{2,1,0:T(8,128)S(1)} %collective-permute-done.8.refs_1_) | copy-start | bytes 3145732
  702.3 71.7 %collective-permute-start.13 = (f32[8,128,256]{2,1,0:T(8,128)}, f32[8,128,256]{2,1,0:T(8,128)}, u32[]{:S(2)}, u32[]{:S(2)}) collective-permute-start(f32[8,128,256]{2,1,0:T(8,128)} %get-tuple-element.59), channel_id=1, source_target_pairs={{0,24},{1,25},{8,16},{9,17},{16,8},{17,9},{24,0},{25,1},{2,26},{3,... | collective-permute-start | bytes 3145736 | tf_op jit(solution)/shard_map/ppermute | solution.py:739
  704.7 86.5 %copy-start.1 = (f32[8,128,256]{2,1,0:T(8,128)}, f32[8,128,256]{2,1,0:T(8,128)S(1)}, u32[]{:S(2)}) copy-start(f32[8,128,256]{2,1,0:T(8,128)S(1)} %collective-permute-done.9.refs_2_) | copy-start | bytes 3145732
  704.7 69.9 %collective-permute-start.14 = (f32[8,128,256]{2,1,0:T(8,128)}, f32[8,128,256]{2,1,0:T(8,128)}, u32[]{:S(2)}, u32[]{:S(2)}) collective-permute-start(f32[8,128,256]{2,1,0:T(8,128)} %get-tuple-element.60), channel_id=1, source_target_pairs={{0,25},{1,24},{8,17},{9,16},{16,9},{17,8},{24,1},{25,0},{2,27},{3,... | collective-permute-start | bytes 3145736 | tf_op jit(solution)/shard_map/ppermute | solution.py:739
  705.0 86.2 %copy-start.2 = (f32[8,128,256]{2,1,0:T(8,128)}, f32[8,128,256]{2,1,0:T(8,128)S(1)}, u32[]{:S(2)}) copy-start(f32[8,128,256]{2,1,0:T(8,128)S(1)} %collective-permute-done.10.refs_3_) | copy-start | bytes 3145732
  705.0 70.5 %collective-permute-start.22 = (f32[8,128,256]{2,1,0:T(8,128)}, f32[8,128,256]{2,1,0:T(8,128)}, u32[]{:S(2)}, u32[]{:S(2)}) collective-permute-start(f32[8,128,256]{2,1,0:T(8,128)} %get-tuple-element.70), channel_id=1, source_target_pairs={{0,1},{1,0},{8,9},{9,8},{16,17},{17,16},{24,25},{25,24},{2,3},{3,2... | collective-permute-start | bytes 3145736 | tf_op jit(solution)/shard_map/ppermute | solution.py:739
  705.3 70.8 %collective-permute-start.23 = (f32[8,128,256]{2,1,0:T(8,128)}, f32[8,128,256]{2,1,0:T(8,128)}, u32[]{:S(2)}, u32[]{:S(2)}) collective-permute-start(f32[8,128,256]{2,1,0:T(8,128)} %get-tuple-element.71), channel_id=1, source_target_pairs={{0,8},{1,9},{8,0},{9,1},{16,24},{17,25},{24,16},{25,17},{2,10},{3,... | collective-permute-start | bytes 3145736 | tf_op jit(solution)/shard_map/ppermute | solution.py:739
  772.5 25.2 %collective-permute-start.24 = (f32[8,128,256]{2,1,0:T(8,128)}, f32[8,128,256]{2,1,0:T(8,128)S(1)}, u32[]{:S(2)}, u32[]{:S(2)}) collective-permute-start(f32[8,128,256]{2,1,0:T(8,128)} %get-tuple-element.72), channel_id=1, source_target_pairs={{0,9},{1,8},{8,1},{9,0},{16,25},{17,24},{24,17},{25,16},{2,11},{3,... | collective-permute-start | bytes 3145736 | tf_op jit(solution)/shard_map/ppermute | solution.py:739
  774.0 71.2 %collective-permute-start.25 = (f32[8,128,256]{2,1,0:T(8,128)}, f32[8,128,256]{2,1,0:T(8,128)S(1)}, u32[]{:S(2)}, u32[]{:S(2)}) collective-permute-start(f32[8,128,256]{2,1,0:T(8,128)} %get-tuple-element.73), channel_id=1, source_target_pairs={{0,16},{1,17},{8,24},{9,25},{16,0},{17,1},{24,8},{25,9},{2,18},{3,... | collective-permute-start | bytes 3145736 | tf_op jit(solution)/shard_map/ppermute | solution.py:739
  774.5 91.5 %collective-permute-start.26 = (f32[8,128,256]{2,1,0:T(8,128)}, f32[8,128,256]{2,1,0:T(8,128)S(1)}, u32[]{:S(2)}, u32[]{:S(2)}) collective-permute-start(f32[8,128,256]{2,1,0:T(8,128)} %get-tuple-element.74), channel_id=1, source_target_pairs={{0,17},{1,16},{8,25},{9,24},{16,1},{17,0},{24,9},{25,8},{2,19},{3,... | collective-permute-start | bytes 3145736 | tf_op jit(solution)/shard_map/ppermute | solution.py:739
  775.5 91.5 %collective-permute-start.27 = (f32[8,128,256]{2,1,0:T(8,128)}, f32[8,128,256]{2,1,0:T(8,128)S(1)}, u32[]{:S(2)}, u32[]{:S(2)}) collective-permute-start(f32[8,128,256]{2,1,0:T(8,128)} %get-tuple-element.75), channel_id=1, source_target_pairs={{0,24},{1,25},{8,16},{9,17},{16,8},{17,9},{24,0},{25,1},{2,26},{3,... | collective-permute-start | bytes 3145736 | tf_op jit(solution)/shard_map/ppermute | solution.py:739
  776.1 91.9 %collective-permute-start.28 = (f32[8,128,256]{2,1,0:T(8,128)}, f32[8,128,256]{2,1,0:T(8,128)S(1)}, u32[]{:S(2)}, u32[]{:S(2)}) collective-permute-start(f32[8,128,256]{2,1,0:T(8,128)} %get-tuple-element.76), channel_id=1, source_target_pairs={{0,25},{1,24},{8,17},{9,16},{16,9},{17,8},{24,1},{25,0},{2,27},{3,... | collective-permute-start | bytes 3145736 | tf_op jit(solution)/shard_map/ppermute | solution.py:739
  797.8 1.0 copy-start.3
  845.1 1.0 copy-start.4
  866.0 1.0 copy-start.5
  867.0 1.0 copy-start.6
  868.0 1.0 copy-start.7
  926.9 6.0 collective-permute-start.32
  929.3 8.2 collective-permute-start.33
  932.8 4.7 copy-start.8
  937.6 0.6 copy-start.9
  970.7 94.6 %collective-permute-start.36 = (f32[2,128,4096]{2,1,0:T(8,128)}, f32[2,128,4096]{2,1,0:T(8,128)S(1)}, u32[]{:S(2)}, u32[]{:S(2)}) collective-permute-start(f32[2,128,4096]{2,1,0:T(8,128)} %get-tuple-element.80), channel_id=1, source_target_pairs={{0,24},{8,16},{16,8},{24,0},{1,25},{9,17},{17,9},{25,1},{2,26},{10... | collective-permute-start | bytes 12582920 | tf_op jit(solution)/shard_map/ppermute | solution.py:739
  973.6 180.4 %collective-permute-start.35 = (f32[2,128,4096]{2,1,0:T(8,128)}, f32[2,128,4096]{2,1,0:T(8,128)S(1)}, u32[]{:S(2)}, u32[]{:S(2)}) collective-permute-start(f32[2,128,4096]{2,1,0:T(8,128)} %get-tuple-element.79), channel_id=1, source_target_pairs={{0,16},{8,24},{16,0},{24,8},{1,17},{9,25},{17,1},{25,9},{2,18},{10... | collective-permute-start | bytes 12582920 | tf_op jit(solution)/shard_map/ppermute | solution.py:739
  973.9 180.1 %collective-permute-start.34 = (f32[2,128,4096]{2,1,0:T(8,128)}, f32[2,128,4096]{2,1,0:T(8,128)S(1)}, u32[]{:S(2)}, u32[]{:S(2)}) collective-permute-start(f32[2,128,4096]{2,1,0:T(8,128)} %get-tuple-element.78), channel_id=1, source_target_pairs={{0,8},{8,0},{16,24},{24,16},{1,9},{9,1},{17,25},{25,17},{2,10},{10... | collective-permute-start | bytes 12582920 | tf_op jit(solution)/shard_map/ppermute | solution.py:739
Sparse Core Ops, SparseCore 0:
  321.3 293.1 all-reduce.3

commit v2 on v1

--- a/solution.py
+++ b/solution.py
@@ -12,7 +12,6 @@
 tv_sharpness = 0.25
 LANES = 128
 GROUPS = 4
-PASSES = 2
 VMEM_BYTES = 60 * 1024 * 1024
 f32 = jnp.float32
 bf16 = jnp.bfloat16
@@ -240,16 +239,6 @@
             parts[span, (2 + at) * LANES : (3 + at) * LANES] = low
             parts[span, (4 + at) * LANES : (5 + at) * LANES] = high
 
-    def multiply(table_ref):
-        step = min(512, 32 * rows)
-
-        def body(i, carry):
-            span = pl.ds(i * step, step)
-            spec[span, :] = dot(parts[span, :], table_ref[...])
-            return carry
-
-        lax.fori_loop(0, 32 * rows // step, body, 0)
-
     def forward(i, carry):
         row = i * 16
         span = pl.ds(row, 16)
@@ -271,18 +260,22 @@
         return carry
 
     lax.fori_loop(0, rows // 16, forward, 0)
-    multiply(forward_ref)
-
-    def middle(tile, carry):
-        tr, ti = transfer(tile)
-        for row in range(0, rows, 16):
-            span = pl.ds(tile * rows + row, 16)
-            re, im = spec[span, :LANES], spec[span, LANES:]
-            put_parts(tile, row, (re * tr - im * ti, re * ti + im * tr))
+    batch = max(1, min(4, 256 // rows))
+
+    def middle(i, carry):
+        span = pl.ds(i * batch * rows, batch * rows)
+        value = dot(parts[span, :], forward_ref[...])
+        pieces = []
+        for t in range(batch):
+            tr, ti = transfer(i * batch + t)
+            re = value[t * rows : (t + 1) * rows, :LANES]
+            im = value[t * rows : (t + 1) * rows, LANES:]
+            pieces.append(jnp.concatenate([re * tr - im * ti, re * ti + im * tr], axis=1))
+        high, low = two_parts(jnp.concatenate(pieces, axis=0))
+        spec[span, :] = dot(jnp.concatenate([high, low, high], axis=1), inverse_ref[...])
         return carry
 
-    lax.fori_loop(0, 32, middle, 0)
-    multiply(inverse_ref)
+    lax.fori_loop(0, 32 // batch, middle, 0, unroll=2)
 
     def inverse(i, carry):
         row = i * 16
@@ -327,50 +320,40 @@
     return pl.BlockSpec(array.shape, lambda *_: (0,) * rank)
 
 
-def column_pass(plan, scalars, field, tables, transfer):
+def column_pass(plan, field, tables, transfer):
     rows = min(64, plan.rows_dev)
-    level, chunk, cols = plan.level, plan.chunk, plan.cols_dev
-    per_piece = cols // LANES
-    n_out = level * PASSES
-
-    def kernel(scal, f_ref, fwd, inv, twd, tra, *rest):
-        outs, (work, parts, spec, staged) = rest[:n_out], rest[n_out:]
+    level, count = plan.level, len(plan.chunks)
+
+    def kernel(f_ref, fwd, inv, twd, tra, *rest):
+        outs, (work, parts, spec) = rest[:count], rest[count:]
 
         def load(tile, row):
             at = slice(tile * LANES, (tile + 1) * LANES)
             return (f_ref[0, pl.ds(row, 16), at], f_ref[1, pl.ds(row, 16), at])
 
         def store(tile, row, value):
-            staged[tile, 0, pl.ds(row, 16), :] = value[0]
-            staged[tile, 1, pl.ds(row, 16), :] = value[1]
+            owner, part, at = plan.place_of(tile)
+            outs[part][owner, 0, pl.ds(row, 16), at] = value[0]
+            outs[part][owner, 1, pl.ds(row, 16), at] = value[1]
 
         def pick(tile):
             return tra[0, pl.ds(tile, 1), :], tra[1, pl.ds(tile, 1), :]
 
         lane_convolve(rows, load, store, work, parts, spec, fwd, inv, twd, pick)
-        for part in range(PASSES):
-            for s in range(level):
-                first = jnp.bitwise_xor(scal[0], s) * per_piece + part * (chunk // LANES)
-                for t in range(chunk // LANES):
-                    for ri in range(2):
-                        outs[part * level + s][ri, :, t * LANES : (t + 1) * LANES] = staged[first + t, ri]
 
     width = field.shape[-1]
     fixed = [tables["forward"], tables["inverse"], tables["twiddle"], transfer]
     return pl.pallas_call(
         kernel,
-        grid_spec=pltpu.PrefetchScalarGridSpec(
-            num_scalar_prefetch=1,
-            grid=(plan.rows_dev // rows,),
-            in_specs=[pl.BlockSpec((2, rows, width), lambda i, _: (0, i, 0))] + [whole_block(a) for a in fixed],
-            out_specs=[pl.BlockSpec((2, rows, chunk), lambda i, _: (0, i, 0))] * n_out,
-            scratch_shapes=lane_scratch(rows) + [pltpu.VMEM((32, 2, rows, LANES), f32)],
-        ),
-        out_shape=[jax.ShapeDtypeStruct((2, plan.rows_dev, chunk), f32)] * n_out,
+        grid=(plan.rows_dev // rows,),
+        in_specs=[pl.BlockSpec((2, rows, width), lambda i: (0, i, 0))] + [whole_block(a) for a in fixed],
+        out_specs=[pl.BlockSpec((level, 2, rows, w), lambda i: (0, 0, i, 0)) for w in plan.chunks],
+        scratch_shapes=lane_scratch(rows),
+        out_shape=[jax.ShapeDtypeStruct((level, 2, plan.rows_dev, w), f32) for w in plan.chunks],
         compiler_params=params(),
         cost_estimate=pl.CostEstimate(flops=13 * 10**9, bytes_accessed=34 * 10**6, transcendentals=0),
         name="column_pass",
-    )(scalars, field, *fixed)
+    )(field, *fixed)
 
 
 def slot_matrices(plan, bases, weights):
@@ -408,23 +391,14 @@
     )(bases, weights)
 
 
-def row_forward(plan, scalars, phases, pieces, holos, high, low):
-    level, chunk, count = plan.level, plan.chunk, plan.slab_tiles
+def row_forward(plan, phases, pieces, holos, high, low):
+    count = plan.slab_tiles
+    chunk = pieces.shape[-1]
     kinds = plan.planes * 2
     size = 2 * LANES
     half = count // 2
 
-    def kernel(scal, phase, *refs):
-        x_refs, (h0, h1, wh, wl, out, eh, el, eo) = refs[:level], refs[level:]
-        flip = scal[3] != 0
-
-        def tiles(first, second, row):
-            left = [first(j, row) for j in range(half)]
-            right = [second(j, row) for j in range(half)]
-            lower = [jnp.where(flip, b, a) for a, b in zip(left, right)]
-            upper = [jnp.where(flip, a, b) for a, b in zip(left, right)]
-            return lower + upper
-
+    def kernel(phase, x_ref, h_ref, wh, wl, out, eh, el, eo):
         for group in range(GROUPS):
 
             @pl.when(pl.program_id(0) == group)
@@ -434,27 +408,22 @@
                     for kind in range(kinds):
                         t, ri = kind // 2, kind % 2
 
-                        def first(j, row, t=t, ri=ri):
-                            return x_refs[2 * t][ri, pl.ds(j * LANES + row, 16), :]
-
-                        def second(j, row, t=t, ri=ri):
-                            return x_refs[2 * t + 1][ri, pl.ds(j * LANES + row, 16), :]
-
-                        outs = slab_forward(tiles(first, second, row), group)
+                        x = []
+                        for j in range(count):
+                            span = pl.ds((j % half) * LANES + row, 16)
+                            x.append(x_ref[2 * t + j // half, ri, span, :])
+                        outs = slab_forward(x, group)
                         for q in range(4):
                             for at in range(2):
                                 a, b = two_parts(outs[q][at])
                                 span = pl.ds(kind * size + at * LANES + row, 16)
                                 eh[q, span, :] = a
                                 el[q, span, :] = b
-                    held = slab_forward(
-                        tiles(
-                            lambda j, row: h0[pl.ds(j * LANES + row, 16), :],
-                            lambda j, row: h1[pl.ds(j * LANES + row, 16), :],
-                            row,
-                        ),
-                        group,
-                    )
+                    x = []
+                    for j in range(count):
+                        span = pl.ds((j % half) * LANES + row, 16)
+                        x.append(h_ref[j // half, span, :])
+                    held = slab_forward(x, group)
                     for q in range(4):
                         for at in range(2):
                             eo[q, pl.ds(at * LANES + row, 16), :] = held[q][at]
@@ -473,10 +442,9 @@
     return pl.pallas_call(
         kernel,
         grid_spec=pltpu.PrefetchScalarGridSpec(
-            num_scalar_prefetch=2,
+            num_scalar_prefetch=1,
             grid=(GROUPS,),
-            in_specs=[whole_block(a) for a in pieces]
-            + [whole_block(a) for a in holos]
+            in_specs=[whole_block(pieces), whole_block(holos)]
             + [pl.BlockSpec((4, size, kinds * size), lambda g, *_: (g, 0, 0))] * 2,
             out_specs=pl.BlockSpec((4, size, chunk), lambda g, *_: (g, 0, 0)),
             scratch_shapes=[
@@ -489,16 +457,16 @@
         compiler_params=params(),
         cost_estimate=pl.CostEstimate(flops=13 * 10**9, bytes_accessed=60 * 10**6, transcendentals=0),
         name="row_forward",
-    )(scalars, phases, *pieces, *holos, high, low)
-
-
-def row_backward(plan, scalars, phases, misfit, high, low):
-    level, chunk, count = plan.level, plan.chunk, plan.slab_tiles
+    )(phases, pieces, holos, high, low)
+
+
+def row_backward(plan, phases, misfit, high, low):
+    level, count = plan.level, plan.slab_tiles
+    chunk = misfit.shape[-1]
     size = 2 * LANES
     piece = plan.piece
 
-    def kernel(scal, phase, m_ref, wh, wl, *rest):
-        outs, (mh, ml, field) = rest[:level], rest[level:]
+    def kernel(phase, m_ref, wh, wl, out, mh, ml, field):
         kind, step = pl.program_id(0), pl.program_id(1)
 
         @pl.when(kind == 0)
@@ -533,59 +501,47 @@
         @pl.when(step == GROUPS - 1)
         def _():
             for s in range(level):
-                other = jnp.bitwise_xor(scal[0], s)
-                start = jnp.bitwise_and(other, 1) * plan.rows_dev + jnp.right_shift(other, 1) * piece
-                outs[s][0] = field[pl.ds(pl.multiple_of(start, 16), piece), :]
+                start = (s % 2) * plan.rows_dev + (s // 2) * piece
+                out[s, 0] = field[start : start + piece, :]
 
     kinds = plan.planes * 2
-
-    def weight_at(kind, step, scal, phase):
-        return (step, 0, jnp.bitwise_xor(kind // 2, scal[1]) * 2 + kind % 2)
 
     return pl.pallas_call(
         kernel,
         grid_spec=pltpu.PrefetchScalarGridSpec(
-            num_scalar_prefetch=2,
+            num_scalar_prefetch=1,
             grid=(kinds, GROUPS),
             in_specs=[
-                pl.BlockSpec((4, size, chunk), lambda kind, step, *_: (jnp.where(kind == 0, step, GROUPS - 1), 0, 0)),
-                pl.BlockSpec((4, size, size), weight_at),
-                pl.BlockSpec((4, size, size), weight_at),
+                pl.BlockSpec((4, size, chunk), lambda kind, step, _: (jnp.where(kind == 0, step, GROUPS - 1), 0, 0)),
+                pl.BlockSpec((4, size, size), lambda kind, step, _: (step, 0, kind)),
+                pl.BlockSpec((4, size, size), lambda kind, step, _: (step, 0, kind)),
             ],
-            out_specs=[pl.BlockSpec((1, piece, chunk), lambda kind, step, *_: (kind, 0, 0))] * level,
+            out_specs=pl.BlockSpec((level, 1, piece, chunk), lambda kind, step, _: (0, kind, 0, 0)),
             scratch_shapes=[
                 pltpu.VMEM((16, size, chunk), bf16),
                 pltpu.VMEM((16, size, chunk), bf16),
                 pltpu.VMEM((count * LANES, chunk), f32),
             ],
         ),
-        out_shape=[jax.ShapeDtypeStruct((kinds, piece, chunk), f32)] * level,
+        out_shape=jax.ShapeDtypeStruct((level, kinds, piece, chunk), f32),
         compiler_params=params(),
         cost_estimate=pl.CostEstimate(flops=13 * 10**9, bytes_accessed=60 * 10**6, transcendentals=0),
         name="row_backward",
-    )(scalars, phases, misfit, high, low)
-
-
-def step_pass(plan, scalars, pieces, held, tables, transfer):
+    )(phases, misfit, high, low)
+
+
+def step_pass(plan, pieces, held, tables, transfer):
     rows = min(64, plan.piece)
-    level, chunk = plan.level, plan.chunk
+    level, count = plan.level, len(plan.chunks)
     width = held.shape[-1]
-    per_piece = plan.cols_dev // LANES
-    n_in = level * PASSES
-    flat = [piece for part in pieces for piece in part]
     scale = 1.0 / plan.planes
 
-    def kernel(scal, *refs):
-        g_refs, (h_ref, fwd, inv, twd, tra, out, work, parts, spec, staged) = refs[:n_in], refs[n_in:]
-        for part in range(PASSES):
-            for s in range(level):
-                first = jnp.bitwise_xor(scal[0], s) * per_piece + part * (chunk // LANES)
-                for t in range(chunk // LANES):
-                    for ri in range(2):
-                        staged[first + t, ri] = g_refs[part * level + s][ri, :, t * LANES : (t + 1) * LANES]
+    def kernel(*refs):
+        g_refs, (h_ref, fwd, inv, twd, tra, out, work, parts, spec) = refs[:count], refs[count:]
 
         def load(tile, row):
-            return (staged[tile, 0, pl.ds(row, 16), :], staged[tile, 1, pl.ds(row, 16), :])
+            owner, part, at = plan.place_of(tile)
+            return (g_refs[part][owner, 0, pl.ds(row, 16), at], g_refs[part][owner, 1, pl.ds(row, 16), at])
 
         def store(tile, row, value):
             at = slice(tile * LANES, (tile + 1) * LANES)
@@ -601,35 +557,33 @@
     fixed = [tables["forward"], tables["inverse"], tables["twiddle"]]
     return pl.pallas_call(
         kernel,
-        grid_spec=pltpu.PrefetchScalarGridSpec(
-            num_scalar_prefetch=1,
-            grid=(plan.planes, plan.piece // rows),
-            in_specs=[pl.BlockSpec((2, rows, chunk), lambda p, i, _: (p, i, 0))] * n_in
-            + [pl.BlockSpec((1, 2, rows, width), lambda p, i, scal: (jnp.bitwise_xor(p, scal[1]), 0, i, 0))]
-            + [whole_block(a) for a in fixed]
-            + [pl.BlockSpec((1, 2, 32, LANES), lambda p, i, _: (p, 0, 0, 0))],
-            out_specs=pl.BlockSpec((1, 2, rows, width), lambda p, i, _: (p, 0, i, 0)),
-            scratch_shapes=lane_scratch(rows) + [pltpu.VMEM((32, 2, rows, LANES), f32)],
-        ),
+        grid=(plan.planes, plan.piece // rows),
+        in_specs=[pl.BlockSpec((level, 2, rows, w), lambda p, i: (0, p, i, 0)) for w in plan.chunks]
+        + [pl.BlockSpec((1, 2, rows, width), lambda p, i: (p, 0, i, 0))]
+        + [whole_block(a) for a in fixed]
+        + [pl.BlockSpec((1, 2, 32, LANES), lambda p, i: (p, 0, 0, 0))],
+        out_specs=pl.BlockSpec((1, 2, rows, width), lambda p, i: (p, 0, i, 0)),
+        scratch_shapes=lane_scratch(rows),
         out_shape=jax.ShapeDtypeStruct((plan.planes, 2, plan.piece, width), f32),
         compiler_params=params(),
         cost_estimate=pl.CostEstimate(flops=13 * 10**9, bytes_accessed=51 * 10**6, transcendentals=0),
         name="step_pass",
-    )(scalars, *flat, held, *fixed, transfer)
-
-
-def shrink_pass(plan, scalars, moved, above, below):
+    )(*pieces, held, *fixed, transfer)
+
+
+def shrink_pass(plan, scalars, moved, above, below, begin, steps):
     planes, width = plan.planes, moved.shape[-1]
-    steps = plan.piece // 8
+    tiles = plan.piece // 8
+    at_top, at_bottom = begin == 0, begin + steps == tiles
     cols = 1024
 
     def kernel(scal, cur, nxt, up, down, *rest):
         outs, (carry, est) = rest[:planes], rest[planes:]
         i = pl.program_id(0)
-        last = i == steps - 1
+        last = jnp.logical_and(i == steps - 1, at_bottom)
         row_ids = lax.broadcasted_iota(jnp.int32, (8, cols), 0)
         lane_ids = lax.broadcasted_iota(jnp.int32, (8, cols), 1)
-        end_row = jnp.logical_and(last, scal[5] != 0)
+        end_row = jnp.logical_and(last, scal[1] != 0)
 
         def flux(tile, next_row, p, start):
             at_end = start + cols == width
@@ -656,14 +610,17 @@
             for p in range(planes):
                 for start in range(0, width, cols):
                     def tile(p, ri, at, wide):
-                        return jnp.broadcast_to(up[p, ri, 0:1, at : at + wide], (8, wide))
+                        line = slice(0, 1) if at_top else slice(7, 8)
+                        return jnp.broadcast_to(up[p, ri, line, at : at + wide], (8, wide))
 
                     def next_row(p, ri, at):
                         return cur[p, ri, 0:1, at : at + cols]
 
                     fy = flux(tile, next_row, p, start)[2]
                     for ri in range(2):
-                        carry[p, ri, :, start : start + cols] = jnp.where(scal[4] != 0, 0.0, fy[ri])
+                        if at_top:
+                            fy[ri] = jnp.where(scal[0] != 0, 0.0, fy[ri])
+                        carry[p, ri, :, start : start + cols] = fy[ri]
 
         def tile(p, ri, at, wide):
             return cur[p, ri, :, at : at + wide]
@@ -696,17 +653,16 @@
                     prior_x[p, ri] = fx[ri][:, cols - LANES :]
                 prior_z = fz
         for s in range(planes):
-            outs[s][...] = est[jnp.bitwise_xor(scal[1], s)]
-
+            outs[s][...] = est[jnp.bitwise_xor(scal[2], s)]
     return pl.pallas_call(
         kernel,
         grid_spec=pltpu.PrefetchScalarGridSpec(
             num_scalar_prefetch=1,
             grid=(steps,),
             in_specs=[
-                pl.BlockSpec((planes, 2, 8, width), lambda i, _: (0, 0, i, 0)),
-                pl.BlockSpec((planes, 2, 8, width), lambda i, _: (0, 0, jnp.minimum(i + 1, steps - 1), 0)),
-                whole_block(above),
+                pl.BlockSpec((planes, 2, 8, width), lambda i, _: (0, 0, begin + i, 0)),
+                pl.BlockSpec((planes, 2, 8, width), lambda i, _: (0, 0, jnp.minimum(begin + i + 1, tiles - 1), 0)),
+                whole_block(above) if at_top else pl.BlockSpec((planes, 2, 8, width), lambda i, _: (0, 0, begin - 1, 0)),
                 whole_block(below),
             ],
             out_specs=[pl.BlockSpec((2, 8, width), lambda i, _: (0, i, 0))] * planes,
@@ -715,11 +671,47 @@
                 pltpu.VMEM((planes, 2, 8, width), f32),
             ],
         ),
-        out_shape=[jax.ShapeDtypeStruct((2, plan.piece, width), f32)] * planes,
+        out_shape=[jax.ShapeDtypeStruct((2, steps * 8, width), f32)] * planes,
         compiler_params=params(),
-        cost_estimate=pl.CostEstimate(flops=10**8, bytes_accessed=34 * 10**6, transcendentals=4 * 10**6),
+        cost_estimate=pl.CostEstimate(flops=10**8, bytes_accessed=9 * 10**6, transcendentals=10**6),
         name="shrink_pass",
-    )(scalars, moved, moved, above, below)
+    )(scalars, moved, moved, above if at_top else moved, below)
+
+
+def place_rows(plan, scalars, pieces, begin, result):
+    rows, width = pieces[0].shape[-2:]
+    count = len(pieces)
+    given = [] if result is None else [result]
+
+    def kernel(scal, *refs):
+        sources, out, sems = refs[:count], refs[count + len(given)], refs[-1]
+        ri = pl.program_id(0)
+        copies = []
+        for s in range(count):
+            start = jnp.bitwise_xor(scal[2], s) * plan.piece + begin
+            span = pl.ds(pl.multiple_of(start, 8), rows)
+            copies.append(pltpu.make_async_copy(sources[s], out.at[pl.ds(ri, 1), span, :], sems.at[s]))
+        for copy in copies:
+            copy.start()
+        for copy in copies:
+            copy.wait()
+
+    return pl.pallas_call(
+        kernel,
+        grid_spec=pltpu.PrefetchScalarGridSpec(
+            num_scalar_prefetch=1,
+            grid=(2,),
+            in_specs=[pl.BlockSpec((1, rows, width), lambda ri, _: (ri, 0, 0))] * count
+            + [pl.BlockSpec(memory_space=pl.ANY)] * len(given),
+            out_specs=pl.BlockSpec(memory_space=pl.ANY),
+            scratch_shapes=[pltpu.SemaphoreType.DMA((count,))],
+        ),
+        out_shape=jax.ShapeDtypeStruct((2, plan.rows_dev, width), f32),
+        input_output_aliases={count + 1: 0} if given else {},
+        compiler_params=pltpu.CompilerParams(vmem_limit_bytes=8 * 1024 * 1024),
+        cost_estimate=pl.CostEstimate(flops=0, bytes_accessed=9 * 10**6, transcendentals=0),
+        name="place_rows",
+    )(scalars, *pieces, *given)
 
 
 class Plan:
@@ -730,13 +722,52 @@
         self.rows_dev = field_shape[-2]
         self.level = depth * 2
         self.cols_dev = self.length // self.level
-        self.chunk = self.cols_dev // PASSES
+        tiles = self.cols_dev // LANES
+        self.chunks = [LANES] * tiles
+        self.starts = [sum(self.chunks[:i]) for i in range(len(self.chunks))]
         self.piece = self.rows_dev // depth
         self.slab_tiles = 2 * self.rows_dev // LANES
 
+    def place_of(self, tile):
+        owner, inner = divmod(tile * LANES, self.cols_dev)
+        part = max(i for i, start in enumerate(self.starts) if start <= inner)
+        first = inner - self.starts[part]
+        return owner, part, slice(first, first + LANES)
+
 
 def swapped(value, axes, size, step):
     return lax.ppermute(value, axes, [(i, i ^ step) for i in range(size)])
+
+
+def after(value, *others):
+    return lax.optimization_barrier((value,) + others)[0]
+
+
+def halving_steps(size):
+    steps = []
+    step = 1
+    while step < size:
+        steps.append(step)
+        step = step * 2
+    return steps
+
+
+def scatter_step(value, axis, size, position, step, others):
+    upper = jnp.bitwise_and(position, step) != 0
+    half = value.shape[0] // 2
+    kept = jnp.where(upper, value[half:], value[:half])
+    given = jnp.where(upper, value[:half], value[half:])
+    return kept + swapped(after(given, *others), axis, size, step)
+
+
+def gather_step(value, axis, size, position, step, others):
+    upper = jnp.bitwise_and(position, step) != 0
+    other = swapped(after(value, *others), axis, size, step)
+    return jnp.concatenate([jnp.where(upper, other, value), jnp.where(upper, value, other)])
+
+
+def exchanged(value, axes):
+    return lax.all_to_all(value, axes, 0, 0, tiled=True)
 
 
 def per_device(field, hologram, defocus):
@@ -747,8 +778,7 @@
     me = d * 2 + c
     order = (z * 2 + c) * depth + d
     n_order = slabs * 2 * depth
-    scalars = jnp.stack([me, d, z, c, (order == 0).astype(jnp.int32), (order == n_order - 1).astype(jnp.int32)])
-    scalars = scalars.astype(jnp.int32)
+    ends = jnp.stack([(order == 0).astype(jnp.int32), (order == n_order - 1).astype(jnp.int32), d.astype(jnp.int32)])
     level_axes = ("depth", "core")
 
     forward, inverse = lane_tables()
@@ -761,20 +791,22 @@
     cos, sin = chirp(defocus[0], column_freqs, length)
     transfer = jnp.stack([cos, -sin]) * (1.0 / length)
 
+    ordered = jnp.concatenate([defocus] + [swapped(defocus, "depth", depth, s) for s in range(1, depth)])
+    depths = ordered[jnp.bitwise_xor(jnp.arange(depth, dtype=jnp.int32), d)]
+
     own = field[:, 0]
-    sent = column_pass(plan, scalars, own, tables, transfer)
-    level = plan.level
-    arrived = []
-    for part in range(PASSES):
-        group = sent[part * level : (part + 1) * level]
-        arrived.append([group[0]] + [swapped(group[s], level_axes, level, s) for s in range(1, level)])
-
-    depths = lax.all_gather(defocus, "depth", axis=0, tiled=True)
-    ordered = depths[jnp.bitwise_xor(jnp.arange(depth, dtype=jnp.int32), d)]
+    quarters = 4
+    by_rows = own.reshape(2, depth, quarters, plan.piece // quarters, length)
+    early = jnp.moveaxis(by_rows[:, :, 0], 1, 0)
+    own, early, depths = lax.optimization_barrier((own, early, depths))
+    held = [exchanged(early, "depth")]
+
+    sent = column_pass(plan, own, tables, transfer)
     bases, freqs = slot_bases(length)
-    cos, sin = chirp(ordered[None, :, None], freqs[:, None, :], length)
+    cos, sin = chirp(depths[None, :, None], freqs[:, None, :], length)
     weights = jnp.stack([cos, sin], axis=2).reshape(16, 2 * depth, 2 * LANES)
-    high, low = slot_matrices(plan, jnp.asarray(bases), weights)
+    weights, bases, *sent = lax.optimization_barrier((weights, jnp.asarray(bases), *sent))
+    high, low = slot_matrices(plan, bases, weights)
 
     slot_k = np.array([g + 4 * q for g in range(GROUPS) for q in range(4)])
     turns = (jnp.asarray(slot_k * plan.slab_tiles, jnp.int32) * z) % 32
@@ -785,33 +817,74 @@
     mine = lax.dynamic_slice_in_dim(hologram, me * plan.cols_dev, plan.cols_dev, 1)
     theirs = lax.dynamic_slice_in_dim(hologram, jnp.bitwise_xor(me, 1) * plan.cols_dev, plan.cols_dev, 1)
     theirs = swapped(theirs, "core", 2, 1)
-
-    by_rows = own.reshape(2, depth, plan.piece, length)
-    held = [lax.dynamic_index_in_dim(by_rows, jnp.bitwise_xor(d, s), 1, keepdims=False) for s in range(depth)]
-    held = jnp.stack([held[0]] + [swapped(held[s], "depth", depth, s) for s in range(1, depth)])
-
-    back = []
-    for part in range(PASSES):
-        span = slice(part * plan.chunk, (part + 1) * plan.chunk)
-        partial = row_forward(plan, scalars, phases, arrived[part], [mine[:, span], theirs[:, span]], high, low)
-        misfit = lax.psum(partial, "slab")
-        group = row_backward(plan, scalars, phases, misfit, high, low)
-        back.append([group[0]] + [swapped(group[s], level_axes, level, s) for s in range(1, level)])
-
+    holos = jnp.where(c == 0, jnp.stack([mine, theirs]), jnp.stack([theirs, mine]))
+
+    count = len(plan.chunks)
+
+    def forward_stage(value, part, others):
+        start = plan.starts[part]
+        here = holos[:, :, start : start + plan.chunks[part]]
+        return row_forward(plan, phases, after(value, *others), here, high, low)
+
+    def backward_stage(value, part, others):
+        return row_backward(plan, phases, after(value, *others), high, low)
+
+    def sum_stage(function, step):
+        return lambda value, part, others: function(value, "slab", slabs, z, step, others)
+
+    halvings = halving_steps(slabs)
+    stages = [forward_stage]
+    stages += [sum_stage(scatter_step, step) for step in halvings]
+    stages += [sum_stage(gather_step, step) for step in reversed(halvings)]
+    stages += [backward_stage]
+
+    queue = list(sent) + [None] * (quarters - 1)
+    state = [None] * count
+    before, back = [held[0]], []
+    slot = 0
+    while len(back) < count:
+        others, before = before, []
+        if queue:
+            value = queue.pop(0)
+            if value is None:
+                value = after(by_rows[:, :, len(held)], *others)
+                held.append(exchanged(jnp.moveaxis(value, 1, 0), "depth"))
+                before.append(held[-1])
+            else:
+                before.append(exchanged(after(value, *others), level_axes))
+                if slot < count:
+                    state[slot] = before[-1]
+                else:
+                    back.append(before[-1])
+        for part in range(count):
+            stage = slot - (part + 1)
+            if 0 <= stage < len(stages):
+                state[part] = stages[stage](state[part], part, others)
+                before.append(state[part])
+                if stage == len(stages) - 1:
+                    queue.append(state[part])
+        if slot == 0:
+            before += [high, low]
+        slot += 1
+
+    held = jnp.stack(held, axis=2).reshape(depth, 2, plan.piece, length)
     cos, sin = chirp(depths[:, None, None], column_freqs[None], length)
     transfer = jnp.stack([cos, sin], axis=1) * (1.0 / length)
-    moved = step_pass(plan, scalars, back, held, tables, transfer)
+    moved = step_pass(plan, back, held, tables, transfer)
 
     all_axes = ("depth", "slab", "core")
     device_at = [(i % depth) * (slabs * 2) + i // depth for i in range(n_order)]
     downward = [(device_at[i], device_at[i + 1]) for i in range(n_order - 1)]
     above = lax.ppermute(moved[:, :, -1:], all_axes, downward)
     below = lax.ppermute(moved[:, :, :1], all_axes, [(b, a) for a, b in downward])
-    parts = shrink_pass(plan, scalars, moved, above, below)
-    parts = [parts[0]] + [swapped(parts[s], "depth", depth, s) for s in range(1, depth)]
-    stacked = jnp.stack(parts, axis=1)
-    stacked = jnp.take(stacked, jnp.bitwise_xor(jnp.arange(depth, dtype=jnp.int32), d), axis=1)
-    return stacked.reshape(field.shape)
+    tiles = plan.piece // 8
+    steps = max(1, tiles // 4)
+    result = None
+    for begin in range(0, tiles, steps):
+        parts = shrink_pass(plan, ends, moved, above, below, begin, steps)
+        parts = [parts[0]] + [swapped(parts[s], "depth", depth, s) for s in range(1, depth)]
+        result = place_rows(plan, ends, parts, begin * 8, result)
+    return result.reshape(field.shape)
 
 
 def solution(mesh):

time: 1210 us -> 973 us (0.80)
  waiting for transfers between devices: 680 us -> 340 us
  Pallas kernels: 338 us -> 437 us
  starting transfers between devices: 38.3 us -> 103 us
  blocking collectives: 46.2 us -> 0 us
  local copies, waits for them, and re-layouts: 52 us -> 34.7 us
  between operations: 14.3 us -> 1.66 us
    psum x1 -> x0, waiting for transfers between devices: 277 us -> none  [per_device(): misfit = lax.psum(partial, 'slab')]
    ppermute x35 -> x32, waiting for transfers between devices: 396 us -> 214 us  [swapped(): return lax.ppermute(value, axes, [(i, i ^ step) for i in range(size)])]
    all_to_all x0 -> x12, waiting for transfers between devices: none -> 120 us  [exchanged(): return lax.all_to_all(value, axes, 0, 0, tiled=True)]
    pallas_call x2 -> x4, Pallas kernels: 84 us -> 144 us  [row_backward(): pl.pallas_call(kernel, grid_spec=pltpu.PrefetchScalarGridSpec(num_scalar_...]
    all_to_all x0 -> x12, starting transfers between devices: none -> 57.6 us  [exchanged(): return lax.all_to_all(value, axes, 0, 0, tiled=True)]
    unnamed x1 -> x0, blocking collectives: 46.2 us -> none
    pallas_call x2 -> x4, Pallas kernels: 78.9 us -> 105 us  [row_forward(): pl.pallas_call(kernel, grid_spec=pltpu.PrefetchScalarGridSpec(num_scalar_...]
    gather x4 -> x1, local copies, waits for them, and re-layouts: 22.7 us -> 0.64 us  [per_device(): depths = ordered[jnp.bitwise_xor(jnp.arange(depth, dtype=jnp.int32), d)]]
  transfers between devices with their start and end apart: 38 -> 46, of which waited for: 12 -> 25; matrix products, arithmetic and copies ran while one was open for 3% -> 8% of each run, Pallas kernels for 13% -> 39%
where the time goes in v2:
time: 973 us; the launch traced here: 961 us
  Pallas kernels  437 us (45%)
  waiting for transfers between devices  340 us (35%)
  starting transfers between devices  103 us (11%)
  other arithmetic  44.7 us (5%)
  local copies, waits for them, and re-layouts  34.7 us (4%)
    ppermute x32, waiting for transfers between devices, swapped(): return lax.ppermute(value, axes, [(i, i ^ step) for i in range(size)])  214 us
    pallas_call x4, Pallas kernels, row_backward(): pl.pallas_call(kernel, grid_spec=pltpu.PrefetchScalarGridSpec(num_scalar_...  144 us
    all_to_all x12, waiting for transfers between devices, exchanged(): return lax.all_to_all(value, axes, 0, 0, tiled=True)  120 us
    pallas_call x4, Pallas kernels, row_forward(): pl.pallas_call(kernel, grid_spec=pltpu.PrefetchScalarGridSpec(num_scalar_...  105 us
    all_to_all x12, starting transfers between devices, exchanged(): return lax.all_to_all(value, axes, 0, 0, tiled=True)  57.6 us
    pallas_call x1, Pallas kernels, step_pass(): pl.pallas_call(kernel, grid=(plan.planes, plan.piece // rows), in_specs=[...  47.9 us
    pallas_call x1, Pallas kernels, column_pass(): pl.pallas_call(kernel, grid=(plan.rows_dev // rows,), in_specs=[pl.BlockS...  45.6 us
    pallas_call x4, Pallas kernels, shrink_pass(): pl.pallas_call(kernel, grid_spec=pltpu.PrefetchScalarGridSpec(num_scalar_...  44.7 us
  transfers between devices with their start and end apart: 46, of which 25 were waited for; matrix products, arithmetic and copies ran while one was open for 8% of the time, Pallas kernels for 39%

profile of v2, /device:TPU:0, one launch (start us, length us, event | category | flops | bytes accessed | tf_op | source)
XLA Modules:
  0.0 960.6 jit_solution(663295128740923806)
XLA Ops:
  0.0 3.9 collective-permute-start.2
  5.2 10.9 %fusion.24 = (f32[2,4,1,32,4096]{4,3,2,1,0:T(8,128)}, f32[2,4,1,32,4096]{4,3,2,1,0:T(8,128)}, f32[2,4,1,32,4096]{4,3,2,1,0:T(8,128)}, f32[2,4,1,32,4096]{4,3,2,1,0:T(8,128)S(1)}) fusion(f32[2,4,4,32,4096]{4,3,2,1,0:T(8,128)} %bitcast.51), kind=kLoop, calls=%fused_computation.98 | loop fusion | bytes 33554432 | tf_op jit(solution)/shard_map/slice | solution.py:850
  21.1 5.0 all-to-all-start
  28.2 45.6 %column_pass.1 = (f32[8,2,512,128]{3,2,1,0:T(8,128)}, f32[8,2,512,128]{3,2,1,0:T(8,128)}, f32[8,2,512,128]{3,2,1,0:T(8,128)}, f32[8,2,512,128]{3,2,1,0:T(8,128)}) custom-call(f32[2,512,4096]{2,1,0:T(8,128)} %bitcast.52, bf16[768,256]{1,0:T(8,128)(2,1)} %constant.31.clone.fwd.refs_5_, bf16[768,256]{1,0:T(8,128)(2,1)} %constant.32.clone.inv.refs_6_, ...), custom_call_target="tpu_custom_call" | custom-call | flops 12999999488 | bytes 34000000 | tf_op jit(solution)/shard_map/column_pass/pallas_call | solution.py:346
  73.8 4.6 all-to-all-start.1
  78.4 33.2 %slot_matrices.1 = (bf16[16,256,2048]{2,1,0:T(8,128)(2,1)}, bf16[16,256,2048]{2,1,0:T(8,128)(2,1)}) custom-call(f32[16,256,256]{2,1,0:T(8,128)} %constant.108.clone.b_ref, f32[16,8,256]{2,1,0:T(8,128)} %copy.41.w_ref), custom_call_target="tpu_custom_call" | custom-call | flops 25999998976 | bytes 34000000 | tf_op jit(solution)/shard_map/slot_matrices/pallas_call | solution.py:379
  111.6 15.9 %all-to-all-done.1.x_ref = f32[8,2,512,128]{3,2,1,0:T(8,128)} async-done(((f32[8,2,512,128]{3,2,1,0:T(8,128)}), f32[8,2,512,128]{3,2,1,0:T(8,128)}, u32[]{:S(2)}, u32[]{:S(2)}) %all-to-all-start.1) | async-done | bytes 4194336 | tf_op jit(solution)/shard_map/all_to_all | solution.py:770
  127.5 4.5 all-to-all-start.2
  138.2 26.3 %row_forward.4 = f32[16,256,128]{2,1,0:T(8,128)} custom-call(f32[4,16]{1,0:T(4,128)} %pad_maximum_fusion.10.phase, f32[8,2,512,128]{3,2,1,0:T(8,128)} %all-to-all-done.1.x_ref, f32[2,512,128]{2,1,0:T(8,128)} %get-tuple-element.158.h_ref, bf16[16,256,2048]{2,1,0:T(8,128)(2,1)} %get-tuple-element.82.wh, bf16[16,256,2048]{2,1,0:T(8,128)(2,1)} %get-tuple-element.83.wl), custom_call_target="tpu_custom_call" | custom-call | flops 12999999488 | bytes 60000000 | tf_op jit(solution)/shard_map/row_forward/pallas_call | solution.py:442
  164.5 16.7 %all-to-all-done.2.x_ref = f32[8,2,512,128]{3,2,1,0:T(8,128)} async-done(((f32[8,2,512,128]{3,2,1,0:T(8,128)}), f32[8,2,512,128]{3,2,1,0:T(8,128)}, u32[]{:S(2)}, u32[]{:S(2)}) %all-to-all-start.2) | async-done | bytes 4194336 | tf_op jit(solution)/shard_map/all_to_all | solution.py:770
  181.2 4.7 all-to-all-start.3
  188.2 26.3 %row_forward.5 = f32[16,256,128]{2,1,0:T(8,128)} custom-call(f32[4,16]{1,0:T(4,128)} %pad_maximum_fusion.10.phase, f32[8,2,512,128]{3,2,1,0:T(8,128)} %all-to-all-done.2.x_ref, f32[2,512,128]{2,1,0:T(8,128)} %get-tuple-element.157.h_ref, bf16[16,256,2048]{2,1,0:T(8,128)(2,1)} %get-tuple-element.82.wh, bf16[16,256,2048]{2,1,0:T(8,128)(2,1)} %get-tuple-element.83.wl), custom_call_target="tpu_custom_call" | custom-call | flops 12999999488 | bytes 60000000 | tf_op jit(solution)/shard_map/row_forward/pallas_call | solution.py:442
  215.8 19.2 %all-to-all-done.3.x_ref = f32[8,2,512,128]{3,2,1,0:T(8,128)} async-done(((f32[8,2,512,128]{3,2,1,0:T(8,128)}), f32[8,2,512,128]{3,2,1,0:T(8,128)}, u32[]{:S(2)}, u32[]{:S(2)}) %all-to-all-start.3) | async-done | bytes 4194336 | tf_op jit(solution)/shard_map/all_to_all | solution.py:770
  235.1 4.6 all-to-all-start.4
  239.6 4.8 copy.52
  246.4 3.1 collective-permute-start.5
  251.0 26.3 %row_forward.6 = f32[16,256,128]{2,1,0:T(8,128)} custom-call(f32[4,16]{1,0:T(4,128)} %pad_maximum_fusion.10.phase, f32[8,2,512,128]{3,2,1,0:T(8,128)} %all-to-all-done.3.x_ref, f32[2,512,128]{2,1,0:T(8,128)} %get-tuple-element.156.h_ref, bf16[16,256,2048]{2,1,0:T(8,128)(2,1)} %get-tuple-element.82.wh, bf16[16,256,2048]{2,1,0:T(8,128)(2,1)} %get-tuple-element.83.wl), custom_call_target="tpu_custom_call" | custom-call | flops 12999999488 | bytes 60000000 | tf_op jit(solution)/shard_map/row_forward/pallas_call | solution.py:442
  278.2 6.8 collective-permute-done.6
  288.7 5.2 all-to-all-start.5
  294.0 4.7 copy.51
  300.7 3.1 collective-permute-start.7
  305.7 26.3 %row_forward.7 = f32[16,256,128]{2,1,0:T(8,128)} custom-call(f32[4,16]{1,0:T(4,128)} %pad_maximum_fusion.10.phase, f32[8,2,512,128]{3,2,1,0:T(8,128)} %all-to-all-done.4.x_ref, f32[2,512,128]{2,1,0:T(8,128)} %get-tuple-element.155.h_ref, bf16[16,256,2048]{2,1,0:T(8,128)(2,1)} %get-tuple-element.82.wh, bf16[16,256,2048]{2,1,0:T(8,128)(2,1)} %get-tuple-element.83.wl), custom_call_target="tpu_custom_call" | custom-call | flops 12999999488 | bytes 60000000 | tf_op jit(solution)/shard_map/row_forward/pallas_call | solution.py:442
  332.0 14.7 %collective-permute-done.8 = f32[4,256,128]{2,1,0:T(8,128)} collective-permute-done((f32[4,256,128]{2,1,0:T(8,128)}, f32[4,256,128]{2,1,0:T(8,128)}, u32[]{:S(2)}, u32[]{:S(2)}) %collective-permute-start.8) | collective-permute-done | bytes 524320 | tf_op jit(solution)/shard_map/ppermute | solution.py:739
  352.9 5.0 all-to-all-start.6
  357.9 4.1 collective-permute-start.10
  362.2 4.7 copy.50
  367.7 17.4 %collective-permute-done.11 = f32[4,256,128]{2,1,0:T(8,128)S(1)} collective-permute-done((f32[4,256,128]{2,1,0:T(8,128)}, f32[4,256,128]{2,1,0:T(8,128)S(1)}, u32[]{:S(2)}, u32[]{:S(2)}) %collective-permute-start.11) | collective-permute-done | bytes 524320 | tf_op jit(solution)/shard_map/ppermute | solution.py:739
  386.4 17.9 %collective-permute-done.12 = f32[4,256,128]{2,1,0:T(8,128)S(1)} collective-permute-done((f32[4,256,128]{2,1,0:T(8,128)S(1)}, f32[4,256,128]{2,1,0:T(8,128)S(1)}, u32[]{:S(2)}, u32[]{:S(2)}) %collective-permute-start.12) | collective-permute-done | bytes 524320 | tf_op jit(solution)/shard_map/ppermute | solution.py:739
  408.2 19.8 %collective-permute-done.13 = f32[8,256,128]{2,1,0:T(8,128)S(1)} collective-permute-done((f32[8,256,128]{2,1,0:T(8,128)S(1)}, f32[8,256,128]{2,1,0:T(8,128)S(1)}, u32[]{:S(2)}, u32[]{:S(2)}) %collective-permute-start.13) | collective-permute-done | bytes 1048608 | tf_op jit(solution)/shard_map/ppermute | solution.py:739
  428.2 5.1 all-to-all-start.7
  434.2 2.5 collective-permute-start.16
  438.4 36.0 %row_backward.4 = f32[8,8,128,128]{3,2,1,0:T(8,128)} custom-call(f32[4,16]{1,0:T(4,128)} %pad_maximum_fusion.10.phase, f32[16,256,128]{2,1,0:T(8,128)} %pad_maximum_fusion.1.m_ref, bf16[16,256,2048]{2,1,0:T(8,128)(2,1)} %get-tuple-element.82.wh, bf16[16,256,2048]{2,1,0:T(8,128)(2,1)} %get-tuple-element.83.wl), custom_call_target="tpu_custom_call" | custom-call | flops 12999999488 | bytes 60000000 | tf_op jit(solution)/shard_map/row_backward/pallas_call | solution.py:509
  474.4 7.6 collective-permute-done.15
  486.1 5.0 all-to-all-start.8
  492.9 2.5 collective-permute-start.17
  495.4 36.0 %row_backward.5 = f32[8,8,128,128]{3,2,1,0:T(8,128)} custom-call(f32[4,16]{1,0:T(4,128)} %pad_maximum_fusion.10.phase, f32[16,256,128]{2,1,0:T(8,128)} %pad_maximum_fusion.2.m_ref, bf16[16,256,2048]{2,1,0:T(8,128)(2,1)} %get-tuple-element.82.wh, bf16[16,256,2048]{2,1,0:T(8,128)(2,1)} %get-tuple-element.83.wl), custom_call_target="tpu_custom_call" | custom-call | flops 12999999488 | bytes 60000000 | tf_op jit(solution)/shard_map/row_backward/pallas_call | solution.py:509
  534.4 5.9 all-to-all-done.8.refs_0_
  540.4 4.8 all-to-all-start.9
  545.9 36.0 %row_backward.6 = f32[8,8,128,128]{3,2,1,0:T(8,128)} custom-call(f32[4,16]{1,0:T(4,128)} %pad_maximum_fusion.10.phase, f32[16,256,128]{2,1,0:T(8,128)} %pad_maximum_fusion.3.m_ref, bf16[16,256,2048]{2,1,0:T(8,128)(2,1)} %get-tuple-element.82.wh, bf16[16,256,2048]{2,1,0:T(8,128)(2,1)} %get-tuple-element.83.wl), custom_call_target="tpu_custom_call" | custom-call | flops 12999999488 | bytes 60000000 | tf_op jit(solution)/shard_map/row_backward/pallas_call | solution.py:509
  583.5 10.8 %all-to-all-done.9.refs_1_ = f32[8,8,128,128]{3,2,1,0:T(8,128)} async-done(((f32[8,8,128,128]{3,2,1,0:T(8,128)}), f32[8,8,128,128]{3,2,1,0:T(8,128)}, u32[]{:S(2)}, u32[]{:S(2)}) %all-to-all-start.9) | async-done | bytes 4194336 | tf_op jit(solution)/shard_map/all_to_all | solution.py:770
  594.3 4.6 all-to-all-start.10
  598.8 36.0 %row_backward.7 = f32[8,8,128,128]{3,2,1,0:T(8,128)} custom-call(f32[4,16]{1,0:T(4,128)} %pad_maximum_fusion.10.phase, f32[16,256,128]{2,1,0:T(8,128)} %pad_maximum_fusion.4.m_ref, bf16[16,256,2048]{2,1,0:T(8,128)(2,1)} %get-tuple-element.82.wh, bf16[16,256,2048]{2,1,0:T(8,128)(2,1)} %get-tuple-element.83.wl), custom_call_target="tpu_custom_call" | custom-call | flops 12999999488 | bytes 60000000 | tf_op jit(solution)/shard_map/row_backward/pallas_call | solution.py:509
  634.9 13.1 %all-to-all-done.10.refs_2_ = f32[8,8,128,128]{3,2,1,0:T(8,128)} async-done(((f32[8,8,128,128]{3,2,1,0:T(8,128)}), f32[8,8,128,128]{3,2,1,0:T(8,128)}, u32[]{:S(2)}, u32[]{:S(2)}) %all-to-all-start.10) | async-done | bytes 4194336 | tf_op jit(solution)/shard_map/all_to_all | solution.py:770
  648.0 4.5 all-to-all-start.11
  653.6 11.7 %pad_maximum_fusion = f32[4,2,4,32,4096]{4,3,2,1,0:T(8,128)} fusion(f32[4,2,1,32,4096]{4,3,2,1,0:T(8,128)} %bitcast.27, f32[4,2,1,32,4096]{4,3,2,1,0:T(8,128)} %bitcast.26, f32[4,2,1,32,4096]{4,3,2,1,0:T(8,128)} %bitcast.25, f32[4,2,1,32,4096]{4,3,2,1,0:T(8,128)} %bitcast.24), kind=kLoop, calls=%fused_computation.1 | loop fusion | flops 12582912 | bytes 33554432 | tf_op jit(solution)/shard_map/stack | solution.py:870
  665.3 36.3 %all-to-all-done.11.refs_3_ = f32[8,8,128,128]{3,2,1,0:T(8,128)} async-done(((f32[8,8,128,128]{3,2,1,0:T(8,128)}), f32[8,8,128,128]{3,2,1,0:T(8,128)}, u32[]{:S(2)}, u32[]{:S(2)}) %all-to-all-start.11) | async-done | bytes 4194336 | tf_op jit(solution)/shard_map/all_to_all | solution.py:770
  701.6 47.9 %step_pass.1.cur.nxt.up = f32[4,2,128,4096]{3,2,1,0:T(8,128)} custom-call(f32[8,8,128,128]{3,2,1,0:T(8,128)} %all-to-all-done.8.refs_0_, f32[8,8,128,128]{3,2,1,0:T(8,128)} %all-to-all-done.9.refs_1_, f32[8,8,128,128]{3,2,1,0:T(8,128)} %all-to-all-done.10.refs_2_, f32[8,8,128,128]{3,2,1,0:T(8,128)} %all-to-all-done.11.refs_3_, f32[4,2,128,4096]{3,2,1,0:T(8,128)} %bitcast.50, ...), custom_call_target="tpu_custom_call" | custom-call | flops 12999999488 | bytes 51000000 | tf_op jit(solution)/shard_map/step_pass/pallas_call | solution.py:558
  751.3 2.4 collective-permute-start.30
  757.1 3.8 collective-permute-done.20.down
  761.6 10.9 %shrink_pass.7 = (f32[2,32,4096]{2,1,0:T(8,128)}, f32[2,32,4096]{2,1,0:T(8,128)}, f32[2,32,4096]{2,1,0:T(8,128)}, f32[2,32,4096]{2,1,0:T(8,128)}) custom-call(s32[3]{0:T(128)} %pad_add_fusion.scal, f32[4,2,128,4096]{3,2,1,0:T(8,128)} %step_pass.1.cur.nxt.up, f32[4,2,128,4096]{3,2,1,0:T(8,128)} %step_pass.1.cur.nxt.up, f32[4,2,1,4096]{3,2,1,0:T(1,128)} %copy-done.23, ...), custom_call_target="tpu_custom_call" | custom-call | flops 100000000 | bytes 9000000 | tf_op jit(solution)/shard_map/shrink_pass/pallas_call | solution.py:657
  776.1 11.2 %shrink_pass.6 = (f32[2,32,4096]{2,1,0:T(8,128)}, f32[2,32,4096]{2,1,0:T(8,128)}, f32[2,32,4096]{2,1,0:T(8,128)}, f32[2,32,4096]{2,1,0:T(8,128)}) custom-call(s32[3]{0:T(128)} %pad_add_fusion.scal, f32[4,2,128,4096]{3,2,1,0:T(8,128)} %step_pass.1.cur.nxt.up, f32[4,2,128,4096]{3,2,1,0:T(8,128)} %step_pass.1.cur.nxt.up, ...), custom_call_target="tpu_custom_call" | custom-call | flops 100000000 | bytes 9000000 | tf_op jit(solution)/shard_map/shrink_pass/pallas_call | solution.py:657
  789.3 11.2 %shrink_pass.5 = (f32[2,32,4096]{2,1,0:T(8,128)}, f32[2,32,4096]{2,1,0:T(8,128)}, f32[2,32,4096]{2,1,0:T(8,128)}, f32[2,32,4096]{2,1,0:T(8,128)}) custom-call(s32[3]{0:T(128)} %pad_add_fusion.scal, f32[4,2,128,4096]{3,2,1,0:T(8,128)} %step_pass.1.cur.nxt.up, f32[4,2,128,4096]{3,2,1,0:T(8,128)} %step_pass.1.cur.nxt.up, ...), custom_call_target="tpu_custom_call" | custom-call | flops 100000000 | bytes 9000000 | tf_op jit(solution)/shard_map/shrink_pass/pallas_call | solution.py:657
  802.1 21.2 %collective-permute-done.32.refs_2_ = f32[2,32,4096]{2,1,0:T(8,128)S(1)} collective-permute-done((f32[2,32,4096]{2,1,0:T(8,128)}, f32[2,32,4096]{2,1,0:T(8,128)S(1)}, u32[]{:S(2)}, u32[]{:S(2)}) %collective-permute-start.32) | collective-permute-done | bytes 1048608 | tf_op jit(solution)/shard_map/ppermute | solution.py:739
  823.3 11.3 %shrink_pass.4 = (f32[2,32,4096]{2,1,0:T(8,128)}, f32[2,32,4096]{2,1,0:T(8,128)}, f32[2,32,4096]{2,1,0:T(8,128)}, f32[2,32,4096]{2,1,0:T(8,128)}) custom-call(s32[3]{0:T(128)} %pad_add_fusion.scal, f32[4,2,128,4096]{3,2,1,0:T(8,128)} %step_pass.1.cur.nxt.up, f32[4,2,128,4096]{3,2,1,0:T(8,128)} %step_pass.1.cur.nxt.up, ...), custom_call_target="tpu_custom_call" | custom-call | flops 100000000 | bytes 9000000 | tf_op jit(solution)/shard_map/shrink_pass/pallas_call | solution.py:657
  835.9 8.1 collective-permute-done.27.refs_1_
  844.4 23.9 %collective-permute-done.28.refs_2_ = f32[2,32,4096]{2,1,0:T(8,128)} collective-permute-done((f32[2,32,4096]{2,1,0:T(8,128)}, f32[2,32,4096]{2,1,0:T(8,128)}, u32[]{:S(2)}, u32[]{:S(2)}) %collective-permute-start.28) | collective-permute-done | bytes 1048608 | tf_op jit(solution)/shard_map/ppermute | solution.py:739
  869.6 19.3 %collective-permute-done.24.refs_1_ = f32[2,32,4096]{2,1,0:T(8,128)} collective-permute-done((f32[2,32,4096]{2,1,0:T(8,128)}, f32[2,32,4096]{2,1,0:T(8,128)}, u32[]{:S(2)}, u32[]{:S(2)}) %collective-permute-start.24) | collective-permute-done | bytes 1048608 | tf_op jit(solution)/shard_map/ppermute | solution.py:739
  889.4 4.2 place_rows.4.refs_4_
  893.6 4.6 place_rows.5.refs_4_
  898.2 14.9 %collective-permute-done.25.refs_2_ = f32[2,32,4096]{2,1,0:T(8,128)S(1)} collective-permute-done((f32[2,32,4096]{2,1,0:T(8,128)}, f32[2,32,4096]{2,1,0:T(8,128)S(1)}, u32[]{:S(2)}, u32[]{:S(2)}) %collective-permute-start.25) | collective-permute-done | bytes 1048608 | tf_op jit(solution)/shard_map/ppermute | solution.py:739
  913.2 4.2 place_rows.6.refs_4_
  917.4 16.4 %collective-permute-done.21.refs_1_ = f32[2,32,4096]{2,1,0:T(8,128)S(1)} collective-permute-done((f32[2,32,4096]{2,1,0:T(8,128)}, f32[2,32,4096]{2,1,0:T(8,128)S(1)}, u32[]{:S(2)}, u32[]{:S(2)}) %collective-permute-start.21) | collective-permute-done | bytes 1048608 | tf_op jit(solution)/shard_map/ppermute | solution.py:739
  933.8 23.3 %collective-permute-done.22.refs_2_ = f32[2,32,4096]{2,1,0:T(8,128)S(1)} collective-permute-done((f32[2,32,4096]{2,1,0:T(8,128)}, f32[2,32,4096]{2,1,0:T(8,128)S(1)}, u32[]{:S(2)}, u32[]{:S(2)}) %collective-permute-start.22) | collective-permute-done | bytes 1048608 | tf_op jit(solution)/shard_map/ppermute | solution.py:739
  957.1 3.2 place_rows.7
  (188 shorter events, 72.9 us)
Async XLA Ops:
  0.0 18.4 %collective-permute-start.2 = (f32[1]{0:T(128)}, f32[1]{0:T(128)}, u32[]{:S(2)}, u32[]{:S(2)}) collective-permute-start(f32[1]{0:T(128)} %param.23), channel_id=1, source_target_pairs={{0,24},{8,16},{16,8},{24,0},{1,25},{9,17},{17,9},{25,1},{2,26},{10... | collective-permute-start | bytes 20 | tf_op jit(solution)/shard_map/ppermute | solution.py:739
  3.9 14.5 %collective-permute-start.1 = (f32[1]{0:T(128)}, f32[1]{0:T(128)}, u32[]{:S(2)}, u32[]{:S(2)}) collective-permute-start(f32[1]{0:T(128)} %param.23), channel_id=1, source_target_pairs={{0,16},{8,24},{16,0},{24,8},{1,17},{9,25},{17,1},{25,9},{2,18},{10... | collective-permute-start | bytes 20 | tf_op jit(solution)/shard_map/ppermute | solution.py:739
  4.4 14.0 %collective-permute-start = (f32[1]{0:T(128)}, f32[1]{0:T(128)}, u32[]{:S(2)}, u32[]{:S(2)}) collective-permute-start(f32[1]{0:T(128)} %param.23), channel_id=1, source_target_pairs={{0,8},{8,0},{16,24},{24,16},{1,9},{9,1},{17,25},{25,17},{2,10},{10... | collective-permute-start | bytes 20 | tf_op jit(solution)/shard_map/ppermute | solution.py:739
  21.1 52.8 %all-to-all-start = ((f32[4,2,32,4096]{3,2,1,0:T(8,128)}), f32[4,2,32,4096]{3,2,1,0:T(8,128)}, u32[]{:S(2)}, u32[]{:S(2)}) async-start(f32[4,2,32,4096]{3,2,1,0:T(8,128)} %bitcast.56), calls=%async_computation | async-start | bytes 8388608 | tf_op jit(solution)/shard_map/all_to_all | solution.py:770
  73.8 53.7 %all-to-all-start.1 = ((f32[8,2,512,128]{3,2,1,0:T(8,128)}), f32[8,2,512,128]{3,2,1,0:T(8,128)}, u32[]{:S(2)}, u32[]{:S(2)}) async-start(f32[8,2,512,128]{3,2,1,0:T(8,128)} %get-tuple-element.79), calls=%async_computation.1 | async-start | bytes 8388608 | tf_op jit(solution)/shard_map/all_to_all | solution.py:770
  127.5 53.7 %all-to-all-start.2 = ((f32[8,2,512,128]{3,2,1,0:T(8,128)}), f32[8,2,512,128]{3,2,1,0:T(8,128)}, u32[]{:S(2)}, u32[]{:S(2)}) async-start(f32[8,2,512,128]{3,2,1,0:T(8,128)} %get-tuple-element.86), calls=%async_computation.2 | async-start | bytes 8388608 | tf_op jit(solution)/shard_map/all_to_all | solution.py:770
  133.8 2.7 collective-permute-start.3
  164.5 21.4 %copy-start.9 = (f32[16,256,128]{2,1,0:T(8,128)S(1)}, f32[16,256,128]{2,1,0:T(8,128)}, u32[]{:S(2)}) copy-start(f32[16,256,128]{2,1,0:T(8,128)} %row_forward.4) | copy-start | bytes 6291460
  181.2 53.9 %all-to-all-start.3 = ((f32[8,2,512,128]{3,2,1,0:T(8,128)}), f32[8,2,512,128]{3,2,1,0:T(8,128)}, u32[]{:S(2)}, u32[]{:S(2)}) async-start(f32[8,2,512,128]{3,2,1,0:T(8,128)} %get-tuple-element.89), calls=%async_computation.3 | async-start | bytes 8388608 | tf_op jit(solution)/shard_map/all_to_all | solution.py:770
  186.1 28.4 %collective-permute-start.4 = (f32[8,256,128]{2,1,0:T(8,128)S(1)}, f32[8,256,128]{2,1,0:T(8,128)}, u32[]{:S(2)}, u32[]{:S(2)}) collective-permute-start(f32[8,256,128]{2,1,0:T(8,128)S(1)} %slice_select_fusion.3), channel_id=1, source_target_pairs={{0,2},{2,0},{4,6},{6,4},{1,3},{3,1},{5,7},{7,5},{8,10},{10,8},{12,... | collective-permute-start | bytes 3145736 | tf_op jit(solution)/shard_map/ppermute | solution.py:739
  235.1 53.7 %all-to-all-start.4 = ((f32[8,2,512,128]{3,2,1,0:T(8,128)}), f32[8,2,512,128]{3,2,1,0:T(8,128)}, u32[]{:S(2)}, u32[]{:S(2)}) async-start(f32[8,2,512,128]{3,2,1,0:T(8,128)} %get-tuple-element.93), calls=%async_computation.4 | async-start | bytes 8388608 | tf_op jit(solution)/shard_map/all_to_all | solution.py:770
  246.4 30.9 %collective-permute-start.5 = (f32[4,256,128]{2,1,0:T(8,128)}, f32[4,256,128]{2,1,0:T(8,128)S(1)}, u32[]{:S(2)}, u32[]{:S(2)}) collective-permute-start(f32[4,256,128]{2,1,0:T(8,128)} %slice_select_fusion.7), channel_id=1, source_target_pairs={{0,4},{2,6},{4,0},{6,2},{1,5},{3,7},{5,1},{7,3},{8,12},{10,14},{12... | collective-permute-start | bytes 1572872 | tf_op jit(solution)/shard_map/ppermute | solution.py:739
  249.5 35.5 %collective-permute-start.6 = (f32[8,256,128]{2,1,0:T(8,128)}, f32[8,256,128]{2,1,0:T(8,128)}, u32[]{:S(2)}, u32[]{:S(2)}) collective-permute-start(f32[8,256,128]{2,1,0:T(8,128)} %slice_select_fusion.2), channel_id=1, source_target_pairs={{0,2},{2,0},{4,6},{6,4},{1,3},{3,1},{5,7},{7,5},{8,10},{10,8},{12,... | collective-permute-start | bytes 3145736 | tf_op jit(solution)/shard_map/ppermute | solution.py:739
  288.7 64.2 %all-to-all-start.5 = ((f32[4,2,32,4096]{3,2,1,0:T(8,128)}), f32[4,2,32,4096]{3,2,1,0:T(8,128)}, u32[]{:S(2)}, u32[]{:S(2)}) async-start(f32[4,2,32,4096]{3,2,1,0:T(8,128)} %bitcast.55), calls=%async_computation.5 | async-start | bytes 8388608 | tf_op jit(solution)/shard_map/all_to_all | solution.py:770
  300.7 47.9 %collective-permute-start.7 = (f32[4,256,128]{2,1,0:T(8,128)S(1)}, f32[4,256,128]{2,1,0:T(8,128)}, u32[]{:S(2)}, u32[]{:S(2)}) collective-permute-start(f32[4,256,128]{2,1,0:T(8,128)S(1)} %copy-done.21), channel_id=1, source_target_pairs={{0,4},{2,6},{4,0},{6,2},{1,5},{3,7},{5,1},{7,3},{8,12},{10,14},{12... | collective-permute-start | bytes 1572872 | tf_op jit(solution)/shard_map/ppermute | solution.py:739
  303.8 42.9 %collective-permute-start.8 = (f32[4,256,128]{2,1,0:T(8,128)}, f32[4,256,128]{2,1,0:T(8,128)}, u32[]{:S(2)}, u32[]{:S(2)}) collective-permute-start(f32[4,256,128]{2,1,0:T(8,128)} %slice_select_fusion.6), channel_id=1, source_target_pairs={{0,4},{2,6},{4,0},{6,2},{1,5},{3,7},{5,1},{7,3},{8,12},{10,14},{12... | collective-permute-start | bytes 1572872 | tf_op jit(solution)/shard_map/ppermute | solution.py:739
  303.8 47.7 %collective-permute-start.9 = (f32[8,256,128]{2,1,0:T(8,128)}, f32[8,256,128]{2,1,0:T(8,128)}, u32[]{:S(2)}, u32[]{:S(2)}) collective-permute-start(f32[8,256,128]{2,1,0:T(8,128)} %slice_select_fusion.1), channel_id=1, source_target_pairs={{0,2},{2,0},{4,6},{6,4},{1,3},{3,1},{5,7},{7,5},{8,10},{10,8},{12,... | collective-permute-start | bytes 3145736 | tf_op jit(solution)/shard_map/ppermute | solution.py:739
  332.0 17.9 %copy-start.5 = (f32[16,256,128]{2,1,0:T(8,128)S(1)}, f32[16,256,128]{2,1,0:T(8,128)}, u32[]{:S(2)}) copy-start(f32[16,256,128]{2,1,0:T(8,128)} %row_forward.7) | copy-start | bytes 6291460
  352.9 75.3 %all-to-all-start.6 = ((f32[4,2,32,4096]{3,2,1,0:T(8,128)}), f32[4,2,32,4096]{3,2,1,0:T(8,128)}, u32[]{:S(2)}, u32[]{:S(2)}) async-start(f32[4,2,32,4096]{3,2,1,0:T(8,128)} %bitcast.53), calls=%async_computation.6 | async-start | bytes 8388608 | tf_op jit(solution)/shard_map/all_to_all | solution.py:770
  357.9 27.3 %collective-permute-start.11 = (f32[4,256,128]{2,1,0:T(8,128)}, f32[4,256,128]{2,1,0:T(8,128)S(1)}, u32[]{:S(2)}, u32[]{:S(2)}) collective-permute-start(f32[4,256,128]{2,1,0:T(8,128)} %select_add_fusion.6), channel_id=1, source_target_pairs={{0,4},{2,6},{4,0},{6,2},{1,5},{3,7},{5,1},{7,3},{8,12},{10,14},{12... | collective-permute-start | bytes 1572872 | tf_op jit(solution)/shard_map/ppermute | solution.py:739
  357.9 48.7 %collective-permute-start.10 = (f32[8,256,128]{2,1,0:T(8,128)}, f32[8,256,128]{2,1,0:T(8,128)S(1)}, u32[]{:S(2)}, u32[]{:S(2)}) collective-permute-start(f32[8,256,128]{2,1,0:T(8,128)} %get-tuple-element.101), channel_id=1, source_target_pairs={{0,2},{2,0},{4,6},{6,4},{1,3},{3,1},{5,7},{7,5},{8,10},{10,8},{12,... | collective-permute-start | bytes 3145736 | tf_op jit(solution)/shard_map/ppermute | solution.py:739
  362.1 42.2 %collective-permute-start.12 = (f32[4,256,128]{2,1,0:T(8,128)S(1)}, f32[4,256,128]{2,1,0:T(8,128)S(1)}, u32[]{:S(2)}, u32[]{:S(2)}) collective-permute-start(f32[4,256,128]{2,1,0:T(8,128)S(1)} %slice_select_fusion.5), channel_id=1, source_target_pairs={{0,4},{2,6},{4,0},{6,2},{1,5},{3,7},{5,1},{7,3},{8,12},{10,14},{12... | collective-permute-start | bytes 1572872 | tf_op jit(solution)/shard_map/ppermute | solution.py:739
  362.2 23.0 %copy-start.19 = (f32[4,256,128]{2,1,0:T(8,128)S(1)}, f32[4,256,128]{2,1,0:T(8,128)}, u32[]{:S(2)}) copy-start(f32[4,256,128]{2,1,0:T(8,128)} %select_add_fusion.6) | copy-start | bytes 1572868
  366.9 39.6 %copy-start.15 = (f32[4,256,128]{2,1,0:T(8,128)S(1)}, f32[4,256,128]{2,1,0:T(8,128)}, u32[]{:S(2)}) copy-start(f32[4,256,128]{2,1,0:T(8,128)} %copy-done.14) | copy-start | bytes 1572868
  366.9 39.7 %copy-start.17 = (f32[4,256,128]{2,1,0:T(8,128)S(1)}, f32[4,256,128]{2,1,0:T(8,128)}, u32[]{:S(2)}) copy-start(f32[4,256,128]{2,1,0:T(8,128)} %copy-done.16) | copy-start | bytes 1572868
  366.9 61.1 %collective-permute-start.13 = (f32[8,256,128]{2,1,0:T(8,128)S(1)}, f32[8,256,128]{2,1,0:T(8,128)S(1)}, u32[]{:S(2)}, u32[]{:S(2)}) collective-permute-start(f32[8,256,128]{2,1,0:T(8,128)S(1)} %copy-done.22), channel_id=1, source_target_pairs={{0,2},{2,0},{4,6},{6,4},{1,3},{3,1},{5,7},{7,5},{8,10},{10,8},{12,... | collective-permute-start | bytes 3145736 | tf_op jit(solution)/shard_map/ppermute | solution.py:739
  385.2 19.9 %copy-start.10 = (f32[4,256,128]{2,1,0:T(8,128)}, f32[4,256,128]{2,1,0:T(8,128)S(1)}, u32[]{:S(2)}) copy-start(f32[4,256,128]{2,1,0:T(8,128)S(1)} %get-tuple-element.163) | copy-start | bytes 1572868
  385.2 19.9 %copy-start.12 = (f32[4,256,128]{2,1,0:T(8,128)}, f32[4,256,128]{2,1,0:T(8,128)S(1)}, u32[]{:S(2)}) copy-start(f32[4,256,128]{2,1,0:T(8,128)S(1)} %get-tuple-element.164) | copy-start | bytes 1572868
  428.2 58.0 %all-to-all-start.7 = ((f32[4,2,32,4096]{3,2,1,0:T(8,128)}), f32[4,2,32,4096]{3,2,1,0:T(8,128)}, u32[]{:S(2)}, u32[]{:S(2)}) async-start(f32[4,2,32,4096]{3,2,1,0:T(8,128)} %bitcast.54), calls=%async_computation.7 | async-start | bytes 8388608 | tf_op jit(solution)/shard_map/all_to_all | solution.py:770
  434.2 49.0 %collective-permute-start.16 = (f32[4,256,128]{2,1,0:T(8,128)}, f32[4,256,128]{2,1,0:T(8,128)S(1)}, u32[]{:S(2)}, u32[]{:S(2)}) collective-permute-start(f32[4,256,128]{2,1,0:T(8,128)} %slice_select_fusion.4), channel_id=1, source_target_pairs={{0,4},{2,6},{4,0},{6,2},{1,5},{3,7},{5,1},{7,3},{8,12},{10,14},{12... | collective-permute-start | bytes 1572872 | tf_op jit(solution)/shard_map/ppermute | solution.py:739
  436.6 45.4 %collective-permute-start.15 = (f32[4,256,128]{2,1,0:T(8,128)S(1)}, f32[4,256,128]{2,1,0:T(8,128)S(1)}, u32[]{:S(2)}, u32[]{:S(2)}) collective-permute-start(f32[4,256,128]{2,1,0:T(8,128)S(1)} %copy-done.20), channel_id=1, source_target_pairs={{0,4},{2,6},{4,0},{6,2},{1,5},{3,7},{5,1},{7,3},{8,12},{10,14},{12... | collective-permute-start | bytes 1572872 | tf_op jit(solution)/shard_map/ppermute | solution.py:739
  437.1 46.1 %collective-permute-start.14 = (f32[8,256,128]{2,1,0:T(8,128)}, f32[8,256,128]{2,1,0:T(8,128)}, u32[]{:S(2)}, u32[]{:S(2)}) collective-permute-start(f32[8,256,128]{2,1,0:T(8,128)} %pad_maximum_fusion.6), channel_id=1, source_target_pairs={{0,2},{2,0},{4,6},{6,4},{1,3},{3,1},{5,7},{7,5},{8,10},{10,8},{12,... | collective-permute-start | bytes 3145736 | tf_op jit(solution)/shard_map/ppermute | solution.py:739
  474.4 8.8 copy-start.13
  486.1 54.2 %all-to-all-start.8 = ((f32[8,8,128,128]{3,2,1,0:T(8,128)}), f32[8,8,128,128]{3,2,1,0:T(8,128)}, u32[]{:S(2)}, u32[]{:S(2)}) async-start(f32[8,8,128,128]{3,2,1,0:T(8,128)} %row_backward.4), calls=%async_computation.8 | async-start | bytes 8388608 | tf_op jit(solution)/shard_map/all_to_all | solution.py:770
  491.1 40.3 %collective-permute-start.18 = (f32[4,256,128]{2,1,0:T(8,128)S(1)}, f32[4,256,128]{2,1,0:T(8,128)S(1)}, u32[]{:S(2)}, u32[]{:S(2)}) collective-permute-start(f32[4,256,128]{2,1,0:T(8,128)S(1)} %select_add_fusion.4), channel_id=1, source_target_pairs={{0,4},{2,6},{4,0},{6,2},{1,5},{3,7},{5,1},{7,3},{8,12},{10,14},{12... | collective-permute-start | bytes 1572872 | tf_op jit(solution)/shard_map/ppermute | solution.py:739
  492.9 38.6 %collective-permute-start.17 = (f32[8,256,128]{2,1,0:T(8,128)}, f32[8,256,128]{2,1,0:T(8,128)}, u32[]{:S(2)}, u32[]{:S(2)}) collective-permute-start(f32[8,256,128]{2,1,0:T(8,128)} %pad_maximum_fusion.7), channel_id=1, source_target_pairs={{0,2},{2,0},{4,6},{6,4},{1,3},{3,1},{5,7},{7,5},{8,10},{10,8},{12,... | collective-permute-start | bytes 3145736 | tf_op jit(solution)/shard_map/ppermute | solution.py:739
  540.4 53.9 %all-to-all-start.9 = ((f32[8,8,128,128]{3,2,1,0:T(8,128)}), f32[8,8,128,128]{3,2,1,0:T(8,128)}, u32[]{:S(2)}, u32[]{:S(2)}) async-start(f32[8,8,128,128]{3,2,1,0:T(8,128)} %row_backward.5), calls=%async_computation.9 | async-start | bytes 8388608 | tf_op jit(solution)/shard_map/all_to_all | solution.py:770
  545.1 36.7 %collective-permute-start.19 = (f32[8,256,128]{2,1,0:T(8,128)S(1)}, f32[8,256,128]{2,1,0:T(8,128)S(1)}, u32[]{:S(2)}, u32[]{:S(2)}) collective-permute-start(f32[8,256,128]{2,1,0:T(8,128)S(1)} %pad_maximum_fusion.8), channel_id=1, source_target_pairs={{0,2},{2,0},{4,6},{6,4},{1,3},{3,1},{5,7},{7,5},{8,10},{10,8},{12,... | collective-permute-start | bytes 3145736 | tf_op jit(solution)/shard_map/ppermute | solution.py:739
  594.3 53.7 %all-to-all-start.10 = ((f32[8,8,128,128]{3,2,1,0:T(8,128)}), f32[8,8,128,128]{3,2,1,0:T(8,128)}, u32[]{:S(2)}, u32[]{:S(2)}) async-start(f32[8,8,128,128]{3,2,1,0:T(8,128)} %row_backward.6), calls=%async_computation.10 | async-start | bytes 8388608 | tf_op jit(solution)/shard_map/all_to_all | solution.py:770
  634.8 17.7 %copy-start.25 = (f32[32,128]{1,0:T(8,128)S(1)}, f32[32,128]{1,0:T(8,128)}, u32[]{:S(2)}) copy-start(f32[32,128]{1,0:T(8,128)} %constant.103.clone) | copy-start | bytes 49156
  634.8 17.7 %copy-start.27 = (f32[32,128]{1,0:T(8,128)S(1)}, f32[32,128]{1,0:T(8,128)}, u32[]{:S(2)}) copy-start(f32[32,128]{1,0:T(8,128)} %constant.102.clone) | copy-start | bytes 49156
  634.8 17.7 %copy-start.29 = (f32[32,128]{1,0:T(8,128)S(1)}, f32[32,128]{1,0:T(8,128)}, u32[]{:S(2)}) copy-start(f32[32,128]{1,0:T(8,128)} %constant.101.clone) | copy-start | bytes 49156
  634.8 17.7 %copy-start.31 = (f32[32,128]{1,0:T(8,128)S(1)}, f32[32,128]{1,0:T(8,128)}, u32[]{:S(2)}) copy-start(f32[32,128]{1,0:T(8,128)} %constant.100.clone) | copy-start | bytes 49156
  634.8 17.7 %copy-start.37 = (f32[4]{0:T(128)S(1)}, f32[4]{0:T(128)}, u32[]{:S(2)}) copy-start(f32[4]{0:T(128)} %copy-done.36) | copy-start | bytes 52
  634.8 17.7 %copy-start.39 = (f32[4]{0:T(128)S(1)}, f32[4]{0:T(128)}, u32[]{:S(2)}) copy-start(f32[4]{0:T(128)} %copy-done.38) | copy-start | bytes 52
  648.0 53.7 %all-to-all-start.11 = ((f32[8,8,128,128]{3,2,1,0:T(8,128)}), f32[8,8,128,128]{3,2,1,0:T(8,128)}, u32[]{:S(2)}, u32[]{:S(2)}) async-start(f32[8,8,128,128]{3,2,1,0:T(8,128)} %row_backward.7), calls=%async_computation.11 | async-start | bytes 8388608 | tf_op jit(solution)/shard_map/all_to_all | solution.py:770
  751.3 5.8 collective-permute-start.30
  753.7 7.2 collective-permute-start.20
  772.5 28.0 %collective-permute-start.31 = (f32[2,32,4096]{2,1,0:T(8,128)}, f32[2,32,4096]{2,1,0:T(8,128)S(1)}, u32[]{:S(2)}, u32[]{:S(2)}) collective-permute-start(f32[2,32,4096]{2,1,0:T(8,128)} %get-tuple-element.134), channel_id=1, source_target_pairs={{0,8},{8,0},{16,24},{24,16},{1,9},{9,1},{17,25},{25,17},{2,10},{10... | collective-permute-start | bytes 3145736 | tf_op jit(solution)/shard_map/ppermute | solution.py:739
  774.6 48.7 %collective-permute-start.32 = (f32[2,32,4096]{2,1,0:T(8,128)}, f32[2,32,4096]{2,1,0:T(8,128)S(1)}, u32[]{:S(2)}, u32[]{:S(2)}) collective-permute-start(f32[2,32,4096]{2,1,0:T(8,128)} %get-tuple-element.135), channel_id=1, source_target_pairs={{0,16},{8,24},{16,0},{24,8},{1,17},{9,25},{17,1},{25,9},{2,18},{10... | collective-permute-start | bytes 3145736 | tf_op jit(solution)/shard_map/ppermute | solution.py:739
  774.6 60.1 %collective-permute-start.33 = (f32[2,32,4096]{2,1,0:T(8,128)}, f32[2,32,4096]{2,1,0:T(8,128)}, u32[]{:S(2)}, u32[]{:S(2)}) collective-permute-start(f32[2,32,4096]{2,1,0:T(8,128)} %get-tuple-element.136), channel_id=1, source_target_pairs={{0,24},{8,16},{16,8},{24,0},{1,25},{9,17},{17,9},{25,1},{2,26},{10... | collective-permute-start | bytes 3145736 | tf_op jit(solution)/shard_map/ppermute | solution.py:739
  787.3 56.6 %collective-permute-start.27 = (f32[2,32,4096]{2,1,0:T(8,128)}, f32[2,32,4096]{2,1,0:T(8,128)}, u32[]{:S(2)}, u32[]{:S(2)}) collective-permute-start(f32[2,32,4096]{2,1,0:T(8,128)} %get-tuple-element.130), channel_id=1, source_target_pairs={{0,8},{8,0},{16,24},{24,16},{1,9},{9,1},{17,25},{25,17},{2,10},{10... | collective-permute-start | bytes 3145736 | tf_op jit(solution)/shard_map/ppermute | solution.py:739
  789.3 79.0 %collective-permute-start.28 = (f32[2,32,4096]{2,1,0:T(8,128)}, f32[2,32,4096]{2,1,0:T(8,128)}, u32[]{:S(2)}, u32[]{:S(2)}) collective-permute-start(f32[2,32,4096]{2,1,0:T(8,128)} %get-tuple-element.131), channel_id=1, source_target_pairs={{0,16},{8,24},{16,0},{24,8},{1,17},{9,25},{17,1},{25,9},{2,18},{10... | collective-permute-start | bytes 3145736 | tf_op jit(solution)/shard_map/ppermute | solution.py:739
  800.5 67.8 %collective-permute-start.29 = (f32[2,32,4096]{2,1,0:T(8,128)}, f32[2,32,4096]{2,1,0:T(8,128)}, u32[]{:S(2)}, u32[]{:S(2)}) collective-permute-start(f32[2,32,4096]{2,1,0:T(8,128)} %get-tuple-element.132), channel_id=1, source_target_pairs={{0,24},{8,16},{16,8},{24,0},{1,25},{9,17},{17,9},{25,1},{2,26},{10... | collective-permute-start | bytes 3145736 | tf_op jit(solution)/shard_map/ppermute | solution.py:739
  823.3 66.1 %copy-start = (f32[2,32,4096]{2,1,0:T(8,128)S(1)}, f32[2,32,4096]{2,1,0:T(8,128)}, u32[]{:S(2)}) copy-start(f32[2,32,4096]{2,1,0:T(8,128)} %get-tuple-element.133.refs_0_) | copy-start | bytes 3145732
  823.3 66.1 %copy-start.4 = (s32[3]{0:T(128)S(1)}, s32[3]{0:T(128)}, u32[]{:S(2)}) copy-start(s32[3]{0:T(128)} %pad_add_fusion.scal) | copy-start | bytes 40
  823.3 65.6 %collective-permute-start.24 = (f32[2,32,4096]{2,1,0:T(8,128)}, f32[2,32,4096]{2,1,0:T(8,128)}, u32[]{:S(2)}, u32[]{:S(2)}) collective-permute-start(f32[2,32,4096]{2,1,0:T(8,128)} %get-tuple-element.126), channel_id=1, source_target_pairs={{0,8},{8,0},{16,24},{24,16},{1,9},{9,1},{17,25},{25,17},{2,10},{10... | collective-permute-start | bytes 3145736 | tf_op jit(solution)/shard_map/ppermute | solution.py:739
  834.6 78.5 %collective-permute-start.25 = (f32[2,32,4096]{2,1,0:T(8,128)}, f32[2,32,4096]{2,1,0:T(8,128)S(1)}, u32[]{:S(2)}, u32[]{:S(2)}) collective-permute-start(f32[2,32,4096]{2,1,0:T(8,128)} %get-tuple-element.127), channel_id=1, source_target_pairs={{0,16},{8,24},{16,0},{24,8},{1,17},{9,25},{17,1},{25,9},{2,18},{10... | collective-permute-start | bytes 3145736 | tf_op jit(solution)/shard_map/ppermute | solution.py:739
  843.9 69.2 %collective-permute-start.26 = (f32[2,32,4096]{2,1,0:T(8,128)}, f32[2,32,4096]{2,1,0:T(8,128)S(1)}, u32[]{:S(2)}, u32[]{:S(2)}) collective-permute-start(f32[2,32,4096]{2,1,0:T(8,128)} %get-tuple-element.128), channel_id=1, source_target_pairs={{0,24},{8,16},{16,8},{24,0},{1,25},{9,17},{17,9},{25,1},{2,26},{10... | collective-permute-start | bytes 3145736 | tf_op jit(solution)/shard_map/ppermute | solution.py:739
  868.3 65.5 %collective-permute-start.21 = (f32[2,32,4096]{2,1,0:T(8,128)}, f32[2,32,4096]{2,1,0:T(8,128)S(1)}, u32[]{:S(2)}, u32[]{:S(2)}) collective-permute-start(f32[2,32,4096]{2,1,0:T(8,128)} %get-tuple-element.122), channel_id=1, source_target_pairs={{0,8},{8,0},{16,24},{24,16},{1,9},{9,1},{17,25},{25,17},{2,10},{10... | collective-permute-start | bytes 3145736 | tf_op jit(solution)/shard_map/ppermute | solution.py:739
  868.3 88.8 %collective-permute-start.22 = (f32[2,32,4096]{2,1,0:T(8,128)}, f32[2,32,4096]{2,1,0:T(8,128)S(1)}, u32[]{:S(2)}, u32[]{:S(2)}) collective-permute-start(f32[2,32,4096]{2,1,0:T(8,128)} %get-tuple-element.123), channel_id=1, source_target_pairs={{0,16},{8,24},{16,0},{24,8},{1,17},{9,25},{17,1},{25,9},{2,18},{10... | collective-permute-start | bytes 3145736 | tf_op jit(solution)/shard_map/ppermute | solution.py:739
  888.9 68.2 %collective-permute-start.23 = (f32[2,32,4096]{2,1,0:T(8,128)}, f32[2,32,4096]{2,1,0:T(8,128)S(1)}, u32[]{:S(2)}, u32[]{:S(2)}) collective-permute-start(f32[2,32,4096]{2,1,0:T(8,128)} %get-tuple-element.124), channel_id=1, source_target_pairs={{0,24},{8,16},{16,8},{24,0},{1,25},{9,17},{17,9},{25,1},{2,26},{10... | collective-permute-start | bytes 3145736 | tf_op jit(solution)/shard_map/ppermute | solution.py:739
  893.6 19.5 %copy-start.1 = (f32[2,32,4096]{2,1,0:T(8,128)S(1)}, f32[2,32,4096]{2,1,0:T(8,128)}, u32[]{:S(2)}) copy-start(f32[2,32,4096]{2,1,0:T(8,128)} %get-tuple-element.125.refs_0_) | copy-start | bytes 3145732
  913.2 44.0 %copy-start.2 = (f32[2,32,4096]{2,1,0:T(8,128)S(1)}, f32[2,32,4096]{2,1,0:T(8,128)}, u32[]{:S(2)}) copy-start(f32[2,32,4096]{2,1,0:T(8,128)} %get-tuple-element.121.refs_0_) | copy-start | bytes 3145732
  (24 other events, 97.8 us)

commit v3 on v2

--- a/solution.py
+++ b/solution.py
@@ -230,85 +230,83 @@
     return jnp.cos(angle), jnp.sin(angle)
 
 
-def lane_convolve(rows, load, store, work, parts, spec, forward_ref, inverse_ref, twiddle_ref, transfer):
-    def put_parts(tile, row, pair):
-        for at, value in enumerate(pair):
-            high, low = two_parts(value)
-            span = pl.ds(tile * rows + row, 16)
-            parts[span, at * LANES : (at + 1) * LANES] = high
-            parts[span, (2 + at) * LANES : (3 + at) * LANES] = low
-            parts[span, (4 + at) * LANES : (5 + at) * LANES] = high
-
-    def forward(i, carry):
-        row = i * 16
-        span = pl.ds(row, 16)
+def lane_convolve(rows, load, store, scratch, forward_ref, inverse_ref, twiddle_ref, transfer):
+    ahead, behind = scratch[0], scratch[1]
+    parts, spec = scratch[2:4], scratch[4:6]
+
+    def twiddle(tile):
+        return twiddle_ref[0, tile : tile + 1, :], twiddle_ref[1, tile : tile + 1, :]
+
+    def forward(chunk):
+        row, out = chunk * 16, parts[chunk % 2]
         for b in range(8):
             x = [load(8 * a + b, row) for a in range(4)]
             y = dft4(x, -1)
             for k in range(4):
                 v = c_rot(y[k], -b * k, 32)
-                work[0, k * 8 + b, span, :] = v[0]
-                work[1, k * 8 + b, span, :] = v[1]
+                ahead[0, k * 8 + b] = v[0]
+                ahead[1, k * 8 + b] = v[1]
         for k in range(4):
-            x = [(work[0, k * 8 + b, span, :], work[1, k * 8 + b, span, :]) for b in range(8)]
-            y = dft8(x, -1)
+            y = dft8([(ahead[0, k * 8 + b], ahead[1, k * 8 + b]) for b in range(8)], -1)
             for m in range(8):
                 tile = k + 4 * m
-                tr, ti = twiddle_ref[0, tile : tile + 1, :], twiddle_ref[1, tile : tile + 1, :]
+                tr, ti = twiddle(tile)
                 re, im = y[m]
-                put_parts(tile, row, (re * tr - im * ti, re * ti + im * tr))
-        return carry
-
-    lax.fori_loop(0, rows // 16, forward, 0)
-    batch = max(1, min(4, 256 // rows))
-
-    def middle(i, carry):
-        span = pl.ds(i * batch * rows, batch * rows)
-        value = dot(parts[span, :], forward_ref[...])
-        pieces = []
-        for t in range(batch):
-            tr, ti = transfer(i * batch + t)
-            re = value[t * rows : (t + 1) * rows, :LANES]
-            im = value[t * rows : (t + 1) * rows, LANES:]
-            pieces.append(jnp.concatenate([re * tr - im * ti, re * ti + im * tr], axis=1))
-        high, low = two_parts(jnp.concatenate(pieces, axis=0))
-        spec[span, :] = dot(jnp.concatenate([high, low, high], axis=1), inverse_ref[...])
-        return carry
-
-    lax.fori_loop(0, 32 // batch, middle, 0, unroll=2)
-
-    def inverse(i, carry):
-        row = i * 16
-        span = pl.ds(row, 16)
+                span = slice(tile * 16, tile * 16 + 16)
+                for at, value in enumerate((re * tr - im * ti, re * ti + im * tr)):
+                    high, low = two_parts(value)
+                    out[span, at * LANES : (at + 1) * LANES] = high
+                    out[span, (2 + at) * LANES : (3 + at) * LANES] = low
+                    out[span, (4 + at) * LANES : (5 + at) * LANES] = high
+
+    def middle(chunk):
+        taken, out = parts[chunk % 2], spec[chunk % 2]
+        for first in range(0, 32, 16):
+            span = slice(first * 16, first * 16 + 256)
+            value = dot(taken[span, :], forward_ref[...])
+            pieces = []
+            for t in range(16):
+                tr, ti = transfer(first + t)
+                re, im = value[t * 16 : t * 16 + 16, :LANES], value[t * 16 : t * 16 + 16, LANES:]
+                pieces.append(jnp.concatenate([re * tr - im * ti, re * ti + im * tr], axis=1))
+            high, low = two_parts(jnp.concatenate(pieces, axis=0))
+            out[span, :] = dot(jnp.concatenate([high, low, high], axis=1), inverse_ref[...])
+
+    def inverse(chunk):
+        row, taken = chunk * 16, spec[chunk % 2]
         for k in range(4):
             x = []
             for m in range(8):
                 tile = k + 4 * m
-                tr, ti = twiddle_ref[0, tile : tile + 1, :], twiddle_ref[1, tile : tile + 1, :]
-                at = pl.ds(tile * rows + row, 16)
-                re, im = spec[at, :LANES], spec[at, LANES:]
+                tr, ti = twiddle(tile)
+                span = slice(tile * 16, tile * 16 + 16)
+                re, im = taken[span, :LANES], taken[span, LANES:]
                 x.append((re * tr + im * ti, im * tr - re * ti))
             y = dft8(x, 1)
             for b in range(8):
                 v = c_rot(y[b], b * k, 32)
-                work[0, k * 8 + b, span, :] = v[0]
-                work[1, k * 8 + b, span, :] = v[1]
+                behind[0, k * 8 + b] = v[0]
+                behind[1, k * 8 + b] = v[1]
         for b in range(8):
-            x = [(work[0, k * 8 + b, span, :], work[1, k * 8 + b, span, :]) for k in range(4)]
-            y = dft4(x, 1)
+            y = dft4([(behind[0, k * 8 + b], behind[1, k * 8 + b]) for k in range(4)], 1)
             for a in range(4):
                 store(8 * a + b, row, y[a])
-        return carry
-
-    lax.fori_loop(0, rows // 16, inverse, 0)
-
-
-def lane_scratch(rows):
-    return [
-        pltpu.VMEM((2, 32, rows, LANES), f32),
-        pltpu.VMEM((32 * rows, 6 * LANES), bf16),
-        pltpu.VMEM((32 * rows, 2 * LANES), f32),
-    ]
+
+    count = rows // 16
+    for t in range(count + 2):
+        if t < count:
+            forward(t)
+        if 0 <= t - 1 < count:
+            middle(t - 1)
+        if 0 <= t - 2 < count:
+            inverse(t - 2)
+
+
+def lane_scratch():
+    work = pltpu.VMEM((2, 32, 16, LANES), f32)
+    parts = pltpu.VMEM((512, 6 * LANES), bf16)
+    spec = pltpu.VMEM((512, 2 * LANES), f32)
+    return [work, work, parts, parts, spec, spec]
 
 
 def params():
@@ -325,7 +323,7 @@
     level, count = plan.level, len(plan.chunks)
 
     def kernel(f_ref, fwd, inv, twd, tra, *rest):
-        outs, (work, parts, spec) = rest[:count], rest[count:]
+        outs, scratch = rest[:count], rest[count:]
 
         def load(tile, row):
             at = slice(tile * LANES, (tile + 1) * LANES)
@@ -337,9 +335,9 @@
             outs[part][owner, 1, pl.ds(row, 16), at] = value[1]
 
         def pick(tile):
-            return tra[0, pl.ds(tile, 1), :], tra[1, pl.ds(tile, 1), :]
-
-        lane_convolve(rows, load, store, work, parts, spec, fwd, inv, twd, pick)
+            return tra[0, tile : tile + 1, :], tra[1, tile : tile + 1, :]
+
+        lane_convolve(rows, load, store, scratch, fwd, inv, twd, pick)
 
     width = field.shape[-1]
     fixed = [tables["forward"], tables["inverse"], tables["twiddle"], transfer]
@@ -348,12 +346,30 @@
         grid=(plan.rows_dev // rows,),
         in_specs=[pl.BlockSpec((2, rows, width), lambda i: (0, i, 0))] + [whole_block(a) for a in fixed],
         out_specs=[pl.BlockSpec((level, 2, rows, w), lambda i: (0, 0, i, 0)) for w in plan.chunks],
-        scratch_shapes=lane_scratch(rows),
+        scratch_shapes=lane_scratch(),
         out_shape=[jax.ShapeDtypeStruct((level, 2, plan.rows_dev, w), f32) for w in plan.chunks],
         compiler_params=params(),
         cost_estimate=pl.CostEstimate(flops=13 * 10**9, bytes_accessed=34 * 10**6, transcendentals=0),
         name="column_pass",
     )(field, *fixed)
+
+
+def cut_rows(plan, field, part, parts):
+    rows, width = plan.piece // parts, field.shape[-1]
+
+    def kernel(x_ref, out_ref):
+        out_ref[0] = x_ref[...]
+
+    return pl.pallas_call(
+        kernel,
+        grid=(plan.planes,),
+        in_specs=[pl.BlockSpec((2, rows, width), lambda p: (0, p * parts + part, 0))],
+        out_specs=pl.BlockSpec((1, 2, rows, width), lambda p: (p, 0, 0, 0)),
+        out_shape=jax.ShapeDtypeStruct((plan.planes, 2, rows, width), f32),
+        compiler_params=params(),
+        cost_estimate=pl.CostEstimate(flops=0, bytes_accessed=9 * 10**6, transcendentals=0),
+        name="cut_rows",
+    )(field)
 
 
 def slot_matrices(plan, bases, weights):
@@ -537,7 +553,7 @@
     scale = 1.0 / plan.planes
 
     def kernel(*refs):
-        g_refs, (h_ref, fwd, inv, twd, tra, out, work, parts, spec) = refs[:count], refs[count:]
+        g_refs, (h_ref, fwd, inv, twd, tra, out), scratch = refs[:count], refs[count : count + 6], refs[count + 6 :]
 
         def load(tile, row):
             owner, part, at = plan.place_of(tile)
@@ -550,9 +566,9 @@
                 out[0, ri, pl.ds(row, 16), at] = before - scale * value[ri]
 
         def pick(tile):
-            return tra[0, 0, pl.ds(tile, 1), :], tra[0, 1, pl.ds(tile, 1), :]
-
-        lane_convolve(rows, load, store, work, parts, spec, fwd, inv, twd, pick)
+            return tra[0, 0, tile : tile + 1, :], tra[0, 1, tile : tile + 1, :]
+
+        lane_convolve(rows, load, store, scratch, fwd, inv, twd, pick)
 
     fixed = [tables["forward"], tables["inverse"], tables["twiddle"]]
     return pl.pallas_call(
@@ -563,7 +579,7 @@
         + [whole_block(a) for a in fixed]
         + [pl.BlockSpec((1, 2, 32, LANES), lambda p, i: (p, 0, 0, 0))],
         out_specs=pl.BlockSpec((1, 2, rows, width), lambda p, i: (p, 0, i, 0)),
-        scratch_shapes=lane_scratch(rows),
+        scratch_shapes=lane_scratch(),
         out_shape=jax.ShapeDtypeStruct((plan.planes, 2, plan.piece, width), f32),
         compiler_params=params(),
         cost_estimate=pl.CostEstimate(flops=13 * 10**9, bytes_accessed=51 * 10**6, transcendentals=0),
@@ -795,10 +811,10 @@
     depths = ordered[jnp.bitwise_xor(jnp.arange(depth, dtype=jnp.int32), d)]
 
     own = field[:, 0]
-    quarters = 4
-    by_rows = own.reshape(2, depth, quarters, plan.piece // quarters, length)
-    early = jnp.moveaxis(by_rows[:, :, 0], 1, 0)
-    own, early, depths = lax.optimization_barrier((own, early, depths))
+    quarters = max(1, min(4, plan.piece // 8))
+    early = cut_rows(plan, own, 0, quarters)
+    own, early = lax.optimization_barrier((own, early))
+    early, depths = lax.optimization_barrier((early, depths))
     held = [exchanged(early, "depth")]
 
     sent = column_pass(plan, own, tables, transfer)
@@ -847,8 +863,8 @@
         if queue:
             value = queue.pop(0)
             if value is None:
-                value = after(by_rows[:, :, len(held)], *others)
-                held.append(exchanged(jnp.moveaxis(value, 1, 0), "depth"))
+                value = cut_rows(plan, field[:, 0], len(held), quarters)
+                held.append(exchanged(after(value, *others), "depth"))
                 before.append(held[-1])
             else:
                 before.append(exchanged(after(value, *others), level_axes))
@@ -857,11 +873,11 @@
                 else:
                     back.append(before[-1])
         for part in range(count):
-            stage = slot - (part + 1)
-            if 0 <= stage < len(stages):
-                state[part] = stages[stage](state[part], part, others)
+            number = slot - (part + 1)
+            if 0 <= number < len(stages):
+                state[part] = stages[number](state[part], part, others)
                 before.append(state[part])
-                if stage == len(stages) - 1:
+                if number == len(stages) - 1:
                     queue.append(state[part])
         if slot == 0:
             before += [high, low]

time: 973 us -> 968 us (level)
  local copies, waits for them, and re-layouts: 34.7 us -> 15.3 us
  waiting for transfers between devices: 340 us -> 353 us
  starting transfers between devices: 103 us -> 113 us
    ppermute x1, waiting for transfers between devices: 1.48 us -> 32 us  [per_device(): above = lax.ppermute(moved[:, :, -1:], all_axes, downward)]
    ppermute x32, waiting for transfers between devices: 214 us -> 188 us  [swapped(): return lax.ppermute(value, axes, [(i, i ^ step) for i in range(size)])]
    pallas_call x0 -> x4, Pallas kernels: none -> 19.4 us  [cut_rows(): pl.pallas_call(kernel, grid=(plan.planes,), in_specs=[pl.BlockSpec((2, ro...]
    unnamed x88 -> x82, local copies, waits for them, and re-layouts: 17.6 us -> 2.81 us
    pallas_call x1, Pallas kernels: 47.9 us -> 35 us  [step_pass(): pl.pallas_call(kernel, grid=(plan.planes, plan.piece // rows), in_specs=[...]
    pallas_call x1, Pallas kernels: 45.6 us -> 33.4 us  [column_pass(): pl.pallas_call(kernel, grid=(plan.rows_dev // rows,), in_specs=[pl.BlockS...]
    slice x1 -> x0, local copies, waits for them, and re-layouts: 10.9 us -> none  [per_device(): value = after(by_rows[:, :, len(held)], *others)]
  transfers between devices with their start and end apart: 46 -> 46, of which waited for: 25 -> 25; matrix products, arithmetic and copies ran while one was open for 8% -> 5% of each run, Pallas kernels for 39% -> 40%
where the time goes in v3:
time: 968 us; the launch traced here: 957 us
  Pallas kernels  430 us (44%)
  waiting for transfers between devices  353 us (36%)
  starting transfers between devices  113 us (12%)
  other arithmetic  43.6 us (5%)
  local copies, waits for them, and re-layouts  15.3 us (2%)
    ppermute x32, waiting for transfers between devices, swapped(): return lax.ppermute(value, axes, [(i, i ^ step) for i in range(size)])  188 us
    pallas_call x4, Pallas kernels, row_backward(): pl.pallas_call(kernel, grid_spec=pltpu.PrefetchScalarGridSpec(num_scalar_...  144 us
    all_to_all x12, waiting for transfers between devices, exchanged(): return lax.all_to_all(value, axes, 0, 0, tiled=True)  128 us
    pallas_call x4, Pallas kernels, row_forward(): pl.pallas_call(kernel, grid_spec=pltpu.PrefetchScalarGridSpec(num_scalar_...  105 us
    all_to_all x12, starting transfers between devices, exchanged(): return lax.all_to_all(value, axes, 0, 0, tiled=True)  58.3 us
    ppermute x32, starting transfers between devices, swapped(): return lax.ppermute(value, axes, [(i, i ^ step) for i in range(size)])  49.4 us
    pallas_call x4, Pallas kernels, shrink_pass(): pl.pallas_call(kernel, grid_spec=pltpu.PrefetchScalarGridSpec(num_scalar_...  44.7 us
    pallas_call x1, Pallas kernels, step_pass(): pl.pallas_call(kernel, grid=(plan.planes, plan.piece // rows), in_specs=[...  35 us
  transfers between devices with their start and end apart: 46, of which 25 were waited for; matrix products, arithmetic and copies ran while one was open for 5% of the time, Pallas kernels for 40%

profile of v3, /device:TPU:0, one launch (start us, length us, event | category | flops | bytes accessed | tf_op | source)
XLA Modules:
  0.0 957.1 jit_solution(7446888666775330359)
XLA Ops:
  0.0 3.9 collective-permute-start.2
  5.2 4.8 cut_rows.4
  12.6 5.0 all-to-all-start
  18.4 33.4 %column_pass.1 = (f32[8,2,512,128]{3,2,1,0:T(8,128)}, f32[8,2,512,128]{3,2,1,0:T(8,128)}, f32[8,2,512,128]{3,2,1,0:T(8,128)}, f32[8,2,512,128]{3,2,1,0:T(8,128)}) custom-call(f32[2,512,4096]{2,1,0:T(8,128)} %bitcast.33, bf16[768,256]{1,0:T(8,128)(2,1)} %constant.31.clone.fwd.refs_5_, bf16[768,256]{1,0:T(8,128)(2,1)} %constant.32.clone.inv.refs_6_, ...), custom_call_target="tpu_custom_call" | custom-call | flops 12999999488 | bytes 34000000 | tf_op jit(solution)/shard_map/column_pass/pallas_call | solution.py:344
  53.1 11.6 %all-to-all-done = f32[4,2,32,4096]{3,2,1,0:T(8,128)} async-done(((f32[4,2,32,4096]{3,2,1,0:T(8,128)}), f32[4,2,32,4096]{3,2,1,0:T(8,128)}, u32[]{:S(2)}, u32[]{:S(2)}) %all-to-all-start) | async-done | bytes 4194336 | tf_op jit(solution)/shard_map/all_to_all | solution.py:786
  64.7 4.6 all-to-all-start.1
  69.3 33.2 %slot_matrices.1 = (bf16[16,256,2048]{2,1,0:T(8,128)(2,1)}, bf16[16,256,2048]{2,1,0:T(8,128)(2,1)}) custom-call(f32[16,256,256]{2,1,0:T(8,128)} %constant.108.clone.b_ref, f32[16,8,256]{2,1,0:T(8,128)} %copy.32.w_ref), custom_call_target="tpu_custom_call" | custom-call | flops 25999998976 | bytes 34000000 | tf_op jit(solution)/shard_map/slot_matrices/pallas_call | solution.py:395
  102.5 15.9 %all-to-all-done.1.x_ref = f32[8,2,512,128]{3,2,1,0:T(8,128)} async-done(((f32[8,2,512,128]{3,2,1,0:T(8,128)}), f32[8,2,512,128]{3,2,1,0:T(8,128)}, u32[]{:S(2)}, u32[]{:S(2)}) %all-to-all-start.1) | async-done | bytes 4194336 | tf_op jit(solution)/shard_map/all_to_all | solution.py:786
  118.4 5.1 all-to-all-start.2
  129.7 26.3 %row_forward.4 = f32[16,256,128]{2,1,0:T(8,128)} custom-call(f32[4,16]{1,0:T(4,128)} %pad_maximum_fusion.10.phase, f32[8,2,512,128]{3,2,1,0:T(8,128)} %all-to-all-done.1.x_ref, f32[2,512,128]{2,1,0:T(8,128)} %get-tuple-element.156.h_ref, bf16[16,256,2048]{2,1,0:T(8,128)(2,1)} %get-tuple-element.84.wh, bf16[16,256,2048]{2,1,0:T(8,128)(2,1)} %get-tuple-element.85.wl), custom_call_target="tpu_custom_call" | custom-call | flops 12999999488 | bytes 60000000 | tf_op jit(solution)/shard_map/row_forward/pallas_call | solution.py:458
  156.0 16.6 %all-to-all-done.2.x_ref = f32[8,2,512,128]{3,2,1,0:T(8,128)} async-done(((f32[8,2,512,128]{3,2,1,0:T(8,128)}), f32[8,2,512,128]{3,2,1,0:T(8,128)}, u32[]{:S(2)}, u32[]{:S(2)}) %all-to-all-start.2) | async-done | bytes 4194336 | tf_op jit(solution)/shard_map/all_to_all | solution.py:786
  172.6 4.6 all-to-all-start.3
  179.2 26.3 %row_forward.5 = f32[16,256,128]{2,1,0:T(8,128)} custom-call(f32[4,16]{1,0:T(4,128)} %pad_maximum_fusion.10.phase, f32[8,2,512,128]{3,2,1,0:T(8,128)} %all-to-all-done.2.x_ref, f32[2,512,128]{2,1,0:T(8,128)} %get-tuple-element.155.h_ref, bf16[16,256,2048]{2,1,0:T(8,128)(2,1)} %get-tuple-element.84.wh, bf16[16,256,2048]{2,1,0:T(8,128)(2,1)} %get-tuple-element.85.wl), custom_call_target="tpu_custom_call" | custom-call | flops 12999999488 | bytes 60000000 | tf_op jit(solution)/shard_map/row_forward/pallas_call | solution.py:458
  206.9 19.5 %all-to-all-done.3.x_ref = f32[8,2,512,128]{3,2,1,0:T(8,128)} async-done(((f32[8,2,512,128]{3,2,1,0:T(8,128)}), f32[8,2,512,128]{3,2,1,0:T(8,128)}, u32[]{:S(2)}, u32[]{:S(2)}) %all-to-all-start.3) | async-done | bytes 4194336 | tf_op jit(solution)/shard_map/all_to_all | solution.py:786
  226.3 4.7 all-to-all-start.4
  231.1 5.0 cut_rows.5
  242.4 26.3 %row_forward.6 = f32[16,256,128]{2,1,0:T(8,128)} custom-call(f32[4,16]{1,0:T(4,128)} %pad_maximum_fusion.10.phase, f32[8,2,512,128]{3,2,1,0:T(8,128)} %all-to-all-done.3.x_ref, f32[2,512,128]{2,1,0:T(8,128)} %get-tuple-element.154.h_ref, bf16[16,256,2048]{2,1,0:T(8,128)(2,1)} %get-tuple-element.84.wh, bf16[16,256,2048]{2,1,0:T(8,128)(2,1)} %get-tuple-element.85.wl), custom_call_target="tpu_custom_call" | custom-call | flops 12999999488 | bytes 60000000 | tf_op jit(solution)/shard_map/row_forward/pallas_call | solution.py:458
  269.5 6.9 collective-permute-done.6
  280.2 4.9 all-to-all-start.5
  285.1 4.9 cut_rows.6
  296.6 26.3 %row_forward.7 = f32[16,256,128]{2,1,0:T(8,128)} custom-call(f32[4,16]{1,0:T(4,128)} %pad_maximum_fusion.10.phase, f32[8,2,512,128]{3,2,1,0:T(8,128)} %all-to-all-done.4.x_ref, f32[2,512,128]{2,1,0:T(8,128)} %get-tuple-element.153.h_ref, bf16[16,256,2048]{2,1,0:T(8,128)(2,1)} %get-tuple-element.84.wh, bf16[16,256,2048]{2,1,0:T(8,128)(2,1)} %get-tuple-element.85.wl), custom_call_target="tpu_custom_call" | custom-call | flops 12999999488 | bytes 60000000 | tf_op jit(solution)/shard_map/row_forward/pallas_call | solution.py:458
  322.9 14.6 %collective-permute-done.8 = f32[4,256,128]{2,1,0:T(8,128)} collective-permute-done((f32[4,256,128]{2,1,0:T(8,128)}, f32[4,256,128]{2,1,0:T(8,128)}, u32[]{:S(2)}, u32[]{:S(2)}) %collective-permute-start.8) | collective-permute-done | bytes 524320 | tf_op jit(solution)/shard_map/ppermute | solution.py:755
  343.9 5.2 all-to-all-start.6
  349.1 4.1 collective-permute-start.10
  354.2 4.8 cut_rows.7
  359.7 16.7 %collective-permute-done.11 = f32[4,256,128]{2,1,0:T(8,128)} collective-permute-done((f32[4,256,128]{2,1,0:T(8,128)}, f32[4,256,128]{2,1,0:T(8,128)}, u32[]{:S(2)}, u32[]{:S(2)}) %collective-permute-start.11) | collective-permute-done | bytes 524320 | tf_op jit(solution)/shard_map/ppermute | solution.py:755
  378.7 16.9 %collective-permute-done.12 = f32[4,256,128]{2,1,0:T(8,128)} collective-permute-done((f32[4,256,128]{2,1,0:T(8,128)}, f32[4,256,128]{2,1,0:T(8,128)}, u32[]{:S(2)}, u32[]{:S(2)}) %collective-permute-start.12) | collective-permute-done | bytes 524320 | tf_op jit(solution)/shard_map/ppermute | solution.py:755
  400.7 18.3 %collective-permute-done.13 = f32[8,256,128]{2,1,0:T(8,128)S(1)} collective-permute-done((f32[8,256,128]{2,1,0:T(8,128)}, f32[8,256,128]{2,1,0:T(8,128)S(1)}, u32[]{:S(2)}, u32[]{:S(2)}) %collective-permute-start.13) | collective-permute-done | bytes 1048608 | tf_op jit(solution)/shard_map/ppermute | solution.py:755
  419.3 5.2 all-to-all-start.7
  425.3 4.2 collective-permute-start.15
  429.5 36.0 %row_backward.4 = f32[8,8,128,128]{3,2,1,0:T(8,128)} custom-call(f32[4,16]{1,0:T(4,128)} %pad_maximum_fusion.10.phase, f32[16,256,128]{2,1,0:T(8,128)} %pad_maximum_fusion.1.m_ref, bf16[16,256,2048]{2,1,0:T(8,128)(2,1)} %get-tuple-element.84.wh, bf16[16,256,2048]{2,1,0:T(8,128)(2,1)} %get-tuple-element.85.wl), custom_call_target="tpu_custom_call" | custom-call | flops 12999999488 | bytes 60000000 | tf_op jit(solution)/shard_map/row_backward/pallas_call | solution.py:525
  466.6 3.1 collective-permute-done.16
  474.9 5.2 all-to-all-start.8
  485.3 36.0 %row_backward.5 = f32[8,8,128,128]{3,2,1,0:T(8,128)} custom-call(f32[4,16]{1,0:T(4,128)} %pad_maximum_fusion.10.phase, f32[16,256,128]{2,1,0:T(8,128)} %pad_maximum_fusion.2.m_ref, bf16[16,256,2048]{2,1,0:T(8,128)(2,1)} %get-tuple-element.84.wh, bf16[16,256,2048]{2,1,0:T(8,128)(2,1)} %get-tuple-element.85.wl), custom_call_target="tpu_custom_call" | custom-call | flops 12999999488 | bytes 60000000 | tf_op jit(solution)/shard_map/row_backward/pallas_call | solution.py:525
  524.4 4.8 all-to-all-done.8.refs_0_
  529.2 4.6 all-to-all-start.9
  536.7 36.0 %row_backward.6 = f32[8,8,128,128]{3,2,1,0:T(8,128)} custom-call(f32[4,16]{1,0:T(4,128)} %pad_maximum_fusion.10.phase, f32[16,256,128]{2,1,0:T(8,128)} %pad_maximum_fusion.3.m_ref, bf16[16,256,2048]{2,1,0:T(8,128)(2,1)} %get-tuple-element.84.wh, bf16[16,256,2048]{2,1,0:T(8,128)(2,1)} %get-tuple-element.85.wl), custom_call_target="tpu_custom_call" | custom-call | flops 12999999488 | bytes 60000000 | tf_op jit(solution)/shard_map/row_backward/pallas_call | solution.py:525
  574.3 8.6 all-to-all-done.9.refs_1_
  582.9 4.6 all-to-all-start.10
  587.5 36.0 %row_backward.7 = f32[8,8,128,128]{3,2,1,0:T(8,128)} custom-call(f32[4,16]{1,0:T(4,128)} %pad_maximum_fusion.10.phase, f32[16,256,128]{2,1,0:T(8,128)} %pad_maximum_fusion.4.m_ref, bf16[16,256,2048]{2,1,0:T(8,128)(2,1)} %get-tuple-element.84.wh, bf16[16,256,2048]{2,1,0:T(8,128)(2,1)} %get-tuple-element.85.wl), custom_call_target="tpu_custom_call" | custom-call | flops 12999999488 | bytes 60000000 | tf_op jit(solution)/shard_map/row_backward/pallas_call | solution.py:525
  623.5 13.1 %all-to-all-done.10.refs_2_ = f32[8,8,128,128]{3,2,1,0:T(8,128)} async-done(((f32[8,8,128,128]{3,2,1,0:T(8,128)}), f32[8,8,128,128]{3,2,1,0:T(8,128)}, u32[]{:S(2)}, u32[]{:S(2)}) %all-to-all-start.10) | async-done | bytes 4194336 | tf_op jit(solution)/shard_map/all_to_all | solution.py:786
  636.6 4.8 all-to-all-start.11
  642.5 6.4 pad_maximum_fusion
  648.9 6.2 copy.30
  655.2 35.4 %all-to-all-done.11.refs_3_ = f32[8,8,128,128]{3,2,1,0:T(8,128)} async-done(((f32[8,8,128,128]{3,2,1,0:T(8,128)}), f32[8,8,128,128]{3,2,1,0:T(8,128)}, u32[]{:S(2)}, u32[]{:S(2)}) %all-to-all-start.11) | async-done | bytes 4194336 | tf_op jit(solution)/shard_map/all_to_all | solution.py:786
  690.6 35.0 %step_pass.1.cur.nxt.up = f32[4,2,128,4096]{3,2,1,0:T(8,128)} custom-call(f32[8,8,128,128]{3,2,1,0:T(8,128)} %all-to-all-done.8.refs_0_, f32[8,8,128,128]{3,2,1,0:T(8,128)} %all-to-all-done.9.refs_1_, f32[8,8,128,128]{3,2,1,0:T(8,128)} %all-to-all-done.10.refs_2_, f32[8,8,128,128]{3,2,1,0:T(8,128)} %all-to-all-done.11.refs_3_, f32[4,2,128,4096]{3,2,1,0:T(8,128)} %bitcast.37, ...), custom_call_target="tpu_custom_call" | custom-call | flops 12999999488 | bytes 51000000 | tf_op jit(solution)/shard_map/step_pass/pallas_call | solution.py:574
  729.2 5.0 collective-permute-done.20.down
  734.8 11.2 %shrink_pass.5 = (f32[2,32,4096]{2,1,0:T(8,128)}, f32[2,32,4096]{2,1,0:T(8,128)}, f32[2,32,4096]{2,1,0:T(8,128)}, f32[2,32,4096]{2,1,0:T(8,128)}) custom-call(s32[3]{0:T(128)} %pad_add_fusion.scal, f32[4,2,128,4096]{3,2,1,0:T(8,128)} %step_pass.1.cur.nxt.up, f32[4,2,128,4096]{3,2,1,0:T(8,128)} %step_pass.1.cur.nxt.up, ...), custom_call_target="tpu_custom_call" | custom-call | flops 100000000 | bytes 9000000 | tf_op jit(solution)/shard_map/shrink_pass/pallas_call | solution.py:673
  747.9 11.3 %shrink_pass.6 = (f32[2,32,4096]{2,1,0:T(8,128)}, f32[2,32,4096]{2,1,0:T(8,128)}, f32[2,32,4096]{2,1,0:T(8,128)}, f32[2,32,4096]{2,1,0:T(8,128)}) custom-call(s32[3]{0:T(128)} %pad_add_fusion.scal, f32[4,2,128,4096]{3,2,1,0:T(8,128)} %step_pass.1.cur.nxt.up, f32[4,2,128,4096]{3,2,1,0:T(8,128)} %step_pass.1.cur.nxt.up, ...), custom_call_target="tpu_custom_call" | custom-call | flops 100000000 | bytes 9000000 | tf_op jit(solution)/shard_map/shrink_pass/pallas_call | solution.py:673
  759.3 4.1 collective-permute-start.30
  765.0 32.0 %collective-permute-done.30.up = f32[4,2,1,4096]{3,2,1,0:T(1,128)S(1)} collective-permute-done((f32[4,2,1,4096]{3,2,1,0:T(1,128)S(1)}, f32[4,2,1,4096]{3,2,1,0:T(1,128)S(1)}, u32[]{:S(2)}, u32[]{:S(2)}) %collective-permute-start.30) | collective-permute-done | bytes 131104 | tf_op jit(solution)/shard_map/ppermute | solution.py:894
  797.7 11.0 %shrink_pass.7 = (f32[2,32,4096]{2,1,0:T(8,128)}, f32[2,32,4096]{2,1,0:T(8,128)}, f32[2,32,4096]{2,1,0:T(8,128)}, f32[2,32,4096]{2,1,0:T(8,128)}) custom-call(s32[3]{0:T(128)} %pad_add_fusion.scal, f32[4,2,128,4096]{3,2,1,0:T(8,128)} %step_pass.1.cur.nxt.up, f32[4,2,128,4096]{3,2,1,0:T(8,128)} %step_pass.1.cur.nxt.up, f32[4,2,1,4096]{3,2,1,0:T(1,128)} %copy-done.22, ...), custom_call_target="tpu_custom_call" | custom-call | flops 100000000 | bytes 9000000 | tf_op jit(solution)/shard_map/shrink_pass/pallas_call | solution.py:673
  812.7 11.3 %shrink_pass.4 = (f32[2,32,4096]{2,1,0:T(8,128)}, f32[2,32,4096]{2,1,0:T(8,128)}, f32[2,32,4096]{2,1,0:T(8,128)}, f32[2,32,4096]{2,1,0:T(8,128)}) custom-call(s32[3]{0:T(128)} %pad_add_fusion.scal, f32[4,2,128,4096]{3,2,1,0:T(8,128)} %step_pass.1.cur.nxt.up, f32[4,2,128,4096]{3,2,1,0:T(8,128)} %step_pass.1.cur.nxt.up, ...), custom_call_target="tpu_custom_call" | custom-call | flops 100000000 | bytes 9000000 | tf_op jit(solution)/shard_map/shrink_pass/pallas_call | solution.py:673
  826.0 16.6 %collective-permute-done.31.refs_1_ = f32[2,32,4096]{2,1,0:T(8,128)} collective-permute-done((f32[2,32,4096]{2,1,0:T(8,128)}, f32[2,32,4096]{2,1,0:T(8,128)}, u32[]{:S(2)}, u32[]{:S(2)}) %collective-permute-start.31) | collective-permute-done | bytes 1048608 | tf_op jit(solution)/shard_map/ppermute | solution.py:755
  842.7 3.4 collective-permute-start.22
  846.0 18.8 %collective-permute-done.33.refs_3_ = f32[2,32,4096]{2,1,0:T(8,128)} collective-permute-done((f32[2,32,4096]{2,1,0:T(8,128)}, f32[2,32,4096]{2,1,0:T(8,128)}, u32[]{:S(2)}, u32[]{:S(2)}) %collective-permute-start.33) | collective-permute-done | bytes 1048608 | tf_op jit(solution)/shard_map/ppermute | solution.py:755
  864.8 3.1 collective-permute-start.23
  869.2 4.6 place_rows.4.refs_4_
  873.8 4.2 place_rows.5.refs_4_
  878.1 9.2 collective-permute-done.25.refs_2_
  887.2 22.6 %collective-permute-done.26.refs_3_ = f32[2,32,4096]{2,1,0:T(8,128)S(1)} collective-permute-done((f32[2,32,4096]{2,1,0:T(8,128)}, f32[2,32,4096]{2,1,0:T(8,128)S(1)}, u32[]{:S(2)}, u32[]{:S(2)}) %collective-permute-start.26) | collective-permute-done | bytes 1048608 | tf_op jit(solution)/shard_map/ppermute | solution.py:755
  909.8 3.2 place_rows.6.refs_4_
  913.0 40.4 %collective-permute-done.22.refs_2_ = f32[2,32,4096]{2,1,0:T(8,128)S(1)} collective-permute-done((f32[2,32,4096]{2,1,0:T(8,128)}, f32[2,32,4096]{2,1,0:T(8,128)S(1)}, u32[]{:S(2)}, u32[]{:S(2)}) %collective-permute-start.22) | collective-permute-done | bytes 1048608 | tf_op jit(solution)/shard_map/ppermute | solution.py:755
  953.4 3.2 place_rows.7
  (186 shorter events, 84.7 us)
Async XLA Ops:
  0.0 9.9 %collective-permute-start.2 = (f32[1]{0:T(128)}, f32[1]{0:T(128)}, u32[]{:S(2)}, u32[]{:S(2)}) collective-permute-start(f32[1]{0:T(128)} %param.23), channel_id=1, source_target_pairs={{0,24},{8,16},{16,8},{24,0},{1,25},{9,17},{17,9},{25,1},{2,26},{10... | collective-permute-start | bytes 20 | tf_op jit(solution)/shard_map/ppermute | solution.py:755
  3.9 6.1 collective-permute-start.1
  4.4 5.6 collective-permute-start
  12.6 52.1 %all-to-all-start = ((f32[4,2,32,4096]{3,2,1,0:T(8,128)}), f32[4,2,32,4096]{3,2,1,0:T(8,128)}, u32[]{:S(2)}, u32[]{:S(2)}) async-start(f32[4,2,32,4096]{3,2,1,0:T(8,128)} %cut_rows.4), calls=%async_computation | async-start | bytes 8388608 | tf_op jit(solution)/shard_map/all_to_all | solution.py:786
  18.4 33.5 %copy-start.31 = (f32[16,256]{1,0:T(8,128)S(1)}, f32[16,256]{1,0:T(8,128)}, u32[]{:S(2)}) copy-start(f32[16,256]{1,0:T(8,128)} %constant.120) | copy-start | bytes 49156
  18.4 33.5 %copy-start.32 = (f32[16,256]{1,0:T(8,128)S(1)}, f32[16,256]{1,0:T(8,128)}, u32[]{:S(2)}) copy-start(f32[16,256]{1,0:T(8,128)} %constant.119) | copy-start | bytes 49156
  18.4 33.5 %copy-start.33 = (f32[16,256]{1,0:T(8,128)S(1)}, f32[16,256]{1,0:T(8,128)}, u32[]{:S(2)}) copy-start(f32[16,256]{1,0:T(8,128)} %constant.118) | copy-start | bytes 49156
  18.4 33.5 %copy-start.34 = (f32[16,256]{1,0:T(8,128)S(1)}, f32[16,256]{1,0:T(8,128)}, u32[]{:S(2)}) copy-start(f32[16,256]{1,0:T(8,128)} %constant.117) | copy-start | bytes 49156
  64.7 53.7 %all-to-all-start.1 = ((f32[8,2,512,128]{3,2,1,0:T(8,128)}), f32[8,2,512,128]{3,2,1,0:T(8,128)}, u32[]{:S(2)}, u32[]{:S(2)}) async-start(f32[8,2,512,128]{3,2,1,0:T(8,128)} %get-tuple-element.81), calls=%async_computation.1 | async-start | bytes 8388608 | tf_op jit(solution)/shard_map/all_to_all | solution.py:786
  118.4 54.2 %all-to-all-start.2 = ((f32[8,2,512,128]{3,2,1,0:T(8,128)}), f32[8,2,512,128]{3,2,1,0:T(8,128)}, u32[]{:S(2)}, u32[]{:S(2)}) async-start(f32[8,2,512,128]{3,2,1,0:T(8,128)} %get-tuple-element.88), calls=%async_computation.2 | async-start | bytes 8388608 | tf_op jit(solution)/shard_map/all_to_all | solution.py:786
  125.3 2.8 collective-permute-start.3
  156.0 21.2 %copy-start.9 = (f32[16,256,128]{2,1,0:T(8,128)S(1)}, f32[16,256,128]{2,1,0:T(8,128)}, u32[]{:S(2)}) copy-start(f32[16,256,128]{2,1,0:T(8,128)} %row_forward.4) | copy-start | bytes 6291460
  172.6 53.7 %all-to-all-start.3 = ((f32[8,2,512,128]{3,2,1,0:T(8,128)}), f32[8,2,512,128]{3,2,1,0:T(8,128)}, u32[]{:S(2)}, u32[]{:S(2)}) async-start(f32[8,2,512,128]{3,2,1,0:T(8,128)} %get-tuple-element.91), calls=%async_computation.3 | async-start | bytes 8388608 | tf_op jit(solution)/shard_map/all_to_all | solution.py:786
  177.4 28.1 %collective-permute-start.4 = (f32[8,256,128]{2,1,0:T(8,128)S(1)}, f32[8,256,128]{2,1,0:T(8,128)}, u32[]{:S(2)}, u32[]{:S(2)}) collective-permute-start(f32[8,256,128]{2,1,0:T(8,128)S(1)} %slice_select_fusion.3), channel_id=1, source_target_pairs={{0,2},{2,0},{4,6},{6,4},{1,3},{3,1},{5,7},{7,5},{8,10},{10,8},{12,... | collective-permute-start | bytes 3145736 | tf_op jit(solution)/shard_map/ppermute | solution.py:755
  226.3 53.9 %all-to-all-start.4 = ((f32[8,2,512,128]{3,2,1,0:T(8,128)}), f32[8,2,512,128]{3,2,1,0:T(8,128)}, u32[]{:S(2)}, u32[]{:S(2)}) async-start(f32[8,2,512,128]{3,2,1,0:T(8,128)} %get-tuple-element.95), calls=%async_computation.4 | async-start | bytes 8388608 | tf_op jit(solution)/shard_map/all_to_all | solution.py:786
  238.0 30.6 %collective-permute-start.5 = (f32[4,256,128]{2,1,0:T(8,128)}, f32[4,256,128]{2,1,0:T(8,128)S(1)}, u32[]{:S(2)}, u32[]{:S(2)}) collective-permute-start(f32[4,256,128]{2,1,0:T(8,128)} %slice_select_fusion.7), channel_id=1, source_target_pairs={{0,4},{2,6},{4,0},{6,2},{1,5},{3,7},{5,1},{7,3},{8,12},{10,14},{12... | collective-permute-start | bytes 1572872 | tf_op jit(solution)/shard_map/ppermute | solution.py:755
  240.8 35.6 %collective-permute-start.6 = (f32[8,256,128]{2,1,0:T(8,128)}, f32[8,256,128]{2,1,0:T(8,128)}, u32[]{:S(2)}, u32[]{:S(2)}) collective-permute-start(f32[8,256,128]{2,1,0:T(8,128)} %slice_select_fusion.2), channel_id=1, source_target_pairs={{0,2},{2,0},{4,6},{6,4},{1,3},{3,1},{5,7},{7,5},{8,10},{10,8},{12,... | collective-permute-start | bytes 3145736 | tf_op jit(solution)/shard_map/ppermute | solution.py:755
  280.2 63.6 %all-to-all-start.5 = ((f32[4,2,32,4096]{3,2,1,0:T(8,128)}), f32[4,2,32,4096]{3,2,1,0:T(8,128)}, u32[]{:S(2)}, u32[]{:S(2)}) async-start(f32[4,2,32,4096]{3,2,1,0:T(8,128)} %cut_rows.5), calls=%async_computation.5 | async-start | bytes 8388608 | tf_op jit(solution)/shard_map/all_to_all | solution.py:786
  291.9 47.6 %collective-permute-start.7 = (f32[4,256,128]{2,1,0:T(8,128)S(1)}, f32[4,256,128]{2,1,0:T(8,128)}, u32[]{:S(2)}, u32[]{:S(2)}) collective-permute-start(f32[4,256,128]{2,1,0:T(8,128)S(1)} %copy-done.21), channel_id=1, source_target_pairs={{0,4},{2,6},{4,0},{6,2},{1,5},{3,7},{5,1},{7,3},{8,12},{10,14},{12... | collective-permute-start | bytes 1572872 | tf_op jit(solution)/shard_map/ppermute | solution.py:755
  294.7 42.9 %collective-permute-start.8 = (f32[4,256,128]{2,1,0:T(8,128)}, f32[4,256,128]{2,1,0:T(8,128)}, u32[]{:S(2)}, u32[]{:S(2)}) collective-permute-start(f32[4,256,128]{2,1,0:T(8,128)} %slice_select_fusion.6), channel_id=1, source_target_pairs={{0,4},{2,6},{4,0},{6,2},{1,5},{3,7},{5,1},{7,3},{8,12},{10,14},{12... | collective-permute-start | bytes 1572872 | tf_op jit(solution)/shard_map/ppermute | solution.py:755
  294.9 47.6 %collective-permute-start.9 = (f32[8,256,128]{2,1,0:T(8,128)}, f32[8,256,128]{2,1,0:T(8,128)}, u32[]{:S(2)}, u32[]{:S(2)}) collective-permute-start(f32[8,256,128]{2,1,0:T(8,128)} %slice_select_fusion.1), channel_id=1, source_target_pairs={{0,2},{2,0},{4,6},{6,4},{1,3},{3,1},{5,7},{7,5},{8,10},{10,8},{12,... | collective-permute-start | bytes 3145736 | tf_op jit(solution)/shard_map/ppermute | solution.py:755
  343.9 75.4 %all-to-all-start.6 = ((f32[4,2,32,4096]{3,2,1,0:T(8,128)}), f32[4,2,32,4096]{3,2,1,0:T(8,128)}, u32[]{:S(2)}, u32[]{:S(2)}) async-start(f32[4,2,32,4096]{3,2,1,0:T(8,128)} %cut_rows.6), calls=%async_computation.6 | async-start | bytes 8388608 | tf_op jit(solution)/shard_map/all_to_all | solution.py:786
  349.1 27.3 %collective-permute-start.11 = (f32[4,256,128]{2,1,0:T(8,128)}, f32[4,256,128]{2,1,0:T(8,128)}, u32[]{:S(2)}, u32[]{:S(2)}) collective-permute-start(f32[4,256,128]{2,1,0:T(8,128)} %select_add_fusion.6), channel_id=1, source_target_pairs={{0,4},{2,6},{4,0},{6,2},{1,5},{3,7},{5,1},{7,3},{8,12},{10,14},{12... | collective-permute-start | bytes 1572872 | tf_op jit(solution)/shard_map/ppermute | solution.py:755
  349.1 48.7 %collective-permute-start.10 = (f32[8,256,128]{2,1,0:T(8,128)}, f32[8,256,128]{2,1,0:T(8,128)}, u32[]{:S(2)}, u32[]{:S(2)}) collective-permute-start(f32[8,256,128]{2,1,0:T(8,128)} %get-tuple-element.103), channel_id=1, source_target_pairs={{0,2},{2,0},{4,6},{6,4},{1,3},{3,1},{5,7},{7,5},{8,10},{10,8},{12,... | collective-permute-start | bytes 3145736 | tf_op jit(solution)/shard_map/ppermute | solution.py:755
  354.1 22.3 %copy-start.19 = (f32[4,256,128]{2,1,0:T(8,128)S(1)}, f32[4,256,128]{2,1,0:T(8,128)}, u32[]{:S(2)}) copy-start(f32[4,256,128]{2,1,0:T(8,128)} %select_add_fusion.6) | copy-start | bytes 1572868
  354.1 41.5 %collective-permute-start.12 = (f32[4,256,128]{2,1,0:T(8,128)}, f32[4,256,128]{2,1,0:T(8,128)}, u32[]{:S(2)}, u32[]{:S(2)}) collective-permute-start(f32[4,256,128]{2,1,0:T(8,128)} %slice_select_fusion.5), channel_id=1, source_target_pairs={{0,4},{2,6},{4,0},{6,2},{1,5},{3,7},{5,1},{7,3},{8,12},{10,14},{12... | collective-permute-start | bytes 1572872 | tf_op jit(solution)/shard_map/ppermute | solution.py:755
  358.9 38.9 %copy-start.15 = (f32[4,256,128]{2,1,0:T(8,128)S(1)}, f32[4,256,128]{2,1,0:T(8,128)}, u32[]{:S(2)}) copy-start(f32[4,256,128]{2,1,0:T(8,128)} %copy-done.14) | copy-start | bytes 1572868
  358.9 38.9 %copy-start.17 = (f32[4,256,128]{2,1,0:T(8,128)S(1)}, f32[4,256,128]{2,1,0:T(8,128)}, u32[]{:S(2)}) copy-start(f32[4,256,128]{2,1,0:T(8,128)} %copy-done.16) | copy-start | bytes 1572868
  358.9 60.1 %collective-permute-start.13 = (f32[8,256,128]{2,1,0:T(8,128)}, f32[8,256,128]{2,1,0:T(8,128)S(1)}, u32[]{:S(2)}, u32[]{:S(2)}) collective-permute-start(f32[8,256,128]{2,1,0:T(8,128)} %get-tuple-element.107), channel_id=1, source_target_pairs={{0,2},{2,0},{4,6},{6,4},{1,3},{3,1},{5,7},{7,5},{8,10},{10,8},{12,... | collective-permute-start | bytes 3145736 | tf_op jit(solution)/shard_map/ppermute | solution.py:755
  377.5 20.0 %copy-start.10 = (f32[4,256,128]{2,1,0:T(8,128)}, f32[4,256,128]{2,1,0:T(8,128)S(1)}, u32[]{:S(2)}) copy-start(f32[4,256,128]{2,1,0:T(8,128)S(1)} %get-tuple-element.161) | copy-start | bytes 1572868
  377.6 19.9 %copy-start.12 = (f32[4,256,128]{2,1,0:T(8,128)}, f32[4,256,128]{2,1,0:T(8,128)S(1)}, u32[]{:S(2)}) copy-start(f32[4,256,128]{2,1,0:T(8,128)S(1)} %get-tuple-element.162) | copy-start | bytes 1572868
  419.3 55.6 %all-to-all-start.7 = ((f32[4,2,32,4096]{3,2,1,0:T(8,128)}), f32[4,2,32,4096]{3,2,1,0:T(8,128)}, u32[]{:S(2)}, u32[]{:S(2)}) async-start(f32[4,2,32,4096]{3,2,1,0:T(8,128)} %cut_rows.7), calls=%async_computation.7 | async-start | bytes 8388608 | tf_op jit(solution)/shard_map/all_to_all | solution.py:786
  425.3 46.7 %collective-permute-start.14 = (f32[8,256,128]{2,1,0:T(8,128)}, f32[8,256,128]{2,1,0:T(8,128)}, u32[]{:S(2)}, u32[]{:S(2)}) collective-permute-start(f32[8,256,128]{2,1,0:T(8,128)} %pad_maximum_fusion.6), channel_id=1, source_target_pairs={{0,2},{2,0},{4,6},{6,4},{1,3},{3,1},{5,7},{7,5},{8,10},{10,8},{12,... | collective-permute-start | bytes 3145736 | tf_op jit(solution)/shard_map/ppermute | solution.py:755
  425.3 40.2 %collective-permute-start.15 = (f32[4,256,128]{2,1,0:T(8,128)S(1)}, f32[4,256,128]{2,1,0:T(8,128)S(1)}, u32[]{:S(2)}, u32[]{:S(2)}) collective-permute-start(f32[4,256,128]{2,1,0:T(8,128)S(1)} %copy-done.20), channel_id=1, source_target_pairs={{0,4},{2,6},{4,0},{6,2},{1,5},{3,7},{5,1},{7,3},{8,12},{10,14},{12... | collective-permute-start | bytes 1572872 | tf_op jit(solution)/shard_map/ppermute | solution.py:755
  429.5 40.3 %collective-permute-start.16 = (f32[4,256,128]{2,1,0:T(8,128)}, f32[4,256,128]{2,1,0:T(8,128)S(1)}, u32[]{:S(2)}, u32[]{:S(2)}) collective-permute-start(f32[4,256,128]{2,1,0:T(8,128)} %slice_select_fusion.4), channel_id=1, source_target_pairs={{0,4},{2,6},{4,0},{6,2},{1,5},{3,7},{5,1},{7,3},{8,12},{10,14},{12... | collective-permute-start | bytes 1572872 | tf_op jit(solution)/shard_map/ppermute | solution.py:755
  474.9 54.4 %all-to-all-start.8 = ((f32[8,8,128,128]{3,2,1,0:T(8,128)}), f32[8,8,128,128]{3,2,1,0:T(8,128)}, u32[]{:S(2)}, u32[]{:S(2)}) async-start(f32[8,8,128,128]{3,2,1,0:T(8,128)} %row_backward.4), calls=%async_computation.8 | async-start | bytes 8388608 | tf_op jit(solution)/shard_map/all_to_all | solution.py:786
  480.0 41.4 %collective-permute-start.17 = (f32[8,256,128]{2,1,0:T(8,128)}, f32[8,256,128]{2,1,0:T(8,128)}, u32[]{:S(2)}, u32[]{:S(2)}) collective-permute-start(f32[8,256,128]{2,1,0:T(8,128)} %pad_maximum_fusion.7), channel_id=1, source_target_pairs={{0,2},{2,0},{4,6},{6,4},{1,3},{3,1},{5,7},{7,5},{8,10},{10,8},{12,... | collective-permute-start | bytes 3145736 | tf_op jit(solution)/shard_map/ppermute | solution.py:755
  482.8 38.5 %collective-permute-start.18 = (f32[4,256,128]{2,1,0:T(8,128)S(1)}, f32[4,256,128]{2,1,0:T(8,128)S(1)}, u32[]{:S(2)}, u32[]{:S(2)}) collective-permute-start(f32[4,256,128]{2,1,0:T(8,128)S(1)} %select_add_fusion.4), channel_id=1, source_target_pairs={{0,4},{2,6},{4,0},{6,2},{1,5},{3,7},{5,1},{7,3},{8,12},{10,14},{12... | collective-permute-start | bytes 1572872 | tf_op jit(solution)/shard_map/ppermute | solution.py:755
  529.2 53.7 %all-to-all-start.9 = ((f32[8,8,128,128]{3,2,1,0:T(8,128)}), f32[8,8,128,128]{3,2,1,0:T(8,128)}, u32[]{:S(2)}, u32[]{:S(2)}) async-start(f32[8,8,128,128]{3,2,1,0:T(8,128)} %row_backward.5), calls=%async_computation.9 | async-start | bytes 8388608 | tf_op jit(solution)/shard_map/all_to_all | solution.py:786
  533.8 38.8 %collective-permute-start.19 = (f32[8,256,128]{2,1,0:T(8,128)S(1)}, f32[8,256,128]{2,1,0:T(8,128)S(1)}, u32[]{:S(2)}, u32[]{:S(2)}) collective-permute-start(f32[8,256,128]{2,1,0:T(8,128)S(1)} %pad_maximum_fusion.8), channel_id=1, source_target_pairs={{0,2},{2,0},{4,6},{6,4},{1,3},{3,1},{5,7},{7,5},{8,10},{10,8},{12,... | collective-permute-start | bytes 3145736 | tf_op jit(solution)/shard_map/ppermute | solution.py:755
  582.9 53.7 %all-to-all-start.10 = ((f32[8,8,128,128]{3,2,1,0:T(8,128)}), f32[8,8,128,128]{3,2,1,0:T(8,128)}, u32[]{:S(2)}, u32[]{:S(2)}) async-start(f32[8,8,128,128]{3,2,1,0:T(8,128)} %row_backward.6), calls=%async_computation.10 | async-start | bytes 8388608 | tf_op jit(solution)/shard_map/all_to_all | solution.py:786
  623.5 18.0 %copy-start.26 = (f32[32,128]{1,0:T(8,128)S(1)}, f32[32,128]{1,0:T(8,128)}, u32[]{:S(2)}) copy-start(f32[32,128]{1,0:T(8,128)} %constant.102.clone) | copy-start | bytes 49156
  623.5 18.0 %copy-start.28 = (f32[32,128]{1,0:T(8,128)S(1)}, f32[32,128]{1,0:T(8,128)}, u32[]{:S(2)}) copy-start(f32[32,128]{1,0:T(8,128)} %constant.101.clone) | copy-start | bytes 49156
  623.5 18.0 %copy-start.30 = (f32[32,128]{1,0:T(8,128)S(1)}, f32[32,128]{1,0:T(8,128)}, u32[]{:S(2)}) copy-start(f32[32,128]{1,0:T(8,128)} %constant.100.clone) | copy-start | bytes 49156
  623.5 18.0 %copy-start.36 = (f32[4]{0:T(128)S(1)}, f32[4]{0:T(128)}, u32[]{:S(2)}) copy-start(f32[4]{0:T(128)} %copy-done.35) | copy-start | bytes 52
  623.5 18.0 %copy-start.38 = (f32[4]{0:T(128)S(1)}, f32[4]{0:T(128)}, u32[]{:S(2)}) copy-start(f32[4]{0:T(128)} %copy-done.37) | copy-start | bytes 52
  636.6 53.9 %all-to-all-start.11 = ((f32[8,8,128,128]{3,2,1,0:T(8,128)}), f32[8,8,128,128]{3,2,1,0:T(8,128)}, u32[]{:S(2)}, u32[]{:S(2)}) async-start(f32[8,8,128,128]{3,2,1,0:T(8,128)} %row_backward.7), calls=%async_computation.11 | async-start | bytes 8388608 | tf_op jit(solution)/shard_map/all_to_all | solution.py:786
  727.3 6.9 collective-permute-start.20
  746.0 65.1 %collective-permute-start.24 = (f32[2,32,4096]{2,1,0:T(8,128)}, f32[2,32,4096]{2,1,0:T(8,128)S(1)}, u32[]{:S(2)}, u32[]{:S(2)}) collective-permute-start(f32[2,32,4096]{2,1,0:T(8,128)} %get-tuple-element.128), channel_id=1, source_target_pairs={{0,8},{8,0},{16,24},{24,16},{1,9},{9,1},{17,25},{25,17},{2,10},{10... | collective-permute-start | bytes 3145736 | tf_op jit(solution)/shard_map/ppermute | solution.py:755
  759.1 52.0 %collective-permute-start.27 = (f32[2,32,4096]{2,1,0:T(8,128)}, f32[2,32,4096]{2,1,0:T(8,128)S(1)}, u32[]{:S(2)}, u32[]{:S(2)}) collective-permute-start(f32[2,32,4096]{2,1,0:T(8,128)} %get-tuple-element.132), channel_id=1, source_target_pairs={{0,8},{8,0},{16,24},{24,16},{1,9},{9,1},{17,25},{25,17},{2,10},{10... | collective-permute-start | bytes 3145736 | tf_op jit(solution)/shard_map/ppermute | solution.py:755
  759.3 37.7 %collective-permute-start.30 = (f32[4,2,1,4096]{3,2,1,0:T(1,128)S(1)}, f32[4,2,1,4096]{3,2,1,0:T(1,128)S(1)}, u32[]{:S(2)}, u32[]{:S(2)}) collective-permute-start(f32[4,2,1,4096]{3,2,1,0:T(1,128)S(1)} %get-tuple-element.141), channel_id=1, source_target_pairs={{0,8},{8,16},{16,24},{24,1},{1,9},{9,17},{17,25},{25,2},{2,10},{10... | collective-permute-start | bytes 393224 | tf_op jit(solution)/shard_map/ppermute | solution.py:894
  763.4 60.5 %collective-permute-start.28 = (f32[2,32,4096]{2,1,0:T(8,128)}, f32[2,32,4096]{2,1,0:T(8,128)S(1)}, u32[]{:S(2)}, u32[]{:S(2)}) collective-permute-start(f32[2,32,4096]{2,1,0:T(8,128)} %get-tuple-element.133), channel_id=1, source_target_pairs={{0,16},{8,24},{16,0},{24,8},{1,17},{9,25},{17,1},{25,9},{2,18},{10... | collective-permute-start | bytes 3145736 | tf_op jit(solution)/shard_map/ppermute | solution.py:755
  763.5 62.5 %collective-permute-start.29 = (f32[2,32,4096]{2,1,0:T(8,128)}, f32[2,32,4096]{2,1,0:T(8,128)}, u32[]{:S(2)}, u32[]{:S(2)}) collective-permute-start(f32[2,32,4096]{2,1,0:T(8,128)} %get-tuple-element.134), channel_id=1, source_target_pairs={{0,24},{8,16},{16,8},{24,0},{1,25},{9,17},{17,9},{25,1},{2,26},{10... | collective-permute-start | bytes 3145736 | tf_op jit(solution)/shard_map/ppermute | solution.py:755
  808.6 34.0 %collective-permute-start.31 = (f32[2,32,4096]{2,1,0:T(8,128)}, f32[2,32,4096]{2,1,0:T(8,128)}, u32[]{:S(2)}, u32[]{:S(2)}) collective-permute-start(f32[2,32,4096]{2,1,0:T(8,128)} %get-tuple-element.136), channel_id=1, source_target_pairs={{0,8},{8,0},{16,24},{24,16},{1,9},{9,1},{17,25},{25,17},{2,10},{10... | collective-permute-start | bytes 3145736 | tf_op jit(solution)/shard_map/ppermute | solution.py:755
  811.1 31.6 %collective-permute-start.32 = (f32[2,32,4096]{2,1,0:T(8,128)}, f32[2,32,4096]{2,1,0:T(8,128)}, u32[]{:S(2)}, u32[]{:S(2)}) collective-permute-start(f32[2,32,4096]{2,1,0:T(8,128)} %get-tuple-element.137), channel_id=1, source_target_pairs={{0,16},{8,24},{16,0},{24,8},{1,17},{9,25},{17,1},{25,9},{2,18},{10... | collective-permute-start | bytes 3145736 | tf_op jit(solution)/shard_map/ppermute | solution.py:755
  811.1 56.9 %copy-start.4 = (s32[3]{0:T(128)S(1)}, s32[3]{0:T(128)}, u32[]{:S(2)}) copy-start(s32[3]{0:T(128)} %pad_add_fusion.scal) | copy-start | bytes 40
  811.1 53.7 %collective-permute-start.33 = (f32[2,32,4096]{2,1,0:T(8,128)}, f32[2,32,4096]{2,1,0:T(8,128)}, u32[]{:S(2)}, u32[]{:S(2)}) collective-permute-start(f32[2,32,4096]{2,1,0:T(8,128)} %get-tuple-element.138), channel_id=1, source_target_pairs={{0,24},{8,16},{16,8},{24,0},{1,25},{9,17},{17,9},{25,1},{2,26},{10... | collective-permute-start | bytes 3145736 | tf_op jit(solution)/shard_map/ppermute | solution.py:755
  823.9 89.1 %collective-permute-start.21 = (f32[2,32,4096]{2,1,0:T(8,128)}, f32[2,32,4096]{2,1,0:T(8,128)S(1)}, u32[]{:S(2)}, u32[]{:S(2)}) collective-permute-start(f32[2,32,4096]{2,1,0:T(8,128)} %get-tuple-element.124), channel_id=1, source_target_pairs={{0,8},{8,0},{16,24},{24,16},{1,9},{9,1},{17,25},{25,17},{2,10},{10... | collective-permute-start | bytes 3145736 | tf_op jit(solution)/shard_map/ppermute | solution.py:755
  825.9 61.3 %collective-permute-start.25 = (f32[2,32,4096]{2,1,0:T(8,128)}, f32[2,32,4096]{2,1,0:T(8,128)S(1)}, u32[]{:S(2)}, u32[]{:S(2)}) collective-permute-start(f32[2,32,4096]{2,1,0:T(8,128)} %get-tuple-element.129), channel_id=1, source_target_pairs={{0,16},{8,24},{16,0},{24,8},{1,17},{9,25},{17,1},{25,9},{2,18},{10... | collective-permute-start | bytes 3145736 | tf_op jit(solution)/shard_map/ppermute | solution.py:755
  842.7 67.1 %collective-permute-start.26 = (f32[2,32,4096]{2,1,0:T(8,128)}, f32[2,32,4096]{2,1,0:T(8,128)S(1)}, u32[]{:S(2)}, u32[]{:S(2)}) collective-permute-start(f32[2,32,4096]{2,1,0:T(8,128)} %get-tuple-element.130), channel_id=1, source_target_pairs={{0,24},{8,16},{16,8},{24,0},{1,25},{9,17},{17,9},{25,1},{2,26},{10... | collective-permute-start | bytes 3145736 | tf_op jit(solution)/shard_map/ppermute | solution.py:755
  842.7 110.7 %collective-permute-start.22 = (f32[2,32,4096]{2,1,0:T(8,128)}, f32[2,32,4096]{2,1,0:T(8,128)S(1)}, u32[]{:S(2)}, u32[]{:S(2)}) collective-permute-start(f32[2,32,4096]{2,1,0:T(8,128)} %get-tuple-element.125), channel_id=1, source_target_pairs={{0,16},{8,24},{16,0},{24,8},{1,17},{9,25},{17,1},{25,9},{2,18},{10... | collective-permute-start | bytes 3145736 | tf_op jit(solution)/shard_map/ppermute | solution.py:755
  864.8 88.6 %collective-permute-start.23 = (f32[2,32,4096]{2,1,0:T(8,128)}, f32[2,32,4096]{2,1,0:T(8,128)S(1)}, u32[]{:S(2)}, u32[]{:S(2)}) collective-permute-start(f32[2,32,4096]{2,1,0:T(8,128)} %get-tuple-element.126), channel_id=1, source_target_pairs={{0,24},{8,16},{16,8},{24,0},{1,25},{9,17},{17,9},{25,1},{2,26},{10... | collective-permute-start | bytes 3145736 | tf_op jit(solution)/shard_map/ppermute | solution.py:755
  873.8 36.0 %copy-start = (f32[2,32,4096]{2,1,0:T(8,128)S(1)}, f32[2,32,4096]{2,1,0:T(8,128)}, u32[]{:S(2)}) copy-start(f32[2,32,4096]{2,1,0:T(8,128)} %get-tuple-element.127.refs_0_) | copy-start | bytes 3145732
  909.8 43.6 %copy-start.2 = (f32[2,32,4096]{2,1,0:T(8,128)S(1)}, f32[2,32,4096]{2,1,0:T(8,128)}, u32[]{:S(2)}) copy-start(f32[2,32,4096]{2,1,0:T(8,128)} %get-tuple-element.123.refs_0_) | copy-start | bytes 3145732
  (23 other events, 105.6 us)

commit v4 on v3

--- a/solution.py
+++ b/solution.py
@@ -354,18 +354,19 @@
     )(field, *fixed)
 
 
-def cut_rows(plan, field, part, parts):
-    rows, width = plan.piece // parts, field.shape[-1]
+def cut_rows(plan, field, first, count):
+    width = field.shape[-1]
+    rows, units = plan.piece // plan.units, plan.units
 
     def kernel(x_ref, out_ref):
         out_ref[0] = x_ref[...]
 
     return pl.pallas_call(
         kernel,
-        grid=(plan.planes,),
-        in_specs=[pl.BlockSpec((2, rows, width), lambda p: (0, p * parts + part, 0))],
-        out_specs=pl.BlockSpec((1, 2, rows, width), lambda p: (p, 0, 0, 0)),
-        out_shape=jax.ShapeDtypeStruct((plan.planes, 2, rows, width), f32),
+        grid=(plan.planes, count),
+        in_specs=[pl.BlockSpec((2, rows, width), lambda p, u: (0, p * units + first + u, 0))],
+        out_specs=pl.BlockSpec((1, 2, rows, width), lambda p, u: (p, 0, u, 0)),
+        out_shape=jax.ShapeDtypeStruct((plan.planes, 2, rows * count, width), f32),
         compiler_params=params(),
         cost_estimate=pl.CostEstimate(flops=0, bytes_accessed=9 * 10**6, transcendentals=0),
         name="cut_rows",
@@ -724,7 +725,7 @@
         ),
         out_shape=jax.ShapeDtypeStruct((2, plan.rows_dev, width), f32),
         input_output_aliases={count + 1: 0} if given else {},
-        compiler_params=pltpu.CompilerParams(vmem_limit_bytes=8 * 1024 * 1024),
+        compiler_params=params(),
         cost_estimate=pl.CostEstimate(flops=0, bytes_accessed=9 * 10**6, transcendentals=0),
         name="place_rows",
     )(scalars, *pieces, *given)
@@ -742,6 +743,8 @@
         self.chunks = [LANES] * tiles
         self.starts = [sum(self.chunks[:i]) for i in range(len(self.chunks))]
         self.piece = self.rows_dev // depth
+        self.units = max(1, min(8, self.piece // 8))
+        self.cuts = [1, 2, 3, 2] if self.units == 8 else [1] * self.units
         self.slab_tiles = 2 * self.rows_dev // LANES
 
     def place_of(self, tile):
@@ -811,8 +814,7 @@
     depths = ordered[jnp.bitwise_xor(jnp.arange(depth, dtype=jnp.int32), d)]
 
     own = field[:, 0]
-    quarters = max(1, min(4, plan.piece // 8))
-    early = cut_rows(plan, own, 0, quarters)
+    early = cut_rows(plan, own, 0, plan.cuts[0])
     own, early = lax.optimization_barrier((own, early))
     early, depths = lax.optimization_barrier((early, depths))
     held = [exchanged(early, "depth")]
@@ -854,7 +856,7 @@
     stages += [sum_stage(gather_step, step) for step in reversed(halvings)]
     stages += [backward_stage]
 
-    queue = list(sent) + [None] * (quarters - 1)
+    queue = list(sent) + [None] * (len(plan.cuts) - 1)
     state = [None] * count
     before, back = [held[0]], []
     slot = 0
@@ -863,7 +865,7 @@
         if queue:
             value = queue.pop(0)
             if value is None:
-                value = cut_rows(plan, field[:, 0], len(held), quarters)
+                value = cut_rows(plan, field[:, 0], sum(plan.cuts[: len(held)]), plan.cuts[len(held)])
                 held.append(exchanged(after(value, *others), "depth"))
                 before.append(held[-1])
             else:
@@ -883,7 +885,7 @@
             before += [high, low]
         slot += 1
 
-    held = jnp.stack(held, axis=2).reshape(depth, 2, plan.piece, length)
+    held = jnp.concatenate(held, axis=2)
     cos, sin = chirp(depths[:, None, None], column_freqs[None], length)
     transfer = jnp.stack([cos, sin], axis=1) * (1.0 / length)
     moved = step_pass(plan, back, held, tables, transfer)
@@ -894,9 +896,9 @@
     above = lax.ppermute(moved[:, :, -1:], all_axes, downward)
     below = lax.ppermute(moved[:, :, :1], all_axes, [(b, a) for a, b in downward])
     tiles = plan.piece // 8
-    steps = max(1, tiles // 4)
+    first = max(1, tiles // 4)
     result = None
-    for begin in range(0, tiles, steps):
+    for begin, steps in ((0, first), (first, tiles - first)):
         parts = shrink_pass(plan, ends, moved, above, below, begin, steps)
         parts = [parts[0]] + [swapped(parts[s], "depth", depth, s) for s in range(1, depth)]
         result = place_rows(plan, ends, parts, begin * 8, result)

time: 968 us -> 986 us (1.019)
  waiting for transfers between devices: 353 us -> 385 us
  starting transfers between devices: 113 us -> 98.7 us
    ppermute x1, waiting for transfers between devices: 32 us -> 132 us  [per_device(): above = lax.ppermute(moved[:, :, -1:], all_axes, downward)]
    ppermute x32 -> x26, waiting for transfers between devices: 188 us -> 128 us  [swapped(): return lax.ppermute(value, axes, [(i, i ^ step) for i in range(size)])]
    ppermute x32 -> x26, starting transfers between devices: 49.4 us -> 36.8 us  [swapped(): return lax.ppermute(value, axes, [(i, i ^ step) for i in range(size)])]
    concatenate x0 -> x1, other arithmetic: none -> 11.1 us  [per_device(): held = jnp.concatenate(held, axis=2)]
    pallas_call x4 -> x2, Pallas kernels: 44.7 us -> 36.5 us  [shrink_pass(): pl.pallas_call(kernel, grid_spec=pltpu.PrefetchScalarGridSpec(num_scalar_...]
  transfers between devices with their start and end apart: 46 -> 40, of which waited for: 25 -> 20; matrix products, arithmetic and copies ran while one was open for 5% -> 5% of each run, Pallas kernels for 40% -> 37%
where the time goes in v4:
time: 986 us; the launch traced here: 975 us
  Pallas kernels  429 us (44%)
  waiting for transfers between devices  385 us (39%)
  starting transfers between devices  98.7 us (10%)
  other arithmetic  48.3 us (5%)
  local copies, waits for them, and re-layouts  11.9 us (1%)
    pallas_call x4, Pallas kernels, row_backward(): pl.pallas_call(kernel, grid_spec=pltpu.PrefetchScalarGridSpec(num_scalar_...  144 us
    ppermute x1, waiting for transfers between devices, per_device(): above = lax.ppermute(moved[:, :, -1:], all_axes, downward)  132 us
    ppermute x26, waiting for transfers between devices, swapped(): return lax.ppermute(value, axes, [(i, i ^ step) for i in range(size)])  128 us
    all_to_all x12, waiting for transfers between devices, exchanged(): return lax.all_to_all(value, axes, 0, 0, tiled=True)  121 us
    pallas_call x4, Pallas kernels, row_forward(): pl.pallas_call(kernel, grid_spec=pltpu.PrefetchScalarGridSpec(num_scalar_...  105 us
    all_to_all x12, starting transfers between devices, exchanged(): return lax.all_to_all(value, axes, 0, 0, tiled=True)  56.8 us
    ppermute x26, starting transfers between devices, swapped(): return lax.ppermute(value, axes, [(i, i ^ step) for i in range(size)])  36.8 us
    pallas_call x2, Pallas kernels, shrink_pass(): pl.pallas_call(kernel, grid_spec=pltpu.PrefetchScalarGridSpec(num_scalar_...  36.5 us
  transfers between devices with their start and end apart: 40, of which 20 were waited for; matrix products, arithmetic and copies ran while one was open for 5% of the time, Pallas kernels for 37%

profile of v4, /device:TPU:0, one launch (start us, length us, event | category | flops | bytes accessed | tf_op | source)
XLA Modules:
  0.0 975.0 jit_solution(2433586142709068320)
XLA Ops:
  0.0 3.9 collective-permute-start.2
  5.2 3.8 cut_rows.4
  9.8 1.9 pad_maximum_fusion.11
  12.3 4.2 all-to-all-start
  16.5 33.4 %column_pass.1 = (f32[8,2,512,128]{3,2,1,0:T(8,128)}, f32[8,2,512,128]{3,2,1,0:T(8,128)}, f32[8,2,512,128]{3,2,1,0:T(8,128)}, f32[8,2,512,128]{3,2,1,0:T(8,128)}) custom-call(f32[2,512,4096]{2,1,0:T(8,128)} %bitcast.28, bf16[768,256]{1,0:T(8,128)(2,1)} %constant.31.clone.fwd.refs_5_, bf16[768,256]{1,0:T(8,128)(2,1)} %constant.32.clone.inv.refs_6_, ...), custom_call_target="tpu_custom_call" | custom-call | flops 12999999488 | bytes 34000000 | tf_op jit(solution)/shard_map/column_pass/pallas_call | solution.py:344
  52.5 4.5 all-to-all-start.1
  57.1 33.2 %slot_matrices.1 = (bf16[16,256,2048]{2,1,0:T(8,128)(2,1)}, bf16[16,256,2048]{2,1,0:T(8,128)(2,1)}) custom-call(f32[16,256,256]{2,1,0:T(8,128)} %constant.108.clone.b_ref, f32[16,8,256]{2,1,0:T(8,128)} %copy.27.w_ref), custom_call_target="tpu_custom_call" | custom-call | flops 25999998976 | bytes 34000000 | tf_op jit(solution)/shard_map/slot_matrices/pallas_call | solution.py:396
  90.2 16.0 %all-to-all-done.1.x_ref = f32[8,2,512,128]{3,2,1,0:T(8,128)} async-done(((f32[8,2,512,128]{3,2,1,0:T(8,128)}), f32[8,2,512,128]{3,2,1,0:T(8,128)}, u32[]{:S(2)}, u32[]{:S(2)}) %all-to-all-start.1) | async-done | bytes 4194336 | tf_op jit(solution)/shard_map/all_to_all | solution.py:789
  106.2 5.0 all-to-all-start.2
  117.4 26.3 %row_forward.4 = f32[16,256,128]{2,1,0:T(8,128)} custom-call(f32[4,16]{1,0:T(4,128)} %pad_maximum_fusion.10.phase, f32[8,2,512,128]{3,2,1,0:T(8,128)} %all-to-all-done.1.x_ref, f32[2,512,128]{2,1,0:T(8,128)} %get-tuple-element.140.h_ref, bf16[16,256,2048]{2,1,0:T(8,128)(2,1)} %get-tuple-element.76.wh, bf16[16,256,2048]{2,1,0:T(8,128)(2,1)} %get-tuple-element.77.wl), custom_call_target="tpu_custom_call" | custom-call | flops 12999999488 | bytes 60000000 | tf_op jit(solution)/shard_map/row_forward/pallas_call | solution.py:459
  143.7 16.6 %all-to-all-done.2.x_ref = f32[8,2,512,128]{3,2,1,0:T(8,128)} async-done(((f32[8,2,512,128]{3,2,1,0:T(8,128)}), f32[8,2,512,128]{3,2,1,0:T(8,128)}, u32[]{:S(2)}, u32[]{:S(2)}) %all-to-all-start.2) | async-done | bytes 4194336 | tf_op jit(solution)/shard_map/all_to_all | solution.py:789
  160.3 4.6 all-to-all-start.3
  166.7 26.3 %row_forward.5 = f32[16,256,128]{2,1,0:T(8,128)} custom-call(f32[4,16]{1,0:T(4,128)} %pad_maximum_fusion.10.phase, f32[8,2,512,128]{3,2,1,0:T(8,128)} %all-to-all-done.2.x_ref, f32[2,512,128]{2,1,0:T(8,128)} %get-tuple-element.139.h_ref, bf16[16,256,2048]{2,1,0:T(8,128)(2,1)} %get-tuple-element.76.wh, bf16[16,256,2048]{2,1,0:T(8,128)(2,1)} %get-tuple-element.77.wl), custom_call_target="tpu_custom_call" | custom-call | flops 12999999488 | bytes 60000000 | tf_op jit(solution)/shard_map/row_forward/pallas_call | solution.py:459
  194.4 19.6 %all-to-all-done.3.x_ref = f32[8,2,512,128]{3,2,1,0:T(8,128)} async-done(((f32[8,2,512,128]{3,2,1,0:T(8,128)}), f32[8,2,512,128]{3,2,1,0:T(8,128)}, u32[]{:S(2)}, u32[]{:S(2)}) %all-to-all-start.3) | async-done | bytes 4194336 | tf_op jit(solution)/shard_map/all_to_all | solution.py:789
  214.0 4.7 all-to-all-start.4
  218.8 6.8 cut_rows.5
  227.6 2.6 collective-permute-start.5
  231.7 26.3 %row_forward.6 = f32[16,256,128]{2,1,0:T(8,128)} custom-call(f32[4,16]{1,0:T(4,128)} %pad_maximum_fusion.10.phase, f32[8,2,512,128]{3,2,1,0:T(8,128)} %all-to-all-done.3.x_ref, f32[2,512,128]{2,1,0:T(8,128)} %get-tuple-element.138.h_ref, bf16[16,256,2048]{2,1,0:T(8,128)(2,1)} %get-tuple-element.76.wh, bf16[16,256,2048]{2,1,0:T(8,128)(2,1)} %get-tuple-element.77.wl), custom_call_target="tpu_custom_call" | custom-call | flops 12999999488 | bytes 60000000 | tf_op jit(solution)/shard_map/row_forward/pallas_call | solution.py:459
  258.9 6.9 collective-permute-done.6
  267.9 4.8 all-to-all-start.5
  272.8 9.5 cut_rows.6
  284.2 2.6 collective-permute-start.7
  288.7 26.3 %row_forward.7 = f32[16,256,128]{2,1,0:T(8,128)} custom-call(f32[4,16]{1,0:T(4,128)} %pad_maximum_fusion.10.phase, f32[8,2,512,128]{3,2,1,0:T(8,128)} %all-to-all-done.4.x_ref, f32[2,512,128]{2,1,0:T(8,128)} %get-tuple-element.137.h_ref, bf16[16,256,2048]{2,1,0:T(8,128)(2,1)} %get-tuple-element.76.wh, bf16[16,256,2048]{2,1,0:T(8,128)(2,1)} %get-tuple-element.77.wl), custom_call_target="tpu_custom_call" | custom-call | flops 12999999488 | bytes 60000000 | tf_op jit(solution)/shard_map/row_forward/pallas_call | solution.py:459
  315.0 16.5 %collective-permute-done.8 = f32[4,256,128]{2,1,0:T(8,128)} collective-permute-done((f32[4,256,128]{2,1,0:T(8,128)}, f32[4,256,128]{2,1,0:T(8,128)}, u32[]{:S(2)}, u32[]{:S(2)}) %collective-permute-start.8) | collective-permute-done | bytes 524320 | tf_op jit(solution)/shard_map/ppermute | solution.py:758
  331.5 1.9 select_add_fusion.6
  338.7 5.5 all-to-all-start.6
  344.3 3.0 collective-permute-start.10
  348.2 6.6 cut_rows.7
  354.9 1.8 collective-permute-start.13
  356.7 13.8 %collective-permute-done.11 = f32[4,256,128]{2,1,0:T(8,128)} collective-permute-done((f32[4,256,128]{2,1,0:T(8,128)}, f32[4,256,128]{2,1,0:T(8,128)}, u32[]{:S(2)}, u32[]{:S(2)}) %collective-permute-start.11) | collective-permute-done | bytes 524320 | tf_op jit(solution)/shard_map/ppermute | solution.py:758
  372.8 17.8 %collective-permute-done.12 = f32[4,256,128]{2,1,0:T(8,128)} collective-permute-done((f32[4,256,128]{2,1,0:T(8,128)}, f32[4,256,128]{2,1,0:T(8,128)}, u32[]{:S(2)}, u32[]{:S(2)}) %collective-permute-start.12) | collective-permute-done | bytes 524320 | tf_op jit(solution)/shard_map/ppermute | solution.py:758
  390.7 1.9 select_add_fusion.5
  395.9 18.4 %collective-permute-done.13 = f32[8,256,128]{2,1,0:T(8,128)S(1)} collective-permute-done((f32[8,256,128]{2,1,0:T(8,128)}, f32[8,256,128]{2,1,0:T(8,128)S(1)}, u32[]{:S(2)}, u32[]{:S(2)}) %collective-permute-start.13) | collective-permute-done | bytes 1048608 | tf_op jit(solution)/shard_map/ppermute | solution.py:758
  414.4 5.0 all-to-all-start.7
  421.1 3.4 collective-permute-start.15
  424.5 36.0 %row_backward.4 = f32[8,8,128,128]{3,2,1,0:T(8,128)} custom-call(f32[4,16]{1,0:T(4,128)} %pad_maximum_fusion.10.phase, f32[16,256,128]{2,1,0:T(8,128)} %pad_maximum_fusion.1.m_ref, bf16[16,256,2048]{2,1,0:T(8,128)(2,1)} %get-tuple-element.76.wh, bf16[16,256,2048]{2,1,0:T(8,128)(2,1)} %get-tuple-element.77.wl), custom_call_target="tpu_custom_call" | custom-call | flops 12999999488 | bytes 60000000 | tf_op jit(solution)/shard_map/row_backward/pallas_call | solution.py:526
  461.6 7.8 collective-permute-done.16
  472.5 4.5 all-to-all-start.8
  477.7 2.4 collective-permute-start.18
  480.1 36.0 %row_backward.5 = f32[8,8,128,128]{3,2,1,0:T(8,128)} custom-call(f32[4,16]{1,0:T(4,128)} %pad_maximum_fusion.10.phase, f32[16,256,128]{2,1,0:T(8,128)} %pad_maximum_fusion.2.m_ref, bf16[16,256,2048]{2,1,0:T(8,128)(2,1)} %get-tuple-element.76.wh, bf16[16,256,2048]{2,1,0:T(8,128)(2,1)} %get-tuple-element.77.wl), custom_call_target="tpu_custom_call" | custom-call | flops 12999999488 | bytes 60000000 | tf_op jit(solution)/shard_map/row_backward/pallas_call | solution.py:526
  519.1 7.0 all-to-all-done.8.refs_0_
  526.2 4.5 all-to-all-start.9
  531.4 36.0 %row_backward.6 = f32[8,8,128,128]{3,2,1,0:T(8,128)} custom-call(f32[4,16]{1,0:T(4,128)} %pad_maximum_fusion.10.phase, f32[16,256,128]{2,1,0:T(8,128)} %pad_maximum_fusion.3.m_ref, bf16[16,256,2048]{2,1,0:T(8,128)(2,1)} %get-tuple-element.76.wh, bf16[16,256,2048]{2,1,0:T(8,128)(2,1)} %get-tuple-element.77.wl), custom_call_target="tpu_custom_call" | custom-call | flops 12999999488 | bytes 60000000 | tf_op jit(solution)/shard_map/row_backward/pallas_call | solution.py:526
  569.1 10.8 %all-to-all-done.9.refs_1_ = f32[8,8,128,128]{3,2,1,0:T(8,128)} async-done(((f32[8,8,128,128]{3,2,1,0:T(8,128)}), f32[8,8,128,128]{3,2,1,0:T(8,128)}, u32[]{:S(2)}, u32[]{:S(2)}) %all-to-all-start.9) | async-done | bytes 4194336 | tf_op jit(solution)/shard_map/all_to_all | solution.py:789
  579.9 4.6 all-to-all-start.10
  584.5 36.0 %row_backward.7 = f32[8,8,128,128]{3,2,1,0:T(8,128)} custom-call(f32[4,16]{1,0:T(4,128)} %pad_maximum_fusion.10.phase, f32[16,256,128]{2,1,0:T(8,128)} %pad_maximum_fusion.4.m_ref, bf16[16,256,2048]{2,1,0:T(8,128)(2,1)} %get-tuple-element.76.wh, bf16[16,256,2048]{2,1,0:T(8,128)(2,1)} %get-tuple-element.77.wl), custom_call_target="tpu_custom_call" | custom-call | flops 12999999488 | bytes 60000000 | tf_op jit(solution)/shard_map/row_backward/pallas_call | solution.py:526
  620.5 13.1 %all-to-all-done.10.refs_2_ = f32[8,8,128,128]{3,2,1,0:T(8,128)} async-done(((f32[8,8,128,128]{3,2,1,0:T(8,128)}), f32[8,8,128,128]{3,2,1,0:T(8,128)}, u32[]{:S(2)}, u32[]{:S(2)}) %all-to-all-start.10) | async-done | bytes 4194336 | tf_op jit(solution)/shard_map/all_to_all | solution.py:789
  633.6 4.8 all-to-all-start.11
  639.5 11.1 %pad_maximum_fusion.refs_4_ = f32[4,2,128,4096]{3,2,1,0:T(8,128)} fusion(f32[4,2,32,4096]{3,2,1,0:T(8,128)} %all-to-all-done.7, f32[4,2,48,4096]{3,2,1,0:T(8,128)} %all-to-all-done.6, f32[4,2,32,4096]{3,2,1,0:T(8,128)} %all-to-all-done.5, f32[4,2,16,4096]{3,2,1,0:T(8,128)S(1)} %copy-done.1), kind=kLoop, calls=%fused_computation.1 | loop fusion | flops 12582912 | bytes 33554432 | tf_op jit(solution)/shard_map/concatenate | solution.py:888
  650.5 37.0 %all-to-all-done.11.refs_3_ = f32[8,8,128,128]{3,2,1,0:T(8,128)} async-done(((f32[8,8,128,128]{3,2,1,0:T(8,128)}), f32[8,8,128,128]{3,2,1,0:T(8,128)}, u32[]{:S(2)}, u32[]{:S(2)}) %all-to-all-start.11) | async-done | bytes 4194336 | tf_op jit(solution)/shard_map/all_to_all | solution.py:789
  687.5 35.0 %step_pass.1.cur.nxt.up = f32[4,2,128,4096]{3,2,1,0:T(8,128)} custom-call(f32[8,8,128,128]{3,2,1,0:T(8,128)} %all-to-all-done.8.refs_0_, f32[8,8,128,128]{3,2,1,0:T(8,128)} %all-to-all-done.9.refs_1_, f32[8,8,128,128]{3,2,1,0:T(8,128)} %all-to-all-done.10.refs_2_, f32[8,8,128,128]{3,2,1,0:T(8,128)} %all-to-all-done.11.refs_3_, ...), custom_call_target="tpu_custom_call" | custom-call | flops 12999999488 | bytes 51000000 | tf_op jit(solution)/shard_map/step_pass/pallas_call | solution.py:575
  722.5 1.7 fusion.23
  726.1 5.0 collective-permute-done.20.down
  731.8 25.6 %shrink_pass.2 = (f32[2,96,4096]{2,1,0:T(8,128)}, f32[2,96,4096]{2,1,0:T(8,128)}, f32[2,96,4096]{2,1,0:T(8,128)}, f32[2,96,4096]{2,1,0:T(8,128)}) custom-call(s32[3]{0:T(128)} %pad_add_fusion.scal, f32[4,2,128,4096]{3,2,1,0:T(8,128)} %step_pass.1.cur.nxt.up, f32[4,2,128,4096]{3,2,1,0:T(8,128)} %step_pass.1.cur.nxt.up, ...), custom_call_target="tpu_custom_call" | custom-call | flops 100000000 | bytes 9000000 | tf_op jit(solution)/shard_map/shrink_pass/pallas_call | solution.py:674
  757.4 1.9 collective-permute-start.21
  760.9 3.8 collective-permute-start.24
  764.7 131.8 %collective-permute-done.24.up = f32[4,2,1,4096]{3,2,1,0:T(1,128)S(1)} collective-permute-done((f32[4,2,1,4096]{3,2,1,0:T(1,128)S(1)}, f32[4,2,1,4096]{3,2,1,0:T(1,128)S(1)}, u32[]{:S(2)}, u32[]{:S(2)}) %collective-permute-start.24) | collective-permute-done | bytes 131104 | tf_op jit(solution)/shard_map/ppermute | solution.py:896
  897.1 10.9 %shrink_pass.3 = (f32[2,32,4096]{2,1,0:T(8,128)}, f32[2,32,4096]{2,1,0:T(8,128)}, f32[2,32,4096]{2,1,0:T(8,128)}, f32[2,32,4096]{2,1,0:T(8,128)}) custom-call(s32[3]{0:T(128)} %pad_add_fusion.scal, f32[4,2,128,4096]{3,2,1,0:T(8,128)} %step_pass.1.cur.nxt.up, f32[4,2,128,4096]{3,2,1,0:T(8,128)} %step_pass.1.cur.nxt.up, f32[4,2,1,4096]{3,2,1,0:T(1,128)} %copy-done.20, ...), custom_call_target="tpu_custom_call" | custom-call | flops 100000000 | bytes 9000000 | tf_op jit(solution)/shard_map/shrink_pass/pallas_call | solution.py:674
  908.0 2.5 collective-permute-start.25
  911.6 21.6 %collective-permute-done.25.refs_1_ = f32[2,32,4096]{2,1,0:T(8,128)} collective-permute-done((f32[2,32,4096]{2,1,0:T(8,128)}, f32[2,32,4096]{2,1,0:T(8,128)}, u32[]{:S(2)}, u32[]{:S(2)}) %collective-permute-start.25) | collective-permute-done | bytes 1048608 | tf_op jit(solution)/shard_map/ppermute | solution.py:758
  933.2 1.7 collective-permute-start.27
  935.0 23.0 %collective-permute-done.27.refs_3_ = f32[2,32,4096]{2,1,0:T(8,128)} collective-permute-done((f32[2,32,4096]{2,1,0:T(8,128)}, f32[2,32,4096]{2,1,0:T(8,128)}, u32[]{:S(2)}, u32[]{:S(2)}) %collective-permute-start.27) | collective-permute-done | bytes 1048608 | tf_op jit(solution)/shard_map/ppermute | solution.py:758
  958.0 4.8 place_rows.2.refs_4_
  964.5 10.1 %place_rows.3 = f32[2,512,4096]{2,1,0:T(8,128)} custom-call(s32[3]{0:T(128)} %pad_add_fusion.scal, f32[2,96,4096]{2,1,0:T(8,128)} %get-tuple-element.115.refs_0_, f32[2,96,4096]{2,1,0:T(8,128)} %copy-done.15, f32[2,96,4096]{2,1,0:T(8,128)} %collective-permute-done.22.refs_2_, ...), custom_call_target="tpu_custom_call", output_to_operand_aliasing={{}: (5, {})} | custom-call | bytes 9000000 | tf_op jit(solution)/shard_map/place_rows/pallas_call | solution.py:716
  (165 shorter events, 56.6 us)
Async XLA Ops:
  0.0 9.8 %collective-permute-start.2 = (f32[1]{0:T(128)}, f32[1]{0:T(128)}, u32[]{:S(2)}, u32[]{:S(2)}) collective-permute-start(f32[1]{0:T(128)} %param.23), channel_id=1, source_target_pairs={{0,24},{8,16},{16,8},{24,0},{1,25},{9,17},{17,9},{25,1},{2,26},{10... | collective-permute-start | bytes 20 | tf_op jit(solution)/shard_map/ppermute | solution.py:758
  3.9 5.9 collective-permute-start.1
  4.4 5.4 collective-permute-start
  5.2 3.9 copy-start.21
  12.3 38.9 %all-to-all-start = ((f32[4,2,16,4096]{3,2,1,0:T(8,128)}), f32[4,2,16,4096]{3,2,1,0:T(8,128)S(1)}, u32[]{:S(2)}, u32[]{:S(2)}) async-start(f32[4,2,16,4096]{3,2,1,0:T(8,128)} %cut_rows.4), calls=%async_computation | async-start | bytes 4194304 | tf_op jit(solution)/shard_map/all_to_all | solution.py:789
  16.5 33.4 %copy-start.29 = (f32[16,256]{1,0:T(8,128)S(1)}, f32[16,256]{1,0:T(8,128)}, u32[]{:S(2)}) copy-start(f32[16,256]{1,0:T(8,128)} %constant.120) | copy-start | bytes 49156
  16.5 33.4 %copy-start.30 = (f32[16,256]{1,0:T(8,128)S(1)}, f32[16,256]{1,0:T(8,128)}, u32[]{:S(2)}) copy-start(f32[16,256]{1,0:T(8,128)} %constant.119) | copy-start | bytes 49156
  16.5 33.5 %copy-start.31 = (f32[16,256]{1,0:T(8,128)S(1)}, f32[16,256]{1,0:T(8,128)}, u32[]{:S(2)}) copy-start(f32[16,256]{1,0:T(8,128)} %constant.118) | copy-start | bytes 49156
  16.5 33.5 %copy-start.32 = (f32[16,256]{1,0:T(8,128)S(1)}, f32[16,256]{1,0:T(8,128)}, u32[]{:S(2)}) copy-start(f32[16,256]{1,0:T(8,128)} %constant.117) | copy-start | bytes 49156
  52.5 53.7 %all-to-all-start.1 = ((f32[8,2,512,128]{3,2,1,0:T(8,128)}), f32[8,2,512,128]{3,2,1,0:T(8,128)}, u32[]{:S(2)}, u32[]{:S(2)}) async-start(f32[8,2,512,128]{3,2,1,0:T(8,128)} %get-tuple-element.73), calls=%async_computation.1 | async-start | bytes 8388608 | tf_op jit(solution)/shard_map/all_to_all | solution.py:789
  106.2 54.1 %all-to-all-start.2 = ((f32[8,2,512,128]{3,2,1,0:T(8,128)}), f32[8,2,512,128]{3,2,1,0:T(8,128)}, u32[]{:S(2)}, u32[]{:S(2)}) async-start(f32[8,2,512,128]{3,2,1,0:T(8,128)} %get-tuple-element.80), calls=%async_computation.2 | async-start | bytes 8388608 | tf_op jit(solution)/shard_map/all_to_all | solution.py:789
  113.0 2.8 collective-permute-start.3
  143.7 21.2 %copy-start.6 = (f32[16,256,128]{2,1,0:T(8,128)S(1)}, f32[16,256,128]{2,1,0:T(8,128)}, u32[]{:S(2)}) copy-start(f32[16,256,128]{2,1,0:T(8,128)} %row_forward.4) | copy-start | bytes 6291460
  160.3 53.7 %all-to-all-start.3 = ((f32[8,2,512,128]{3,2,1,0:T(8,128)}), f32[8,2,512,128]{3,2,1,0:T(8,128)}, u32[]{:S(2)}, u32[]{:S(2)}) async-start(f32[8,2,512,128]{3,2,1,0:T(8,128)} %get-tuple-element.83), calls=%async_computation.3 | async-start | bytes 8388608 | tf_op jit(solution)/shard_map/all_to_all | solution.py:789
  165.1 28.0 %collective-permute-start.4 = (f32[8,256,128]{2,1,0:T(8,128)S(1)}, f32[8,256,128]{2,1,0:T(8,128)}, u32[]{:S(2)}, u32[]{:S(2)}) collective-permute-start(f32[8,256,128]{2,1,0:T(8,128)S(1)} %slice_select_fusion.3), channel_id=1, source_target_pairs={{0,2},{2,0},{4,6},{6,4},{1,3},{3,1},{5,7},{7,5},{8,10},{10,8},{12,... | collective-permute-start | bytes 3145736 | tf_op jit(solution)/shard_map/ppermute | solution.py:758
  214.0 53.9 %all-to-all-start.4 = ((f32[8,2,512,128]{3,2,1,0:T(8,128)}), f32[8,2,512,128]{3,2,1,0:T(8,128)}, u32[]{:S(2)}, u32[]{:S(2)}) async-start(f32[8,2,512,128]{3,2,1,0:T(8,128)} %get-tuple-element.87), calls=%async_computation.4 | async-start | bytes 8388608 | tf_op jit(solution)/shard_map/all_to_all | solution.py:789
  218.8 6.8 copy-start.5
  227.6 30.4 %collective-permute-start.5 = (f32[4,256,128]{2,1,0:T(8,128)}, f32[4,256,128]{2,1,0:T(8,128)S(1)}, u32[]{:S(2)}, u32[]{:S(2)}) collective-permute-start(f32[4,256,128]{2,1,0:T(8,128)} %slice_select_fusion.7), channel_id=1, source_target_pairs={{0,4},{2,6},{4,0},{6,2},{1,5},{3,7},{5,1},{7,3},{8,12},{10,14},{12... | collective-permute-start | bytes 1572872 | tf_op jit(solution)/shard_map/ppermute | solution.py:758
  230.2 35.7 %collective-permute-start.6 = (f32[8,256,128]{2,1,0:T(8,128)}, f32[8,256,128]{2,1,0:T(8,128)}, u32[]{:S(2)}, u32[]{:S(2)}) collective-permute-start(f32[8,256,128]{2,1,0:T(8,128)} %slice_select_fusion.2), channel_id=1, source_target_pairs={{0,2},{2,0},{4,6},{6,4},{1,3},{3,1},{5,7},{7,5},{8,10},{10,8},{12,... | collective-permute-start | bytes 3145736 | tf_op jit(solution)/shard_map/ppermute | solution.py:758
  267.9 70.8 %all-to-all-start.5 = ((f32[4,2,32,4096]{3,2,1,0:T(8,128)}), f32[4,2,32,4096]{3,2,1,0:T(8,128)}, u32[]{:S(2)}, u32[]{:S(2)}) async-start(f32[4,2,32,4096]{3,2,1,0:T(8,128)} %cut_rows.5), calls=%async_computation.5 | async-start | bytes 8388608 | tf_op jit(solution)/shard_map/all_to_all | solution.py:789
  272.8 9.5 copy-start.3
  284.2 49.2 %collective-permute-start.7 = (f32[4,256,128]{2,1,0:T(8,128)S(1)}, f32[4,256,128]{2,1,0:T(8,128)}, u32[]{:S(2)}, u32[]{:S(2)}) collective-permute-start(f32[4,256,128]{2,1,0:T(8,128)S(1)} %copy-done.18), channel_id=1, source_target_pairs={{0,4},{2,6},{4,0},{6,2},{1,5},{3,7},{5,1},{7,3},{8,12},{10,14},{12... | collective-permute-start | bytes 1572872 | tf_op jit(solution)/shard_map/ppermute | solution.py:758
  286.7 44.7 %collective-permute-start.8 = (f32[4,256,128]{2,1,0:T(8,128)}, f32[4,256,128]{2,1,0:T(8,128)}, u32[]{:S(2)}, u32[]{:S(2)}) collective-permute-start(f32[4,256,128]{2,1,0:T(8,128)} %slice_select_fusion.6), channel_id=1, source_target_pairs={{0,4},{2,6},{4,0},{6,2},{1,5},{3,7},{5,1},{7,3},{8,12},{10,14},{12... | collective-permute-start | bytes 1572872 | tf_op jit(solution)/shard_map/ppermute | solution.py:758
  287.1 49.1 %collective-permute-start.9 = (f32[8,256,128]{2,1,0:T(8,128)}, f32[8,256,128]{2,1,0:T(8,128)}, u32[]{:S(2)}, u32[]{:S(2)}) collective-permute-start(f32[8,256,128]{2,1,0:T(8,128)} %slice_select_fusion.1), channel_id=1, source_target_pairs={{0,2},{2,0},{4,6},{6,4},{1,3},{3,1},{5,7},{7,5},{8,10},{10,8},{12,... | collective-permute-start | bytes 3145736 | tf_op jit(solution)/shard_map/ppermute | solution.py:758
  315.0 19.6 %copy-start.2 = (f32[16,256,128]{2,1,0:T(8,128)S(1)}, f32[16,256,128]{2,1,0:T(8,128)}, u32[]{:S(2)}) copy-start(f32[16,256,128]{2,1,0:T(8,128)} %row_forward.7) | copy-start | bytes 6291460
  338.7 75.7 %all-to-all-start.6 = ((f32[4,2,48,4096]{3,2,1,0:T(8,128)}), f32[4,2,48,4096]{3,2,1,0:T(8,128)}, u32[]{:S(2)}, u32[]{:S(2)}) async-start(f32[4,2,48,4096]{3,2,1,0:T(8,128)} %cut_rows.6), calls=%async_computation.6 | async-start | bytes 12582912 | tf_op jit(solution)/shard_map/all_to_all | solution.py:789
  344.2 26.3 %collective-permute-start.11 = (f32[4,256,128]{2,1,0:T(8,128)}, f32[4,256,128]{2,1,0:T(8,128)}, u32[]{:S(2)}, u32[]{:S(2)}) collective-permute-start(f32[4,256,128]{2,1,0:T(8,128)} %select_add_fusion.6), channel_id=1, source_target_pairs={{0,4},{2,6},{4,0},{6,2},{1,5},{3,7},{5,1},{7,3},{8,12},{10,14},{12... | collective-permute-start | bytes 1572872 | tf_op jit(solution)/shard_map/ppermute | solution.py:758
  344.3 48.7 %collective-permute-start.10 = (f32[8,256,128]{2,1,0:T(8,128)}, f32[8,256,128]{2,1,0:T(8,128)}, u32[]{:S(2)}, u32[]{:S(2)}) collective-permute-start(f32[8,256,128]{2,1,0:T(8,128)} %get-tuple-element.95), channel_id=1, source_target_pairs={{0,2},{2,0},{4,6},{6,4},{1,3},{3,1},{5,7},{7,5},{8,10},{10,8},{12,... | collective-permute-start | bytes 3145736 | tf_op jit(solution)/shard_map/ppermute | solution.py:758
  348.1 22.4 %copy-start.16 = (f32[4,256,128]{2,1,0:T(8,128)S(1)}, f32[4,256,128]{2,1,0:T(8,128)}, u32[]{:S(2)}) copy-start(f32[4,256,128]{2,1,0:T(8,128)} %select_add_fusion.6) | copy-start | bytes 1572868
  348.1 42.6 %collective-permute-start.12 = (f32[4,256,128]{2,1,0:T(8,128)}, f32[4,256,128]{2,1,0:T(8,128)}, u32[]{:S(2)}, u32[]{:S(2)}) collective-permute-start(f32[4,256,128]{2,1,0:T(8,128)} %slice_select_fusion.5), channel_id=1, source_target_pairs={{0,4},{2,6},{4,0},{6,2},{1,5},{3,7},{5,1},{7,3},{8,12},{10,14},{12... | collective-permute-start | bytes 1572872 | tf_op jit(solution)/shard_map/ppermute | solution.py:758
  354.9 38.1 %copy-start.12 = (f32[4,256,128]{2,1,0:T(8,128)S(1)}, f32[4,256,128]{2,1,0:T(8,128)}, u32[]{:S(2)}) copy-start(f32[4,256,128]{2,1,0:T(8,128)} %copy-done.11) | copy-start | bytes 1572868
  354.9 38.1 %copy-start.14 = (f32[4,256,128]{2,1,0:T(8,128)S(1)}, f32[4,256,128]{2,1,0:T(8,128)}, u32[]{:S(2)}) copy-start(f32[4,256,128]{2,1,0:T(8,128)} %copy-done.13) | copy-start | bytes 1572868
  354.9 59.4 %collective-permute-start.13 = (f32[8,256,128]{2,1,0:T(8,128)}, f32[8,256,128]{2,1,0:T(8,128)S(1)}, u32[]{:S(2)}, u32[]{:S(2)}) collective-permute-start(f32[8,256,128]{2,1,0:T(8,128)} %get-tuple-element.99), channel_id=1, source_target_pairs={{0,2},{2,0},{4,6},{6,4},{1,3},{3,1},{5,7},{7,5},{8,10},{10,8},{12,... | collective-permute-start | bytes 3145736 | tf_op jit(solution)/shard_map/ppermute | solution.py:758
  371.6 21.0 %copy-start.7 = (f32[4,256,128]{2,1,0:T(8,128)}, f32[4,256,128]{2,1,0:T(8,128)S(1)}, u32[]{:S(2)}) copy-start(f32[4,256,128]{2,1,0:T(8,128)S(1)} %get-tuple-element.145) | copy-start | bytes 1572868
  371.6 21.0 %copy-start.9 = (f32[4,256,128]{2,1,0:T(8,128)}, f32[4,256,128]{2,1,0:T(8,128)S(1)}, u32[]{:S(2)}) copy-start(f32[4,256,128]{2,1,0:T(8,128)S(1)} %get-tuple-element.146) | copy-start | bytes 1572868
  414.4 6.6 copy-start.17
  414.4 58.1 %all-to-all-start.7 = ((f32[4,2,32,4096]{3,2,1,0:T(8,128)}), f32[4,2,32,4096]{3,2,1,0:T(8,128)}, u32[]{:S(2)}, u32[]{:S(2)}) async-start(f32[4,2,32,4096]{3,2,1,0:T(8,128)} %cut_rows.7), calls=%async_computation.7 | async-start | bytes 8388608 | tf_op jit(solution)/shard_map/all_to_all | solution.py:789
  420.3 49.2 %collective-permute-start.14 = (f32[8,256,128]{2,1,0:T(8,128)}, f32[8,256,128]{2,1,0:T(8,128)}, u32[]{:S(2)}, u32[]{:S(2)}) collective-permute-start(f32[8,256,128]{2,1,0:T(8,128)} %pad_maximum_fusion.6), channel_id=1, source_target_pairs={{0,2},{2,0},{4,6},{6,4},{1,3},{3,1},{5,7},{7,5},{8,10},{10,8},{12,... | collective-permute-start | bytes 3145736 | tf_op jit(solution)/shard_map/ppermute | solution.py:758
  421.1 39.4 %collective-permute-start.15 = (f32[4,256,128]{2,1,0:T(8,128)S(1)}, f32[4,256,128]{2,1,0:T(8,128)S(1)}, u32[]{:S(2)}, u32[]{:S(2)}) collective-permute-start(f32[4,256,128]{2,1,0:T(8,128)S(1)} %copy-done.17), channel_id=1, source_target_pairs={{0,4},{2,6},{4,0},{6,2},{1,5},{3,7},{5,1},{7,3},{8,12},{10,14},{12... | collective-permute-start | bytes 1572872 | tf_op jit(solution)/shard_map/ppermute | solution.py:758
  424.4 45.0 %collective-permute-start.16 = (f32[4,256,128]{2,1,0:T(8,128)}, f32[4,256,128]{2,1,0:T(8,128)S(1)}, u32[]{:S(2)}, u32[]{:S(2)}) collective-permute-start(f32[4,256,128]{2,1,0:T(8,128)} %slice_select_fusion.4), channel_id=1, source_target_pairs={{0,4},{2,6},{4,0},{6,2},{1,5},{3,7},{5,1},{7,3},{8,12},{10,14},{12... | collective-permute-start | bytes 1572872 | tf_op jit(solution)/shard_map/ppermute | solution.py:758
  460.4 9.1 copy-start.8
  460.4 9.1 copy-start.10
  472.5 53.7 %all-to-all-start.8 = ((f32[8,8,128,128]{3,2,1,0:T(8,128)}), f32[8,8,128,128]{3,2,1,0:T(8,128)}, u32[]{:S(2)}, u32[]{:S(2)}) async-start(f32[8,8,128,128]{3,2,1,0:T(8,128)} %row_backward.4), calls=%async_computation.8 | async-start | bytes 8388608 | tf_op jit(solution)/shard_map/all_to_all | solution.py:789
  477.1 39.1 %collective-permute-start.17 = (f32[8,256,128]{2,1,0:T(8,128)}, f32[8,256,128]{2,1,0:T(8,128)}, u32[]{:S(2)}, u32[]{:S(2)}) collective-permute-start(f32[8,256,128]{2,1,0:T(8,128)} %pad_maximum_fusion.7), channel_id=1, source_target_pairs={{0,2},{2,0},{4,6},{6,4},{1,3},{3,1},{5,7},{7,5},{8,10},{10,8},{12,... | collective-permute-start | bytes 3145736 | tf_op jit(solution)/shard_map/ppermute | solution.py:758
  477.7 38.4 %collective-permute-start.18 = (f32[4,256,128]{2,1,0:T(8,128)S(1)}, f32[4,256,128]{2,1,0:T(8,128)S(1)}, u32[]{:S(2)}, u32[]{:S(2)}) collective-permute-start(f32[4,256,128]{2,1,0:T(8,128)S(1)} %select_add_fusion.4), channel_id=1, source_target_pairs={{0,4},{2,6},{4,0},{6,2},{1,5},{3,7},{5,1},{7,3},{8,12},{10,14},{12... | collective-permute-start | bytes 1572872 | tf_op jit(solution)/shard_map/ppermute | solution.py:758
  526.2 53.7 %all-to-all-start.9 = ((f32[8,8,128,128]{3,2,1,0:T(8,128)}), f32[8,8,128,128]{3,2,1,0:T(8,128)}, u32[]{:S(2)}, u32[]{:S(2)}) async-start(f32[8,8,128,128]{3,2,1,0:T(8,128)} %row_backward.5), calls=%async_computation.9 | async-start | bytes 8388608 | tf_op jit(solution)/shard_map/all_to_all | solution.py:789
  530.7 36.6 %collective-permute-start.19 = (f32[8,256,128]{2,1,0:T(8,128)S(1)}, f32[8,256,128]{2,1,0:T(8,128)S(1)}, u32[]{:S(2)}, u32[]{:S(2)}) collective-permute-start(f32[8,256,128]{2,1,0:T(8,128)S(1)} %pad_maximum_fusion.8), channel_id=1, source_target_pairs={{0,2},{2,0},{4,6},{6,4},{1,3},{3,1},{5,7},{7,5},{8,10},{10,8},{12,... | collective-permute-start | bytes 3145736 | tf_op jit(solution)/shard_map/ppermute | solution.py:758
  579.9 53.7 %all-to-all-start.10 = ((f32[8,8,128,128]{3,2,1,0:T(8,128)}), f32[8,8,128,128]{3,2,1,0:T(8,128)}, u32[]{:S(2)}, u32[]{:S(2)}) async-start(f32[8,8,128,128]{3,2,1,0:T(8,128)} %row_backward.6), calls=%async_computation.10 | async-start | bytes 8388608 | tf_op jit(solution)/shard_map/all_to_all | solution.py:789
  620.4 17.9 %copy-start.22 = (f32[32,128]{1,0:T(8,128)S(1)}, f32[32,128]{1,0:T(8,128)}, u32[]{:S(2)}) copy-start(f32[32,128]{1,0:T(8,128)} %constant.103.clone) | copy-start | bytes 49156
  620.4 18.0 %copy-start.24 = (f32[32,128]{1,0:T(8,128)S(1)}, f32[32,128]{1,0:T(8,128)}, u32[]{:S(2)}) copy-start(f32[32,128]{1,0:T(8,128)} %constant.102.clone) | copy-start | bytes 49156
  620.5 18.0 %copy-start.26 = (f32[32,128]{1,0:T(8,128)S(1)}, f32[32,128]{1,0:T(8,128)}, u32[]{:S(2)}) copy-start(f32[32,128]{1,0:T(8,128)} %constant.101.clone) | copy-start | bytes 49156
  620.5 18.0 %copy-start.28 = (f32[32,128]{1,0:T(8,128)S(1)}, f32[32,128]{1,0:T(8,128)}, u32[]{:S(2)}) copy-start(f32[32,128]{1,0:T(8,128)} %constant.100.clone) | copy-start | bytes 49156
  620.5 18.0 %copy-start.34 = (f32[4]{0:T(128)S(1)}, f32[4]{0:T(128)}, u32[]{:S(2)}) copy-start(f32[4]{0:T(128)} %copy-done.33) | copy-start | bytes 52
  620.5 18.0 %copy-start.36 = (f32[4]{0:T(128)S(1)}, f32[4]{0:T(128)}, u32[]{:S(2)}) copy-start(f32[4]{0:T(128)} %copy-done.35) | copy-start | bytes 52
  620.5 19.0 %copy-start.1 = (f32[4,2,16,4096]{3,2,1,0:T(8,128)S(1)}, f32[4,2,16,4096]{3,2,1,0:T(8,128)}, u32[]{:S(2)}) copy-start(f32[4,2,16,4096]{3,2,1,0:T(8,128)} %copy-done) | copy-start | bytes 6291460
  633.6 53.9 %all-to-all-start.11 = ((f32[8,8,128,128]{3,2,1,0:T(8,128)}), f32[8,8,128,128]{3,2,1,0:T(8,128)}, u32[]{:S(2)}, u32[]{:S(2)}) async-start(f32[8,8,128,128]{3,2,1,0:T(8,128)} %row_backward.7), calls=%async_computation.11 | async-start | bytes 8388608 | tf_op jit(solution)/shard_map/all_to_all | solution.py:789
  724.2 6.9 collective-permute-start.20
  757.4 205.4 %collective-permute-start.21 = (f32[2,96,4096]{2,1,0:T(8,128)}, f32[2,96,4096]{2,1,0:T(8,128)S(1)}, u32[]{:S(2)}, u32[]{:S(2)}) collective-permute-start(f32[2,96,4096]{2,1,0:T(8,128)} %get-tuple-element.116), channel_id=1, source_target_pairs={{0,8},{8,0},{16,24},{24,16},{1,9},{9,1},{17,25},{25,17},{2,10},{10... | collective-permute-start | bytes 9437192 | tf_op jit(solution)/shard_map/ppermute | solution.py:758
  759.3 203.5 %collective-permute-start.22 = (f32[2,96,4096]{2,1,0:T(8,128)}, f32[2,96,4096]{2,1,0:T(8,128)}, u32[]{:S(2)}, u32[]{:S(2)}) collective-permute-start(f32[2,96,4096]{2,1,0:T(8,128)} %get-tuple-element.117), channel_id=1, source_target_pairs={{0,16},{8,24},{16,0},{24,8},{1,17},{9,25},{17,1},{25,9},{2,18},{10... | collective-permute-start | bytes 9437192 | tf_op jit(solution)/shard_map/ppermute | solution.py:758
  760.3 202.6 %collective-permute-start.23 = (f32[2,96,4096]{2,1,0:T(8,128)}, f32[2,96,4096]{2,1,0:T(8,128)}, u32[]{:S(2)}, u32[]{:S(2)}) collective-permute-start(f32[2,96,4096]{2,1,0:T(8,128)} %get-tuple-element.118), channel_id=1, source_target_pairs={{0,24},{8,16},{16,8},{24,0},{1,25},{9,17},{17,9},{25,1},{2,26},{10... | collective-permute-start | bytes 9437192 | tf_op jit(solution)/shard_map/ppermute | solution.py:758
  760.9 135.6 %collective-permute-start.24 = (f32[4,2,1,4096]{3,2,1,0:T(1,128)S(1)}, f32[4,2,1,4096]{3,2,1,0:T(1,128)S(1)}, u32[]{:S(2)}, u32[]{:S(2)}) collective-permute-start(f32[4,2,1,4096]{3,2,1,0:T(1,128)S(1)} %get-tuple-element.125), channel_id=1, source_target_pairs={{0,8},{8,16},{16,24},{24,1},{1,9},{9,17},{17,25},{25,2},{2,10},{10... | collective-permute-start | bytes 393224 | tf_op jit(solution)/shard_map/ppermute | solution.py:896
  908.0 25.2 %collective-permute-start.25 = (f32[2,32,4096]{2,1,0:T(8,128)}, f32[2,32,4096]{2,1,0:T(8,128)}, u32[]{:S(2)}, u32[]{:S(2)}) collective-permute-start(f32[2,32,4096]{2,1,0:T(8,128)} %get-tuple-element.120), channel_id=1, source_target_pairs={{0,8},{8,0},{16,24},{24,16},{1,9},{9,1},{17,25},{25,17},{2,10},{10... | collective-permute-start | bytes 3145736 | tf_op jit(solution)/shard_map/ppermute | solution.py:758
  910.5 24.5 %collective-permute-start.26 = (f32[2,32,4096]{2,1,0:T(8,128)}, f32[2,32,4096]{2,1,0:T(8,128)}, u32[]{:S(2)}, u32[]{:S(2)}) collective-permute-start(f32[2,32,4096]{2,1,0:T(8,128)} %get-tuple-element.121), channel_id=1, source_target_pairs={{0,16},{8,24},{16,0},{24,8},{1,17},{9,25},{17,1},{25,9},{2,18},{10... | collective-permute-start | bytes 3145736 | tf_op jit(solution)/shard_map/ppermute | solution.py:758
  933.2 24.7 %collective-permute-start.27 = (f32[2,32,4096]{2,1,0:T(8,128)}, f32[2,32,4096]{2,1,0:T(8,128)}, u32[]{:S(2)}, u32[]{:S(2)}) collective-permute-start(f32[2,32,4096]{2,1,0:T(8,128)} %get-tuple-element.122), channel_id=1, source_target_pairs={{0,24},{8,16},{16,8},{24,0},{1,25},{9,17},{17,9},{25,1},{2,26},{10... | collective-permute-start | bytes 3145736 | tf_op jit(solution)/shard_map/ppermute | solution.py:758
  (15 other events, 29.4 us)

commit v5 on v4

--- a/solution.py
+++ b/solution.py
@@ -858,15 +858,14 @@
 
     queue = list(sent) + [None] * (len(plan.cuts) - 1)
     state = [None] * count
-    before, back = [held[0]], []
+    before, back, cuts = [held[0]], [], []
     slot = 0
     while len(back) < count:
         others, before = before, []
         if queue:
             value = queue.pop(0)
             if value is None:
-                value = cut_rows(plan, field[:, 0], sum(plan.cuts[: len(held)]), plan.cuts[len(held)])
-                held.append(exchanged(after(value, *others), "depth"))
+                held.append(exchanged(after(cuts[len(held) - 1], *others), "depth"))
                 before.append(held[-1])
             else:
                 before.append(exchanged(after(value, *others), level_axes))
@@ -883,6 +882,9 @@
                     queue.append(state[part])
         if slot == 0:
             before += [high, low]
+        if slot + 1 < len(plan.cuts):
+            cuts.append(cut_rows(plan, field[:, 0], sum(plan.cuts[: slot + 1]), plan.cuts[slot + 1]))
+            before.append(cuts[-1])
         slot += 1
 
     held = jnp.concatenate(held, axis=2)
@@ -899,6 +901,8 @@
     first = max(1, tiles // 4)
     result = None
     for begin, steps in ((0, first), (first, tiles - first)):
+        if result is not None:
+            moved = after(moved, parts[0])
         parts = shrink_pass(plan, ends, moved, above, below, begin, steps)
         parts = [parts[0]] + [swapped(parts[s], "depth", depth, s) for s in range(1, depth)]
         result = place_rows(plan, ends, parts, begin * 8, result)

time: 986 us -> 975 us (0.989)
    ppermute x26, waiting for transfers between devices: 128 us -> 268 us  [swapped(): return lax.ppermute(value, axes, [(i, i ^ step) for i in range(size)])]
    ppermute x1, waiting for transfers between devices: 132 us -> 1.37 us  [per_device(): above = lax.ppermute(moved[:, :, -1:], all_axes, downward)]
    all_to_all x12, waiting for transfers between devices: 121 us -> 107 us  [exchanged(): return lax.all_to_all(value, axes, 0, 0, tiled=True)]
  transfers between devices with their start and end apart: 40 -> 40, of which waited for: 20 -> 21; matrix products, arithmetic and copies ran while one was open for 5% -> 5% of each run, Pallas kernels for 37% -> 36%
where the time goes in v5:
time: 975 us; the launch traced here: 964 us
  Pallas kernels  428 us (44%)
  waiting for transfers between devices  380 us (39%)
  starting transfers between devices  97.1 us (10%)
  other arithmetic  45.2 us (5%)
  local copies, waits for them, and re-layouts  11.3 us (1%)
    ppermute x26, waiting for transfers between devices, swapped(): return lax.ppermute(value, axes, [(i, i ^ step) for i in range(size)])  268 us
    pallas_call x4, Pallas kernels, row_backward(): pl.pallas_call(kernel, grid_spec=pltpu.PrefetchScalarGridSpec(num_scalar_...  144 us
    all_to_all x12, waiting for transfers between devices, exchanged(): return lax.all_to_all(value, axes, 0, 0, tiled=True)  107 us
    pallas_call x4, Pallas kernels, row_forward(): pl.pallas_call(kernel, grid_spec=pltpu.PrefetchScalarGridSpec(num_scalar_...  105 us
    all_to_all x12, starting transfers between devices, exchanged(): return lax.all_to_all(value, axes, 0, 0, tiled=True)  56.6 us
    ppermute x26, starting transfers between devices, swapped(): return lax.ppermute(value, axes, [(i, i ^ step) for i in range(size)])  36.8 us
    pallas_call x2, Pallas kernels, shrink_pass(): pl.pallas_call(kernel, grid_spec=pltpu.PrefetchScalarGridSpec(num_scalar_...  36.5 us
    pallas_call x1, Pallas kernels, step_pass(): pl.pallas_call(kernel, grid=(plan.planes, plan.piece // rows), in_specs=[...  35 us
  transfers between devices with their start and end apart: 40, of which 21 were waited for; matrix products, arithmetic and copies ran while one was open for 5% of the time, Pallas kernels for 36%

profile of v5, /device:TPU:0, one launch (start us, length us, event | category | flops | bytes accessed | tf_op | source)
XLA Modules:
  0.0 964.2 jit_solution(12896554464390642181)
XLA Ops:
  0.0 3.9 collective-permute-start.2
  5.2 3.8 cut_rows.4
  9.8 1.9 pad_maximum_fusion.11
  12.4 4.2 all-to-all-start
  16.6 33.4 %column_pass.1 = (f32[8,2,512,128]{3,2,1,0:T(8,128)}, f32[8,2,512,128]{3,2,1,0:T(8,128)}, f32[8,2,512,128]{3,2,1,0:T(8,128)}, f32[8,2,512,128]{3,2,1,0:T(8,128)}) custom-call(f32[2,512,4096]{2,1,0:T(8,128)} %bitcast.28, bf16[768,256]{1,0:T(8,128)(2,1)} %constant.31.clone.fwd.refs_5_, bf16[768,256]{1,0:T(8,128)(2,1)} %constant.32.clone.inv.refs_6_, ...), custom_call_target="tpu_custom_call" | custom-call | flops 12999999488 | bytes 34000000 | tf_op jit(solution)/shard_map/column_pass/pallas_call | solution.py:344
  52.5 4.5 all-to-all-start.1
  57.0 6.7 cut_rows.5
  63.7 33.2 %slot_matrices.1 = (bf16[16,256,2048]{2,1,0:T(8,128)(2,1)}, bf16[16,256,2048]{2,1,0:T(8,128)(2,1)}) custom-call(f32[16,256,256]{2,1,0:T(8,128)} %constant.108.clone.b_ref, f32[16,8,256]{2,1,0:T(8,128)} %copy.27.w_ref), custom_call_target="tpu_custom_call" | custom-call | flops 25999998976 | bytes 34000000 | tf_op jit(solution)/shard_map/slot_matrices/pallas_call | solution.py:396
  96.8 9.3 all-to-all-done.1.x_ref
  106.2 4.8 all-to-all-start.2
  111.0 1.7 dynamic-slice_bitcast_fusion
  113.2 9.3 cut_rows.6
  124.9 26.3 %row_forward.4 = f32[16,256,128]{2,1,0:T(8,128)} custom-call(f32[4,16]{1,0:T(4,128)} %pad_maximum_fusion.10.phase, f32[8,2,512,128]{3,2,1,0:T(8,128)} %all-to-all-done.1.x_ref, f32[2,512,128]{2,1,0:T(8,128)} %get-tuple-element.142.h_ref, bf16[16,256,2048]{2,1,0:T(8,128)(2,1)} %get-tuple-element.77.wh, bf16[16,256,2048]{2,1,0:T(8,128)(2,1)} %get-tuple-element.78.wl), custom_call_target="tpu_custom_call" | custom-call | flops 12999999488 | bytes 60000000 | tf_op jit(solution)/shard_map/row_forward/pallas_call | solution.py:459
  151.2 8.9 all-to-all-done.2.x_ref
  160.1 4.5 all-to-all-start.3
  164.7 6.8 cut_rows.7
  173.2 26.3 %row_forward.5 = f32[16,256,128]{2,1,0:T(8,128)} custom-call(f32[4,16]{1,0:T(4,128)} %pad_maximum_fusion.10.phase, f32[8,2,512,128]{3,2,1,0:T(8,128)} %all-to-all-done.2.x_ref, f32[2,512,128]{2,1,0:T(8,128)} %get-tuple-element.141.h_ref, bf16[16,256,2048]{2,1,0:T(8,128)(2,1)} %get-tuple-element.77.wh, bf16[16,256,2048]{2,1,0:T(8,128)(2,1)} %get-tuple-element.78.wl), custom_call_target="tpu_custom_call" | custom-call | flops 12999999488 | bytes 60000000 | tf_op jit(solution)/shard_map/row_forward/pallas_call | solution.py:459
  200.9 12.9 %all-to-all-done.3.x_ref = f32[8,2,512,128]{3,2,1,0:T(8,128)} async-done(((f32[8,2,512,128]{3,2,1,0:T(8,128)}), f32[8,2,512,128]{3,2,1,0:T(8,128)}, u32[]{:S(2)}, u32[]{:S(2)}) %all-to-all-start.3) | async-done | bytes 4194336 | tf_op jit(solution)/shard_map/all_to_all | solution.py:789
  213.8 5.0 all-to-all-start.4
  220.8 2.6 collective-permute-start.5
  224.9 26.3 %row_forward.6 = f32[16,256,128]{2,1,0:T(8,128)} custom-call(f32[4,16]{1,0:T(4,128)} %pad_maximum_fusion.10.phase, f32[8,2,512,128]{3,2,1,0:T(8,128)} %all-to-all-done.3.x_ref, f32[2,512,128]{2,1,0:T(8,128)} %get-tuple-element.140.h_ref, bf16[16,256,2048]{2,1,0:T(8,128)(2,1)} %get-tuple-element.77.wh, bf16[16,256,2048]{2,1,0:T(8,128)(2,1)} %get-tuple-element.78.wl), custom_call_target="tpu_custom_call" | custom-call | flops 12999999488 | bytes 60000000 | tf_op jit(solution)/shard_map/row_forward/pallas_call | solution.py:459
  252.1 6.9 collective-permute-done.6
  260.4 7.5 all-to-all-done.4.x_ref
  267.9 4.8 all-to-all-start.5
  274.7 2.6 collective-permute-start.7
  279.2 26.3 %row_forward.7 = f32[16,256,128]{2,1,0:T(8,128)} custom-call(f32[4,16]{1,0:T(4,128)} %pad_maximum_fusion.10.phase, f32[8,2,512,128]{3,2,1,0:T(8,128)} %all-to-all-done.4.x_ref, f32[2,512,128]{2,1,0:T(8,128)} %get-tuple-element.139.h_ref, bf16[16,256,2048]{2,1,0:T(8,128)(2,1)} %get-tuple-element.77.wh, bf16[16,256,2048]{2,1,0:T(8,128)(2,1)} %get-tuple-element.78.wl), custom_call_target="tpu_custom_call" | custom-call | flops 12999999488 | bytes 60000000 | tf_op jit(solution)/shard_map/row_forward/pallas_call | solution.py:459
  305.5 14.7 %collective-permute-done.8 = f32[4,256,128]{2,1,0:T(8,128)} collective-permute-done((f32[4,256,128]{2,1,0:T(8,128)}, f32[4,256,128]{2,1,0:T(8,128)}, u32[]{:S(2)}, u32[]{:S(2)}) %collective-permute-start.8) | collective-permute-done | bytes 524320 | tf_op jit(solution)/shard_map/ppermute | solution.py:758
  320.2 1.9 select_add_fusion.6
  327.5 5.3 all-to-all-start.6
  332.9 4.0 collective-permute-start.10
  338.0 22.2 %collective-permute-done.11 = f32[4,256,128]{2,1,0:T(8,128)S(1)} collective-permute-done((f32[4,256,128]{2,1,0:T(8,128)}, f32[4,256,128]{2,1,0:T(8,128)S(1)}, u32[]{:S(2)}, u32[]{:S(2)}) %collective-permute-start.11) | collective-permute-done | bytes 524320 | tf_op jit(solution)/shard_map/ppermute | solution.py:758
  362.5 16.7 %collective-permute-done.12 = f32[4,256,128]{2,1,0:T(8,128)S(1)} collective-permute-done((f32[4,256,128]{2,1,0:T(8,128)S(1)}, f32[4,256,128]{2,1,0:T(8,128)S(1)}, u32[]{:S(2)}, u32[]{:S(2)}) %collective-permute-start.12) | collective-permute-done | bytes 524320 | tf_op jit(solution)/shard_map/ppermute | solution.py:758
  383.2 19.8 %collective-permute-done.13 = f32[8,256,128]{2,1,0:T(8,128)S(1)} collective-permute-done((f32[8,256,128]{2,1,0:T(8,128)}, f32[8,256,128]{2,1,0:T(8,128)S(1)}, u32[]{:S(2)}, u32[]{:S(2)}) %collective-permute-start.13) | collective-permute-done | bytes 1048608 | tf_op jit(solution)/shard_map/ppermute | solution.py:758
  403.9 5.0 all-to-all-start.7
  409.8 1.8 collective-permute-start.14
  411.5 3.4 collective-permute-start.15
  415.0 36.0 %row_backward.4 = f32[8,8,128,128]{3,2,1,0:T(8,128)} custom-call(f32[4,16]{1,0:T(4,128)} %pad_maximum_fusion.10.phase, f32[16,256,128]{2,1,0:T(8,128)} %pad_maximum_fusion.1.m_ref, bf16[16,256,2048]{2,1,0:T(8,128)(2,1)} %get-tuple-element.77.wh, bf16[16,256,2048]{2,1,0:T(8,128)(2,1)} %get-tuple-element.78.wl), custom_call_target="tpu_custom_call" | custom-call | flops 12999999488 | bytes 60000000 | tf_op jit(solution)/shard_map/row_backward/pallas_call | solution.py:526
  452.0 7.8 collective-permute-done.16
  462.9 4.5 all-to-all-start.8
  468.1 2.4 collective-permute-start.18
  470.5 36.0 %row_backward.5 = f32[8,8,128,128]{3,2,1,0:T(8,128)} custom-call(f32[4,16]{1,0:T(4,128)} %pad_maximum_fusion.10.phase, f32[16,256,128]{2,1,0:T(8,128)} %pad_maximum_fusion.2.m_ref, bf16[16,256,2048]{2,1,0:T(8,128)(2,1)} %get-tuple-element.77.wh, bf16[16,256,2048]{2,1,0:T(8,128)(2,1)} %get-tuple-element.78.wl), custom_call_target="tpu_custom_call" | custom-call | flops 12999999488 | bytes 60000000 | tf_op jit(solution)/shard_map/row_backward/pallas_call | solution.py:526
  509.5 7.1 all-to-all-done.8.refs_0_
  516.6 4.5 all-to-all-start.9
  521.7 35.9 %row_backward.6 = f32[8,8,128,128]{3,2,1,0:T(8,128)} custom-call(f32[4,16]{1,0:T(4,128)} %pad_maximum_fusion.10.phase, f32[16,256,128]{2,1,0:T(8,128)} %pad_maximum_fusion.3.m_ref, bf16[16,256,2048]{2,1,0:T(8,128)(2,1)} %get-tuple-element.77.wh, bf16[16,256,2048]{2,1,0:T(8,128)(2,1)} %get-tuple-element.78.wl), custom_call_target="tpu_custom_call" | custom-call | flops 12999999488 | bytes 60000000 | tf_op jit(solution)/shard_map/row_backward/pallas_call | solution.py:526
  559.4 10.9 %all-to-all-done.9.refs_1_ = f32[8,8,128,128]{3,2,1,0:T(8,128)} async-done(((f32[8,8,128,128]{3,2,1,0:T(8,128)}), f32[8,8,128,128]{3,2,1,0:T(8,128)}, u32[]{:S(2)}, u32[]{:S(2)}) %all-to-all-start.9) | async-done | bytes 4194336 | tf_op jit(solution)/shard_map/all_to_all | solution.py:789
  570.3 4.6 all-to-all-start.10
  574.9 36.0 %row_backward.7 = f32[8,8,128,128]{3,2,1,0:T(8,128)} custom-call(f32[4,16]{1,0:T(4,128)} %pad_maximum_fusion.10.phase, f32[16,256,128]{2,1,0:T(8,128)} %pad_maximum_fusion.4.m_ref, bf16[16,256,2048]{2,1,0:T(8,128)(2,1)} %get-tuple-element.77.wh, bf16[16,256,2048]{2,1,0:T(8,128)(2,1)} %get-tuple-element.78.wl), custom_call_target="tpu_custom_call" | custom-call | flops 12999999488 | bytes 60000000 | tf_op jit(solution)/shard_map/row_backward/pallas_call | solution.py:526
  610.9 13.1 %all-to-all-done.10.refs_2_ = f32[8,8,128,128]{3,2,1,0:T(8,128)} async-done(((f32[8,8,128,128]{3,2,1,0:T(8,128)}), f32[8,8,128,128]{3,2,1,0:T(8,128)}, u32[]{:S(2)}, u32[]{:S(2)}) %all-to-all-start.10) | async-done | bytes 4194336 | tf_op jit(solution)/shard_map/all_to_all | solution.py:789
  624.0 4.8 all-to-all-start.11
  629.8 11.1 %pad_maximum_fusion.refs_4_ = f32[4,2,128,4096]{3,2,1,0:T(8,128)} fusion(f32[4,2,32,4096]{3,2,1,0:T(8,128)} %all-to-all-done.7, f32[4,2,48,4096]{3,2,1,0:T(8,128)} %all-to-all-done.6, f32[4,2,32,4096]{3,2,1,0:T(8,128)} %all-to-all-done.5, f32[4,2,16,4096]{3,2,1,0:T(8,128)S(1)} %copy-done.1), kind=kLoop, calls=%fused_computation.1 | loop fusion | flops 12582912 | bytes 33554432 | tf_op jit(solution)/shard_map/concatenate | solution.py:890
  640.9 37.0 %all-to-all-done.11.refs_3_ = f32[8,8,128,128]{3,2,1,0:T(8,128)} async-done(((f32[8,8,128,128]{3,2,1,0:T(8,128)}), f32[8,8,128,128]{3,2,1,0:T(8,128)}, u32[]{:S(2)}, u32[]{:S(2)}) %all-to-all-start.11) | async-done | bytes 4194336 | tf_op jit(solution)/shard_map/all_to_all | solution.py:789
  677.9 35.0 %step_pass.1.cur.nxt.up = f32[4,2,128,4096]{3,2,1,0:T(8,128)} custom-call(f32[8,8,128,128]{3,2,1,0:T(8,128)} %all-to-all-done.8.refs_0_, f32[8,8,128,128]{3,2,1,0:T(8,128)} %all-to-all-done.9.refs_1_, f32[8,8,128,128]{3,2,1,0:T(8,128)} %all-to-all-done.10.refs_2_, f32[8,8,128,128]{3,2,1,0:T(8,128)} %all-to-all-done.11.refs_3_, ...), custom_call_target="tpu_custom_call" | custom-call | flops 12999999488 | bytes 51000000 | tf_op jit(solution)/shard_map/step_pass/pallas_call | solution.py:575
  712.8 1.7 fusion.23
  714.6 2.4 collective-permute-start.20
  720.4 3.9 collective-permute-done.21.down
  724.9 10.9 %shrink_pass.2 = (f32[2,32,4096]{2,1,0:T(8,128)}, f32[2,32,4096]{2,1,0:T(8,128)}, f32[2,32,4096]{2,1,0:T(8,128)}, f32[2,32,4096]{2,1,0:T(8,128)}) custom-call(s32[3]{0:T(128)} %pad_add_fusion.scal, f32[4,2,128,4096]{3,2,1,0:T(8,128)} %step_pass.1.cur.nxt.up, f32[4,2,128,4096]{3,2,1,0:T(8,128)} %step_pass.1.cur.nxt.up, f32[4,2,1,4096]{3,2,1,0:T(1,128)} %copy-done.19, ...), custom_call_target="tpu_custom_call" | custom-call | flops 100000000 | bytes 9000000 | tf_op jit(solution)/shard_map/shrink_pass/pallas_call | solution.py:674
  735.8 25.6 %shrink_pass.3 = (f32[2,96,4096]{2,1,0:T(8,128)}, f32[2,96,4096]{2,1,0:T(8,128)}, f32[2,96,4096]{2,1,0:T(8,128)}, f32[2,96,4096]{2,1,0:T(8,128)}) custom-call(s32[3]{0:T(128)} %pad_add_fusion.scal, f32[4,2,128,4096]{3,2,1,0:T(8,128)} %step_pass.1.cur.nxt.up, f32[4,2,128,4096]{3,2,1,0:T(8,128)} %step_pass.1.cur.nxt.up, ...), custom_call_target="tpu_custom_call" | custom-call | flops 100000000 | bytes 9000000 | tf_op jit(solution)/shard_map/shrink_pass/pallas_call | solution.py:674
  761.4 2.0 collective-permute-start.22
  765.0 2.0 collective-permute-start.25
  766.9 153.8 %collective-permute-done.25.refs_1_ = f32[2,32,4096]{2,1,0:T(8,128)} collective-permute-done((f32[2,32,4096]{2,1,0:T(8,128)}, f32[2,32,4096]{2,1,0:T(8,128)}, u32[]{:S(2)}, u32[]{:S(2)}) %collective-permute-start.25) | collective-permute-done | bytes 1048608 | tf_op jit(solution)/shard_map/ppermute | solution.py:758
  920.7 2.1 collective-permute-start.27
  923.5 23.7 %collective-permute-done.27.refs_3_ = f32[2,32,4096]{2,1,0:T(8,128)} collective-permute-done((f32[2,32,4096]{2,1,0:T(8,128)}, f32[2,32,4096]{2,1,0:T(8,128)}, u32[]{:S(2)}, u32[]{:S(2)}) %collective-permute-start.27) | collective-permute-done | bytes 1048608 | tf_op jit(solution)/shard_map/ppermute | solution.py:758
  947.2 4.8 place_rows.2.refs_4_
  953.8 10.1 %place_rows.3 = f32[2,512,4096]{2,1,0:T(8,128)} custom-call(s32[3]{0:T(128)} %pad_add_fusion.scal, f32[2,96,4096]{2,1,0:T(8,128)} %get-tuple-element.118.refs_0_, f32[2,96,4096]{2,1,0:T(8,128)} %copy-done.15, f32[2,96,4096]{2,1,0:T(8,128)} %collective-permute-done.23.refs_2_, ...), custom_call_target="tpu_custom_call", output_to_operand_aliasing={{}: (5, {})} | custom-call | bytes 9000000 | tf_op jit(solution)/shard_map/place_rows/pallas_call | solution.py:716
  (163 shorter events, 53.6 us)
Async XLA Ops:
  0.0 9.8 %collective-permute-start.2 = (f32[1]{0:T(128)}, f32[1]{0:T(128)}, u32[]{:S(2)}, u32[]{:S(2)}) collective-permute-start(f32[1]{0:T(128)} %param.23), channel_id=1, source_target_pairs={{0,24},{8,16},{16,8},{24,0},{1,25},{9,17},{17,9},{25,1},{2,26},{10... | collective-permute-start | bytes 20 | tf_op jit(solution)/shard_map/ppermute | solution.py:758
  3.9 5.9 collective-permute-start.1
  4.4 5.4 collective-permute-start
  12.4 38.8 %all-to-all-start = ((f32[4,2,16,4096]{3,2,1,0:T(8,128)}), f32[4,2,16,4096]{3,2,1,0:T(8,128)S(1)}, u32[]{:S(2)}, u32[]{:S(2)}) async-start(f32[4,2,16,4096]{3,2,1,0:T(8,128)} %cut_rows.4), calls=%async_computation | async-start | bytes 4194304 | tf_op jit(solution)/shard_map/all_to_all | solution.py:789
  16.5 33.4 %copy-start.28 = (f32[16,256]{1,0:T(8,128)S(1)}, f32[16,256]{1,0:T(8,128)}, u32[]{:S(2)}) copy-start(f32[16,256]{1,0:T(8,128)} %constant.120) | copy-start | bytes 49156
  16.5 33.4 %copy-start.29 = (f32[16,256]{1,0:T(8,128)S(1)}, f32[16,256]{1,0:T(8,128)}, u32[]{:S(2)}) copy-start(f32[16,256]{1,0:T(8,128)} %constant.119) | copy-start | bytes 49156
  16.5 33.4 %copy-start.30 = (f32[16,256]{1,0:T(8,128)S(1)}, f32[16,256]{1,0:T(8,128)}, u32[]{:S(2)}) copy-start(f32[16,256]{1,0:T(8,128)} %constant.118) | copy-start | bytes 49156
  16.5 33.4 %copy-start.31 = (f32[16,256]{1,0:T(8,128)S(1)}, f32[16,256]{1,0:T(8,128)}, u32[]{:S(2)}) copy-start(f32[16,256]{1,0:T(8,128)} %constant.117) | copy-start | bytes 49156
  52.5 53.7 %all-to-all-start.1 = ((f32[8,2,512,128]{3,2,1,0:T(8,128)}), f32[8,2,512,128]{3,2,1,0:T(8,128)}, u32[]{:S(2)}, u32[]{:S(2)}) async-start(f32[8,2,512,128]{3,2,1,0:T(8,128)} %get-tuple-element.74), calls=%async_computation.1 | async-start | bytes 8388608 | tf_op jit(solution)/shard_map/all_to_all | solution.py:789
  106.2 53.9 %all-to-all-start.2 = ((f32[8,2,512,128]{3,2,1,0:T(8,128)}), f32[8,2,512,128]{3,2,1,0:T(8,128)}, u32[]{:S(2)}, u32[]{:S(2)}) async-start(f32[8,2,512,128]{3,2,1,0:T(8,128)} %get-tuple-element.81), calls=%async_computation.2 | async-start | bytes 8388608 | tf_op jit(solution)/shard_map/all_to_all | solution.py:789
  112.7 10.5 %collective-permute-start.3 = (f32[512,512]{1,0:T(8,128)S(1)}, f32[512,512]{1,0:T(8,128)S(1)}, u32[]{:S(2)}, u32[]{:S(2)}) collective-permute-start(f32[512,512]{1,0:T(8,128)S(1)} %get-tuple-element.130), channel_id=1, source_target_pairs={{0,1},{1,0},{2,3},{3,2},{4,5},{5,4},{6,7},{7,6},{8,9},{9,8},{10,11... | collective-permute-start | bytes 3145736 | tf_op jit(solution)/shard_map/ppermute | solution.py:758
  113.2 9.3 copy-start.37
  113.2 9.4 copy-start.36
  160.1 53.7 %all-to-all-start.3 = ((f32[8,2,512,128]{3,2,1,0:T(8,128)}), f32[8,2,512,128]{3,2,1,0:T(8,128)}, u32[]{:S(2)}, u32[]{:S(2)}) async-start(f32[8,2,512,128]{3,2,1,0:T(8,128)} %get-tuple-element.84), calls=%async_computation.3 | async-start | bytes 8388608 | tf_op jit(solution)/shard_map/all_to_all | solution.py:789
  164.6 6.8 copy-start.6
  171.5 28.0 %collective-permute-start.4 = (f32[8,256,128]{2,1,0:T(8,128)S(1)}, f32[8,256,128]{2,1,0:T(8,128)}, u32[]{:S(2)}, u32[]{:S(2)}) collective-permute-start(f32[8,256,128]{2,1,0:T(8,128)S(1)} %slice_select_fusion.3), channel_id=1, source_target_pairs={{0,2},{2,0},{4,6},{6,4},{1,3},{3,1},{5,7},{7,5},{8,10},{10,8},{12,... | collective-permute-start | bytes 3145736 | tf_op jit(solution)/shard_map/ppermute | solution.py:758
  200.9 17.9 %copy-start.5 = (f32[16,256,128]{2,1,0:T(8,128)S(1)}, f32[16,256,128]{2,1,0:T(8,128)}, u32[]{:S(2)}) copy-start(f32[16,256,128]{2,1,0:T(8,128)} %row_forward.5) | copy-start | bytes 6291460
  213.8 54.1 %all-to-all-start.4 = ((f32[8,2,512,128]{3,2,1,0:T(8,128)}), f32[8,2,512,128]{3,2,1,0:T(8,128)}, u32[]{:S(2)}, u32[]{:S(2)}) async-start(f32[8,2,512,128]{3,2,1,0:T(8,128)} %get-tuple-element.88), calls=%async_computation.4 | async-start | bytes 8388608 | tf_op jit(solution)/shard_map/all_to_all | solution.py:789
  220.8 30.5 %collective-permute-start.5 = (f32[4,256,128]{2,1,0:T(8,128)}, f32[4,256,128]{2,1,0:T(8,128)S(1)}, u32[]{:S(2)}, u32[]{:S(2)}) collective-permute-start(f32[4,256,128]{2,1,0:T(8,128)} %slice_select_fusion.7), channel_id=1, source_target_pairs={{0,4},{2,6},{4,0},{6,2},{1,5},{3,7},{5,1},{7,3},{8,12},{10,14},{12... | collective-permute-start | bytes 1572872 | tf_op jit(solution)/shard_map/ppermute | solution.py:758
  223.3 35.7 %collective-permute-start.6 = (f32[8,256,128]{2,1,0:T(8,128)}, f32[8,256,128]{2,1,0:T(8,128)}, u32[]{:S(2)}, u32[]{:S(2)}) collective-permute-start(f32[8,256,128]{2,1,0:T(8,128)} %slice_select_fusion.2), channel_id=1, source_target_pairs={{0,2},{2,0},{4,6},{6,4},{1,3},{3,1},{5,7},{7,5},{8,10},{10,8},{12,... | collective-permute-start | bytes 3145736 | tf_op jit(solution)/shard_map/ppermute | solution.py:758
  260.4 12.3 %copy-start.3 = (f32[16,256,128]{2,1,0:T(8,128)S(1)}, f32[16,256,128]{2,1,0:T(8,128)}, u32[]{:S(2)}) copy-start(f32[16,256,128]{2,1,0:T(8,128)} %row_forward.6) | copy-start | bytes 6291460
  267.9 59.6 %all-to-all-start.5 = ((f32[4,2,32,4096]{3,2,1,0:T(8,128)}), f32[4,2,32,4096]{3,2,1,0:T(8,128)}, u32[]{:S(2)}, u32[]{:S(2)}) async-start(f32[4,2,32,4096]{3,2,1,0:T(8,128)} %cut_rows.5), calls=%async_computation.5 | async-start | bytes 8388608 | tf_op jit(solution)/shard_map/all_to_all | solution.py:789
  274.7 47.5 %collective-permute-start.7 = (f32[4,256,128]{2,1,0:T(8,128)S(1)}, f32[4,256,128]{2,1,0:T(8,128)}, u32[]{:S(2)}, u32[]{:S(2)}) collective-permute-start(f32[4,256,128]{2,1,0:T(8,128)S(1)} %copy-done.17), channel_id=1, source_target_pairs={{0,4},{2,6},{4,0},{6,2},{1,5},{3,7},{5,1},{7,3},{8,12},{10,14},{12... | collective-permute-start | bytes 1572872 | tf_op jit(solution)/shard_map/ppermute | solution.py:758
  277.3 42.9 %collective-permute-start.8 = (f32[4,256,128]{2,1,0:T(8,128)}, f32[4,256,128]{2,1,0:T(8,128)}, u32[]{:S(2)}, u32[]{:S(2)}) collective-permute-start(f32[4,256,128]{2,1,0:T(8,128)} %slice_select_fusion.6), channel_id=1, source_target_pairs={{0,4},{2,6},{4,0},{6,2},{1,5},{3,7},{5,1},{7,3},{8,12},{10,14},{12... | collective-permute-start | bytes 1572872 | tf_op jit(solution)/shard_map/ppermute | solution.py:758
  277.6 47.3 %collective-permute-start.9 = (f32[8,256,128]{2,1,0:T(8,128)}, f32[8,256,128]{2,1,0:T(8,128)}, u32[]{:S(2)}, u32[]{:S(2)}) collective-permute-start(f32[8,256,128]{2,1,0:T(8,128)} %slice_select_fusion.1), channel_id=1, source_target_pairs={{0,2},{2,0},{4,6},{6,4},{1,3},{3,1},{5,7},{7,5},{8,10},{10,8},{12,... | collective-permute-start | bytes 3145736 | tf_op jit(solution)/shard_map/ppermute | solution.py:758
  305.5 17.8 %copy-start.2 = (f32[16,256,128]{2,1,0:T(8,128)S(1)}, f32[16,256,128]{2,1,0:T(8,128)}, u32[]{:S(2)}) copy-start(f32[16,256,128]{2,1,0:T(8,128)} %row_forward.7) | copy-start | bytes 6291460
  327.5 76.4 %all-to-all-start.6 = ((f32[4,2,48,4096]{3,2,1,0:T(8,128)}), f32[4,2,48,4096]{3,2,1,0:T(8,128)}, u32[]{:S(2)}, u32[]{:S(2)}) async-start(f32[4,2,48,4096]{3,2,1,0:T(8,128)} %cut_rows.6), calls=%async_computation.6 | async-start | bytes 12582912 | tf_op jit(solution)/shard_map/all_to_all | solution.py:789
  332.8 27.3 %collective-permute-start.11 = (f32[4,256,128]{2,1,0:T(8,128)}, f32[4,256,128]{2,1,0:T(8,128)S(1)}, u32[]{:S(2)}, u32[]{:S(2)}) collective-permute-start(f32[4,256,128]{2,1,0:T(8,128)} %select_add_fusion.6), channel_id=1, source_target_pairs={{0,4},{2,6},{4,0},{6,2},{1,5},{3,7},{5,1},{7,3},{8,12},{10,14},{12... | collective-permute-start | bytes 1572872 | tf_op jit(solution)/shard_map/ppermute | solution.py:758
  332.9 48.7 %collective-permute-start.10 = (f32[8,256,128]{2,1,0:T(8,128)}, f32[8,256,128]{2,1,0:T(8,128)S(1)}, u32[]{:S(2)}, u32[]{:S(2)}) collective-permute-start(f32[8,256,128]{2,1,0:T(8,128)} %get-tuple-element.96), channel_id=1, source_target_pairs={{0,2},{2,0},{4,6},{6,4},{1,3},{3,1},{5,7},{7,5},{8,10},{10,8},{12,... | collective-permute-start | bytes 3145736 | tf_op jit(solution)/shard_map/ppermute | solution.py:758
  337.0 42.2 %collective-permute-start.12 = (f32[4,256,128]{2,1,0:T(8,128)S(1)}, f32[4,256,128]{2,1,0:T(8,128)S(1)}, u32[]{:S(2)}, u32[]{:S(2)}) collective-permute-start(f32[4,256,128]{2,1,0:T(8,128)S(1)} %slice_select_fusion.5), channel_id=1, source_target_pairs={{0,4},{2,6},{4,0},{6,2},{1,5},{3,7},{5,1},{7,3},{8,12},{10,14},{12... | collective-permute-start | bytes 1572872 | tf_op jit(solution)/shard_map/ppermute | solution.py:758
  337.1 44.5 %copy-start.12 = (f32[4,256,128]{2,1,0:T(8,128)S(1)}, f32[4,256,128]{2,1,0:T(8,128)}, u32[]{:S(2)}) copy-start(f32[4,256,128]{2,1,0:T(8,128)} %copy-done.11) | copy-start | bytes 1572868
  337.1 44.5 %copy-start.14 = (f32[4,256,128]{2,1,0:T(8,128)S(1)}, f32[4,256,128]{2,1,0:T(8,128)}, u32[]{:S(2)}) copy-start(f32[4,256,128]{2,1,0:T(8,128)} %copy-done.13) | copy-start | bytes 1572868
  337.1 65.9 %collective-permute-start.13 = (f32[8,256,128]{2,1,0:T(8,128)}, f32[8,256,128]{2,1,0:T(8,128)S(1)}, u32[]{:S(2)}, u32[]{:S(2)}) collective-permute-start(f32[8,256,128]{2,1,0:T(8,128)} %get-tuple-element.100), channel_id=1, source_target_pairs={{0,2},{2,0},{4,6},{6,4},{1,3},{3,1},{5,7},{7,5},{8,10},{10,8},{12,... | collective-permute-start | bytes 3145736 | tf_op jit(solution)/shard_map/ppermute | solution.py:758
  361.3 18.9 %copy-start.7 = (f32[4,256,128]{2,1,0:T(8,128)}, f32[4,256,128]{2,1,0:T(8,128)S(1)}, u32[]{:S(2)}) copy-start(f32[4,256,128]{2,1,0:T(8,128)S(1)} %get-tuple-element.147) | copy-start | bytes 1572868
  361.3 18.9 %copy-start.9 = (f32[4,256,128]{2,1,0:T(8,128)}, f32[4,256,128]{2,1,0:T(8,128)S(1)}, u32[]{:S(2)}) copy-start(f32[4,256,128]{2,1,0:T(8,128)S(1)} %get-tuple-element.148) | copy-start | bytes 1572868
  403.3 8.3 copy-start.16
  403.9 59.0 %all-to-all-start.7 = ((f32[4,2,32,4096]{3,2,1,0:T(8,128)}), f32[4,2,32,4096]{3,2,1,0:T(8,128)}, u32[]{:S(2)}, u32[]{:S(2)}) async-start(f32[4,2,32,4096]{3,2,1,0:T(8,128)} %cut_rows.7), calls=%async_computation.7 | async-start | bytes 8388608 | tf_op jit(solution)/shard_map/all_to_all | solution.py:789
  409.8 50.2 %collective-permute-start.14 = (f32[8,256,128]{2,1,0:T(8,128)}, f32[8,256,128]{2,1,0:T(8,128)}, u32[]{:S(2)}, u32[]{:S(2)}) collective-permute-start(f32[8,256,128]{2,1,0:T(8,128)} %pad_maximum_fusion.6), channel_id=1, source_target_pairs={{0,2},{2,0},{4,6},{6,4},{1,3},{3,1},{5,7},{7,5},{8,10},{10,8},{12,... | collective-permute-start | bytes 3145736 | tf_op jit(solution)/shard_map/ppermute | solution.py:758
  411.5 39.4 %collective-permute-start.15 = (f32[4,256,128]{2,1,0:T(8,128)S(1)}, f32[4,256,128]{2,1,0:T(8,128)S(1)}, u32[]{:S(2)}, u32[]{:S(2)}) collective-permute-start(f32[4,256,128]{2,1,0:T(8,128)S(1)} %copy-done.16), channel_id=1, source_target_pairs={{0,4},{2,6},{4,0},{6,2},{1,5},{3,7},{5,1},{7,3},{8,12},{10,14},{12... | collective-permute-start | bytes 1572872 | tf_op jit(solution)/shard_map/ppermute | solution.py:758
  414.9 45.0 %collective-permute-start.16 = (f32[4,256,128]{2,1,0:T(8,128)}, f32[4,256,128]{2,1,0:T(8,128)S(1)}, u32[]{:S(2)}, u32[]{:S(2)}) collective-permute-start(f32[4,256,128]{2,1,0:T(8,128)} %slice_select_fusion.4), channel_id=1, source_target_pairs={{0,4},{2,6},{4,0},{6,2},{1,5},{3,7},{5,1},{7,3},{8,12},{10,14},{12... | collective-permute-start | bytes 1572872 | tf_op jit(solution)/shard_map/ppermute | solution.py:758
  450.9 9.1 copy-start.8
  450.9 9.1 copy-start.10
  462.9 53.7 %all-to-all-start.8 = ((f32[8,8,128,128]{3,2,1,0:T(8,128)}), f32[8,8,128,128]{3,2,1,0:T(8,128)}, u32[]{:S(2)}, u32[]{:S(2)}) async-start(f32[8,8,128,128]{3,2,1,0:T(8,128)} %row_backward.4), calls=%async_computation.8 | async-start | bytes 8388608 | tf_op jit(solution)/shard_map/all_to_all | solution.py:789
  467.5 39.1 %collective-permute-start.17 = (f32[8,256,128]{2,1,0:T(8,128)}, f32[8,256,128]{2,1,0:T(8,128)}, u32[]{:S(2)}, u32[]{:S(2)}) collective-permute-start(f32[8,256,128]{2,1,0:T(8,128)} %pad_maximum_fusion.7), channel_id=1, source_target_pairs={{0,2},{2,0},{4,6},{6,4},{1,3},{3,1},{5,7},{7,5},{8,10},{10,8},{12,... | collective-permute-start | bytes 3145736 | tf_op jit(solution)/shard_map/ppermute | solution.py:758
  468.1 38.3 %collective-permute-start.18 = (f32[4,256,128]{2,1,0:T(8,128)S(1)}, f32[4,256,128]{2,1,0:T(8,128)S(1)}, u32[]{:S(2)}, u32[]{:S(2)}) collective-permute-start(f32[4,256,128]{2,1,0:T(8,128)S(1)} %select_add_fusion.4), channel_id=1, source_target_pairs={{0,4},{2,6},{4,0},{6,2},{1,5},{3,7},{5,1},{7,3},{8,12},{10,14},{12... | collective-permute-start | bytes 1572872 | tf_op jit(solution)/shard_map/ppermute | solution.py:758
  516.6 53.7 %all-to-all-start.9 = ((f32[8,8,128,128]{3,2,1,0:T(8,128)}), f32[8,8,128,128]{3,2,1,0:T(8,128)}, u32[]{:S(2)}, u32[]{:S(2)}) async-start(f32[8,8,128,128]{3,2,1,0:T(8,128)} %row_backward.5), calls=%async_computation.9 | async-start | bytes 8388608 | tf_op jit(solution)/shard_map/all_to_all | solution.py:789
  521.1 36.6 %collective-permute-start.19 = (f32[8,256,128]{2,1,0:T(8,128)S(1)}, f32[8,256,128]{2,1,0:T(8,128)S(1)}, u32[]{:S(2)}, u32[]{:S(2)}) collective-permute-start(f32[8,256,128]{2,1,0:T(8,128)S(1)} %pad_maximum_fusion.8), channel_id=1, source_target_pairs={{0,2},{2,0},{4,6},{6,4},{1,3},{3,1},{5,7},{7,5},{8,10},{10,8},{12,... | collective-permute-start | bytes 3145736 | tf_op jit(solution)/shard_map/ppermute | solution.py:758
  570.3 53.7 %all-to-all-start.10 = ((f32[8,8,128,128]{3,2,1,0:T(8,128)}), f32[8,8,128,128]{3,2,1,0:T(8,128)}, u32[]{:S(2)}, u32[]{:S(2)}) async-start(f32[8,8,128,128]{3,2,1,0:T(8,128)} %row_backward.6), calls=%async_computation.10 | async-start | bytes 8388608 | tf_op jit(solution)/shard_map/all_to_all | solution.py:789
  610.8 17.9 %copy-start.21 = (f32[32,128]{1,0:T(8,128)S(1)}, f32[32,128]{1,0:T(8,128)}, u32[]{:S(2)}) copy-start(f32[32,128]{1,0:T(8,128)} %constant.103.clone) | copy-start | bytes 49156
  610.8 17.9 %copy-start.23 = (f32[32,128]{1,0:T(8,128)S(1)}, f32[32,128]{1,0:T(8,128)}, u32[]{:S(2)}) copy-start(f32[32,128]{1,0:T(8,128)} %constant.102.clone) | copy-start | bytes 49156
  610.8 17.9 %copy-start.25 = (f32[32,128]{1,0:T(8,128)S(1)}, f32[32,128]{1,0:T(8,128)}, u32[]{:S(2)}) copy-start(f32[32,128]{1,0:T(8,128)} %constant.101.clone) | copy-start | bytes 49156
  610.8 17.9 %copy-start.27 = (f32[32,128]{1,0:T(8,128)S(1)}, f32[32,128]{1,0:T(8,128)}, u32[]{:S(2)}) copy-start(f32[32,128]{1,0:T(8,128)} %constant.100.clone) | copy-start | bytes 49156
  610.9 17.9 %copy-start.33 = (f32[4]{0:T(128)S(1)}, f32[4]{0:T(128)}, u32[]{:S(2)}) copy-start(f32[4]{0:T(128)} %copy-done.32) | copy-start | bytes 52
  610.9 17.9 %copy-start.35 = (f32[4]{0:T(128)S(1)}, f32[4]{0:T(128)}, u32[]{:S(2)}) copy-start(f32[4]{0:T(128)} %copy-done.34) | copy-start | bytes 52
  610.9 18.9 %copy-start.1 = (f32[4,2,16,4096]{3,2,1,0:T(8,128)S(1)}, f32[4,2,16,4096]{3,2,1,0:T(8,128)}, u32[]{:S(2)}) copy-start(f32[4,2,16,4096]{3,2,1,0:T(8,128)} %copy-done) | copy-start | bytes 6291460
  624.0 53.9 %all-to-all-start.11 = ((f32[8,8,128,128]{3,2,1,0:T(8,128)}), f32[8,8,128,128]{3,2,1,0:T(8,128)}, u32[]{:S(2)}, u32[]{:S(2)}) async-start(f32[8,8,128,128]{3,2,1,0:T(8,128)} %row_backward.7), calls=%async_computation.11 | async-start | bytes 8388608 | tf_op jit(solution)/shard_map/all_to_all | solution.py:789
  714.6 5.8 collective-permute-start.20
  717.0 7.2 collective-permute-start.21
  761.4 190.7 %collective-permute-start.22 = (f32[2,96,4096]{2,1,0:T(8,128)}, f32[2,96,4096]{2,1,0:T(8,128)S(1)}, u32[]{:S(2)}, u32[]{:S(2)}) collective-permute-start(f32[2,96,4096]{2,1,0:T(8,128)} %get-tuple-element.119), channel_id=1, source_target_pairs={{0,8},{8,0},{16,24},{24,16},{1,9},{9,1},{17,25},{25,17},{2,10},{10... | collective-permute-start | bytes 9437192 | tf_op jit(solution)/shard_map/ppermute | solution.py:758
  763.4 188.7 %collective-permute-start.23 = (f32[2,96,4096]{2,1,0:T(8,128)}, f32[2,96,4096]{2,1,0:T(8,128)}, u32[]{:S(2)}, u32[]{:S(2)}) collective-permute-start(f32[2,96,4096]{2,1,0:T(8,128)} %get-tuple-element.120), channel_id=1, source_target_pairs={{0,16},{8,24},{16,0},{24,8},{1,17},{9,25},{17,1},{25,9},{2,18},{10... | collective-permute-start | bytes 9437192 | tf_op jit(solution)/shard_map/ppermute | solution.py:758
  763.4 188.7 %collective-permute-start.24 = (f32[2,96,4096]{2,1,0:T(8,128)}, f32[2,96,4096]{2,1,0:T(8,128)}, u32[]{:S(2)}, u32[]{:S(2)}) collective-permute-start(f32[2,96,4096]{2,1,0:T(8,128)} %get-tuple-element.121), channel_id=1, source_target_pairs={{0,24},{8,16},{16,8},{24,0},{1,25},{9,17},{17,9},{25,1},{2,26},{10... | collective-permute-start | bytes 9437192 | tf_op jit(solution)/shard_map/ppermute | solution.py:758
  765.0 155.7 %collective-permute-start.25 = (f32[2,32,4096]{2,1,0:T(8,128)}, f32[2,32,4096]{2,1,0:T(8,128)}, u32[]{:S(2)}, u32[]{:S(2)}) collective-permute-start(f32[2,32,4096]{2,1,0:T(8,128)} %get-tuple-element.122), channel_id=1, source_target_pairs={{0,8},{8,0},{16,24},{24,16},{1,9},{9,1},{17,25},{25,17},{2,10},{10... | collective-permute-start | bytes 3145736 | tf_op jit(solution)/shard_map/ppermute | solution.py:758
  766.9 156.6 %collective-permute-start.26 = (f32[2,32,4096]{2,1,0:T(8,128)}, f32[2,32,4096]{2,1,0:T(8,128)}, u32[]{:S(2)}, u32[]{:S(2)}) collective-permute-start(f32[2,32,4096]{2,1,0:T(8,128)} %get-tuple-element.123), channel_id=1, source_target_pairs={{0,16},{8,24},{16,0},{24,8},{1,17},{9,25},{17,1},{25,9},{2,18},{10... | collective-permute-start | bytes 3145736 | tf_op jit(solution)/shard_map/ppermute | solution.py:758
  920.7 26.5 %collective-permute-start.27 = (f32[2,32,4096]{2,1,0:T(8,128)}, f32[2,32,4096]{2,1,0:T(8,128)}, u32[]{:S(2)}, u32[]{:S(2)}) collective-permute-start(f32[2,32,4096]{2,1,0:T(8,128)} %get-tuple-element.124), channel_id=1, source_target_pairs={{0,24},{8,16},{16,8},{24,0},{1,25},{9,17},{17,9},{25,1},{2,26},{10... | collective-permute-start | bytes 3145736 | tf_op jit(solution)/shard_map/ppermute | solution.py:758
  (14 other events, 32.0 us)
